TPU v7x, 32 devices: a whole 2x2x4 slice. The times are simulated.
32 devices in a mesh: groups: 2 (over y), vocab: 8 (over z, x), dp: 2 (over core).
Axes of the slice: x: 2, y: 2, z: 4, core: 2. Of those that a mesh axis runs over, the one named last changes fastest.
Arguments:
- hidden_states: bfloat16 [1024, 4096], P(('groups', 'dp')), parts along dimension 0, may hold values from -100 to 100
- targets: int32 [1024], P(('groups', 'dp')), parts along dimension 0, may hold values from 0 to 127
- old_embed: bfloat16 [2048, 4096], P('vocab'), may hold values from -3 to 3
- decomp: int32 [256, 8], P(('groups', 'vocab')), parts along dimension 0, may hold values from -1 to 2047, as said below
- counts: int32 [256], P(('groups', 'vocab')), parts along dimension 0, may hold values from 6 to 8, as said below
- w_in: bfloat16 [4096, 4096], P('dp', 'vocab'), may hold values from -0.359375 to 0.359375
- w_out: bfloat16 [4096, 4096], P('vocab'), may hold values from -0.09375 to 0.09375
Outputs:
- loss_value: float32 [2], P('groups'), parts along dimension 0
- grad_in: float32 [8192, 4096], P(('groups', 'dp'), 'vocab'), parts along dimension 0
- grad_out: float32 [8192, 4096], P(('groups', 'vocab')), parts along dimension 0
There are 2 independent parts, one for each index of `groups`. A program takes and returns all parts, laid end to end along the dimension named above; an argument that names none is the same for every part. Nothing has to cross between parts.
Inputs may be any that keep to these rules, and one draw needn't show every extreme that they name: `decomp`: row r holds ids in its first counts[r] entries and -1 in the rest. Over the 16 rows of one vocab index, at most 16 used entries lie in one owner's range [o * 256, (o + 1) * 256), and some owner has exactly 16. `counts`: the first of every 16 rows has 8.
All inputs are finite; a program needn't handle non-finite values.
Results may differ from a plain program's by a relative error of at most 0.0061.
Values may be sent and summed in bfloat16 or wider, within the bound.
No kernel may reach another device: no remote copies, remote signals or barrier semaphores. Data moves between devices by JAX's collectives and lax.ppermute only.
A program may use at most 128 MiB of HBM per device.

v0:
```python
import jax
import jax.numpy as jnp
from jax import lax
from jax.sharding import PartitionSpec as P


def activate(values):
    return jax.nn.gelu(values, approximate=True)


def slot_places(flat_ids, old_rows, groups, capacity):
    usable = flat_ids >= 0
    owners = jnp.where(usable, flat_ids // old_rows, groups)
    local_rows = jnp.where(usable, flat_ids % old_rows, 0)
    owner_range = jnp.arange(groups, dtype=jnp.int32)
    onehot = (owners[:, None] == owner_range[None, :]).astype(jnp.int32)
    before = jnp.cumsum(onehot, 0) - onehot
    ranking = jnp.sum(before * onehot, 1)
    places = jnp.where(usable, owners * capacity + ranking, groups * capacity)
    return (usable, local_rows, places)


def shards(hidden_states, targets, old_embed, decomp, counts, w_in, w_out):
    new_rows, k_slots = decomp.shape
    old_rows, width = old_embed.shape
    groups = lax.axis_size("vocab")
    own_index = lax.axis_index("vocab")
    capacity = max(2, new_rows * k_slots // groups)
    flat_ids = decomp.reshape(-1)
    usable, local_rows, places = slot_places(flat_ids, old_rows, groups, capacity)
    asked = jnp.full((groups * capacity,), -1, jnp.int32).at[places].set(local_rows, mode="drop")
    asked = asked.reshape(groups, capacity)
    look_asked = lax.all_to_all(asked, "vocab", split_axis=0, concat_axis=0, tiled=True)
    present = look_asked >= 0
    fetched = old_embed[jnp.where(present, look_asked, 0)]
    arrived = lax.all_to_all(
        jnp.where(present[:, :, None], fetched, jnp.zeros((), fetched.dtype)),
        "vocab",
        split_axis=0,
        concat_axis=0,
        tiled=True,
    )
    table = arrived.reshape(groups * capacity, width)
    picked_rows = table[jnp.where(usable, places, 0)]
    picked_rows = jnp.where(usable[:, None], picked_rows, jnp.zeros((), picked_rows.dtype)).astype(
        jnp.float32
    )
    summed = jnp.sum(picked_rows.reshape(new_rows, k_slots, width), 1)
    new_embed = (summed / counts[:, None].astype(jnp.float32)).astype(jnp.bfloat16)
    half_width = w_in.shape[0]
    dp_index = lax.axis_index("dp")
    own_half = lax.dynamic_slice_in_dim(new_embed, dp_index * half_width, half_width, 1)
    new_all = lax.all_gather(own_half, "vocab", axis=0, tiled=True)
    pre_units = lax.psum(jnp.dot(new_all, w_in, preferred_element_type=jnp.float32), "dp")
    hidden_units = activate(pre_units).astype(jnp.bfloat16)
    contract_last = (((1,), (1,)), ((), ()))
    contract_first = (((0,), (0,)), ((), ()))
    basis = lax.dot_general(
        hidden_states, w_out, contract_last, preferred_element_type=jnp.float32
    ).astype(jnp.bfloat16)
    logits = lax.dot_general(
        hidden_states, new_embed, contract_last, preferred_element_type=jnp.float32
    )
    logits = (
        logits
        + lax.psum_scatter(
            lax.dot_general(hidden_units, basis, contract_last, preferred_element_type=jnp.float32),
            "vocab",
            scatter_dimension=0,
            tiled=True,
        ).T
    )
    row_top = lax.pmax(jnp.max(logits, 1), "vocab")
    columns = own_index * new_rows + jnp.arange(new_rows, dtype=jnp.int32)
    target_hits = targets[:, None] == columns[None, :]
    exp_local = jnp.sum(jnp.exp(logits - row_top[:, None]), 1)
    target_local = jnp.sum(jnp.where(target_hits, logits, jnp.float32(0.0)), 1)
    exp_totals, picked = lax.psum((exp_local, target_local), "vocab")
    log_totals = row_top + jnp.log(exp_totals)
    token_count = hidden_states.shape[0] * lax.axis_size("dp")
    loss_value = (lax.psum(jnp.sum(log_totals - picked), "dp") / token_count).reshape(1)
    probs = jnp.exp(logits - log_totals[:, None])
    dlogits = (probs - target_hits.astype(jnp.float32)).astype(jnp.bfloat16)
    dlogits_all = lax.all_gather(dlogits, "vocab", axis=1, tiled=True)
    mixed = jnp.dot(dlogits_all, hidden_units, preferred_element_type=jnp.float32).astype(
        jnp.bfloat16
    )
    out_partial = lax.dot_general(
        mixed, hidden_states, contract_first, preferred_element_type=jnp.float32
    )
    units_partial = lax.dot_general(
        dlogits_all, basis, contract_first, preferred_element_type=jnp.float32
    )
    grad_units, grad_out = lax.psum((units_partial, out_partial), "dp")
    grad_pre = jax.vjp(activate, pre_units)[1](grad_units)[0].astype(jnp.bfloat16)
    grad_in = lax.dot_general(new_all, grad_pre, contract_first, preferred_element_type=jnp.float32)
    return (loss_value, grad_in, grad_out)


def solution(mesh):
    in_specs = (
        P(("groups", "dp"), None),
        P(("groups", "dp")),
        P("vocab", None),
        P(("groups", "vocab"), None),
        P(("groups", "vocab")),
        P("dp", "vocab"),
        P("vocab", None),
    )
    out_specs = (P("groups"), P(("groups", "dp"), "vocab"), P(("groups", "vocab"), None))
    return jax.shard_map(shards, mesh=mesh, in_specs=in_specs, out_specs=out_specs, check_vma=False)
```

profile of v0, /device:TPU:0, one launch (start us, length us, event | category | flops | bytes accessed | tf_op | source)
XLA Modules:
  0.0 310.5 jit_solution(4572578184742502189)
XLA Ops:
  7.2 0.9 copy.17
  8.8 1.0 scatter_custom_fusion
  9.8 13.5 %all_to_all.17 = s32[8,1,16]{2,1,0:T(1,128)S(1)} all-to-all(s32[8,1,16]{2,1,0:T(1,128)S(1)} %bitcast.52), channel_id=1, replica_groups=mesh['groups'=2,'vocab'=8,'dp'=2] {'vocab'}, dimensions={0} | all-to-all | bytes 1024 | tf_op jit(solution)/shard_map/all_to_all | solution.py:33
  23.4 4.1 %gather_fusion = bf16[128,4096]{1,0:T(8,128)(2,1)S(1)} fusion(bf16[256,4096]{1,0:T(8,128)(2,1)} %param.9, s32[1024]{0:T(1024)S(1)} %pad_clamp_fusion.1), kind=kCustom, calls=%fused_computation | custom fusion | bytes 2097664 | tf_op jit(solution)/shard_map/gather | solution.py:35
  27.5 1.1 broadcast_select_fusion
  28.6 3.6 %all-to-all-start.1 = ((bf16[8,16,4096]{2,1,0:T(8,128)(2,1)}), bf16[8,16,4096]{2,1,0:T(8,128)(2,1)S(1)}, u32[]{:S(2)}, u32[]{:S(2)}) async-start(bf16[8,16,4096]{2,1,0:T(8,128)(2,1)} %broadcast_select_fusion), calls=%async_computation.1 | async-start | bytes 2097152 | tf_op jit(solution)/shard_map/all_to_all | solution.py:36
  32.4 24.5 %all-to-all-done.1 = bf16[8,16,4096]{2,1,0:T(8,128)(2,1)S(1)} async-done(((bf16[8,16,4096]{2,1,0:T(8,128)(2,1)}), bf16[8,16,4096]{2,1,0:T(8,128)(2,1)S(1)}, u32[]{:S(2)}, u32[]{:S(2)}) %all-to-all-start.1) | async-done | bytes 1048608 | tf_op jit(solution)/shard_map/all_to_all | solution.py:36
  56.9 2.2 gather_fusion.1
  59.1 2.2 convert_reduce_fusion
  61.4 31.5 %all_gather.6 = bf16[128,2048]{1,0:T(8,128)(2,1)S(1)} all-gather(bf16[16,2048]{1,0:T(8,128)(2,1)S(1)} %constant_dynamic-slice_fusion), channel_id=1, replica_groups=mesh['groups'=2,'vocab'=8,'dp'=2] {'vocab'}, dimensions={0}, use_global_device_ids=true | all-gather | bytes 589824 | tf_op jit(solution)/shard_map/all_gather | solution.py:53
  92.9 1.2 fusion.37
  94.1 3.5 %convolution_convert_fusion.1 = bf16[256,512]{1,0:T(8,128)(2,1)S(1)} fusion(bf16[256,4096]{1,0:T(8,128)(2,1)S(1)} %copy-done, bf16[512,4096]{1,0:T(8,128)(2,1)} %param.13), kind=kOutput, calls=%fused_computation.5 | convolution fusion | flops 1073872896 | bytes 6553600 | tf_op jit(solution)/shard_map/dot_general | solution.py:58
  97.6 13.8 %all-reduce.5.cloned.1.call-done = f32[128,512]{1,0:T(8,128)} async-done(((f32[128,512]{1,0:T(8,128)}), f32[128,512]{1,0:T(8,128)}) %all-reduce.5.cloned.1.call-update) | async-done | bytes 262160 | tf_op jit(solution)/shard_map/psum | solution.py:54
  111.4 1.9 fusion.34
  113.4 64.3 %reduce-scatter.2.cloned.1.call-done = f32[16,256]{1,0:T(8,128)} async-done(((f32[128,256]{1,0:T(8,128)}), f32[16,256]{1,0:T(8,128)}) %reduce-scatter.2.cloned.1.call-update) | async-done | bytes 16400 | tf_op jit(solution)/shard_map/reduce_scatter | solution.py:66
  177.7 1.4 fusion.36
  179.1 19.5 %pmax.7 = f32[256]{0:T(256)S(1)} all-reduce(f32[256]{0:T(256)S(1)} %get-tuple-element.15), channel_id=1, replica_groups=mesh['groups'=2,'vocab'=8,'dp'=2] {'vocab'}, use_global_device_ids=true, to_apply=%region_7.8 | all-reduce | flops 256 | bytes 2048 | tf_op jit(solution)/shard_map/pmax | solution.py:73
  198.7 17.1 %all-reduce = (f32[256]{0:T(256)S(1)}, f32[256]{0:T(256)S(1)}) all-reduce(f32[256]{0:T(256)S(1)} %get-tuple-element.4, f32[256]{0:T(256)S(1)} %get-tuple-element.3), channel_id=1, replica_groups=mesh['groups'=2,'vocab'=8,'dp'=2] {'vocab'}, use_global_device_ids=true, to_apply=%region_9.10 | all-reduce | flops 512 | bytes 4096 | tf_op jit(solution)/shard_map/psum | solution.py:78
  216.5 30.5 %all_gather.7 = bf16[256,128]{0,1:T(8,128)(2,1)S(1)} all-gather(bf16[256,16]{0,1:T(8,128)(2,1)S(1)} %fusion.19), channel_id=1, replica_groups=mesh['groups'=2,'vocab'=8,'dp'=2] {'vocab'}, dimensions={1}, use_global_device_ids=true | all-gather | bytes 73728 | tf_op jit(solution)/shard_map/all_gather | solution.py:84
  247.9 4.9 %fusion = f32[512,4096]{1,0:T(8,128)} fusion(bf16[256,4096]{1,0:T(8,128)(2,1)S(1)} %copy-done, bf16[256,128]{0,1:T(8,128)(2,1)S(1)} %all_gather.7, f32[128,512]{1,0:T(8,128)S(1)} %copy-done.2), kind=kOutput, calls=%fused_computation.6 | convolution fusion | flops 1108017152 | bytes 10813440 | tf_op jit(solution)/shard_map/dot_general | solution.py:88
  252.8 3.1 %psum.45 = f32[]{:T(128)} all-reduce(f32[]{:T(128)} %get-tuple-element.9), channel_id=1, replica_groups=mesh['groups'=2,'vocab'=8,'dp'=2] {'dp'}, use_global_device_ids=true, to_apply=%region_13.14 | all-reduce | flops 1 | bytes 8 | tf_op jit(solution)/shard_map/psum | solution.py:81
  256.6 34.6 %all-reduce.7.cloned.1.call-done = (f32[128,512]{1,0:T(8,128)}, f32[512,4096]{1,0:T(8,128)}) async-done(((f32[128,512]{1,0:T(8,128)}, f32[512,4096]{1,0:T(8,128)}), (f32[128,512]{1,0:T(8,128)}, f32[512,4096]{1,0:T(8,128)})) %all-reduce.7.cloned.1.call-update) | async-done | bytes 8650768 | tf_op jit(solution)/shard_map/psum | solution.py:94
  291.2 3.8 %fusion.8 = f32[2048,512]{1,0:T(8,128)} fusion(bf16[128,2048]{1,0:T(8,128)(2,1)S(1)} %all_gather.6, f32[128,512]{1,0:T(8,128)S(1)} %copy-done.2, f32[128,512]{1,0:T(8,128)} %get-tuple-element.7), kind=kOutput, calls=%fused_computation.21 | convolution fusion | flops 269746176 | bytes 5242880 | tf_op jit(solution)/shard_map/dot_general | solution.py:96
  295.0 7.8 %copy.24 = f32[512,4096]{1,0:T(8,128)} copy(f32[512,4096]{1,0:T(8,128)} %get-tuple-element.19) | data formatting | bytes 16777216
  (42 shorter events, 2.9 us)
Async XLA Ops:
  7.2 87.0 %copy-start = (bf16[256,4096]{1,0:T(8,128)(2,1)S(1)}, bf16[256,4096]{1,0:T(8,128)(2,1)}, u32[]{:S(2)}) copy-start(bf16[256,4096]{1,0:T(8,128)(2,1)} %param.7) | copy-start | bytes 6291460
  27.5 4.8 %copy-start.5 = (s32[16]{0:T(128)S(1)}, s32[16]{0:T(128)}, u32[]{:S(2)}) copy-start(s32[16]{0:T(128)} %param.11) | copy-start | bytes 196
  27.5 4.8 %copy-start.3 = (s32[16,8]{0,1:T(8,128)S(1)}, s32[16,8]{0,1:T(8,128)}, u32[]{:S(2)}) copy-start(s32[16,8]{0,1:T(8,128)} %param.10) | copy-start | bytes 1540
  28.6 28.3 %all-to-all-start.1 = ((bf16[8,16,4096]{2,1,0:T(8,128)(2,1)}), bf16[8,16,4096]{2,1,0:T(8,128)(2,1)S(1)}, u32[]{:S(2)}, u32[]{:S(2)}) async-start(bf16[8,16,4096]{2,1,0:T(8,128)(2,1)} %broadcast_select_fusion), calls=%async_computation.1 | async-start | bytes 2097152 | tf_op jit(solution)/shard_map/all_to_all | solution.py:36
  32.2 79.2 %all-reduce.5.cloned.1.call-start = ((), (), s32[]{:S(2)}) async-start(), calls=%async_computation.3 | async-start | bytes 524288 | tf_op jit(solution)/shard_map/psum | solution.py:54
  59.1 33.8 %copy-start.1 = (bf16[2048,512]{1,0:T(8,128)(2,1)S(1)}, bf16[2048,512]{1,0:T(8,128)(2,1)}, u32[]{:S(2)}) copy-start(bf16[2048,512]{1,0:T(8,128)(2,1)} %param.12) | copy-start | bytes 6291460
  94.1 83.7 %reduce-scatter.2.cloned.1.call-start = ((), (), s32[]{:S(2)}) async-start(), calls=%async_computation.4 | async-start | bytes 147456 | tf_op jit(solution)/shard_map/reduce_scatter | solution.py:66
  97.6 101.0 %copy-start.4 = (s32[256]{0:T(256)S(1)}, s32[256]{0:T(256)}, u32[]{:S(2)}) copy-start(s32[256]{0:T(256)} %param.8) | copy-start | bytes 3076
  111.4 136.4 %copy-start.2 = (f32[128,512]{1,0:T(8,128)S(1)}, f32[128,512]{1,0:T(8,128)}, u32[]{:S(2)}) copy-start(f32[128,512]{1,0:T(8,128)} %all-reduce.5.cloned.1.call-done) | copy-start | bytes 786436
  113.4 177.8 %all-reduce.7.cloned.1.call-start = ((), (), s32[]{:S(2)}) async-start(), calls=%async_computation.5 | async-start | bytes 17301504 | tf_op jit(solution)/shard_map/psum | solution.py:94
Sparse Core Ops, SparseCore 0:
  94.2 17.1 all-reduce.4
  115.7 62.0 reduce-scatter.1
  253.0 38.1 all-reduce.6
where the time goes:
time: 311 us; the launch traced here: 310 us
  waiting for transfers between devices  137 us (44%)
  blocking collectives  115 us (37%)
  matrix products  17.6 us (6%)
  local copies, waits for them, and re-layouts  16.4 us (5%)
  between operations  15.7 us (5%)
  other arithmetic  4.63 us (1%)
  starting transfers between devices  3.68 us (1%)
    reduce_scatter x1, waiting for transfers between devices, shards(): lax.psum_scatter(lax.dot_general(hidden_units, basis, contract_last, pref...  64.3 us
    psum x1, waiting for transfers between devices, shards(): grad_units, grad_out = lax.psum((units_partial, out_partial), 'dp')  34.6 us
    all_gather x1, blocking collectives, shards(): new_all = lax.all_gather(own_half, 'vocab', axis=0, tiled=True)  31.5 us
    all_gather x1, blocking collectives, shards(): dlogits_all = lax.all_gather(dlogits, 'vocab', axis=1, tiled=True)  30.5 us
    all_to_all x1, waiting for transfers between devices, shards(): lax.all_to_all(jnp.where(present[:, :, None], fetched, jnp.zeros((), fetc...  24.5 us
    pmax x1, blocking collectives, shards(): row_top = lax.pmax(jnp.max(logits, 1), 'vocab')  19.5 us
    psum x1, blocking collectives, shards(): exp_totals, picked = lax.psum((exp_local, target_local), 'vocab')  17.1 us
    psum x1, waiting for transfers between devices, shards(): lax.psum(jnp.dot(new_all, w_in, preferred_element_type=jnp.float32), 'dp')  13.8 us
  transfers between devices with their start and end apart: 4, of which 4 were waited for; matrix products, arithmetic and copies ran while one was open for 1% of the time, Pallas kernels for 0%

commit v1 on v0

v1 whole, which is shorter than its diff:
```python
import jax
import jax.numpy as jnp
from jax import lax
from jax.sharding import PartitionSpec as P

LAST = (((1,), (1,)), ((), ()))
FIRST = (((0,), (0,)), ((), ()))


def activate(values):
    return jax.nn.gelu(values, approximate=True)


def dot(a, b, dims=(((1,), (0,)), ((), ()))):
    return lax.dot_general(a, b, dims, preferred_element_type=jnp.float32)


def place_slots(decomp, old_rows, groups, capacity):
    new_rows, k_slots = decomp.shape
    slots = new_rows * k_slots
    flat = decomp.reshape(1, slots)
    usable = flat >= 0
    owners = jnp.where(usable, flat // old_rows, groups)
    local = jnp.where(usable, flat % old_rows, 0)
    onehot = owners == lax.broadcasted_iota(jnp.int32, (groups, slots), 0)
    earlier = lax.broadcasted_iota(jnp.int32, (slots, slots), 0) < lax.broadcasted_iota(
        jnp.int32, (slots, slots), 1
    )
    before = dot(onehot.astype(jnp.bfloat16), earlier.astype(jnp.bfloat16)).astype(jnp.int32)
    ranking = jnp.sum(jnp.where(onehot, before, 0), 0, keepdims=True)
    places = jnp.where(usable, owners * capacity + ranking, -1)
    taken = places == lax.broadcasted_iota(jnp.int32, (groups * capacity, slots), 0)
    asked = jnp.sum(jnp.where(taken, local + 1, 0), 1) - 1
    token = lax.broadcasted_iota(jnp.int32, (new_rows, slots), 1) // k_slots
    mine = token == lax.broadcasted_iota(jnp.int32, (new_rows, slots), 0)
    adder = dot(mine.astype(jnp.bfloat16), taken.astype(jnp.bfloat16), LAST).astype(jnp.bfloat16)
    return asked, adder


def shards(hidden_states, targets, old_embed, decomp, counts, w_in, w_out):
    new_rows, k_slots = decomp.shape
    old_rows, width = old_embed.shape
    groups = lax.axis_size("vocab")
    cores = lax.axis_size("dp")
    own_index = lax.axis_index("vocab")
    dp_index = lax.axis_index("dp")
    tokens = hidden_states.shape[0]
    half_width = w_in.shape[0]
    columns_all = groups * new_rows
    capacity = max(2, new_rows * k_slots // groups)
    swap = [(0, 1), (1, 0)]

    asked, adder = place_slots(decomp, old_rows, groups, capacity)
    look = lax.all_to_all(asked.reshape(groups, capacity), "vocab", 0, 0, tiled=True)
    hidden_other = lax.ppermute(hidden_states, "dp", swap)
    basis = dot(hidden_states, w_out, LAST).astype(jnp.bfloat16)
    basis_other = lax.ppermute(basis, "dp", swap)
    old_half = lax.dynamic_slice_in_dim(old_embed, dp_index * half_width, half_width, 1)

    select = look.reshape(-1, 1) == lax.broadcasted_iota(
        jnp.int32, (groups * capacity, old_rows), 1
    )
    fetched = dot(select.astype(jnp.bfloat16), old_half).astype(jnp.bfloat16)
    arrived = lax.all_to_all(
        fetched.reshape(groups, capacity, half_width), "vocab", 0, 0, tiled=True
    ).reshape(groups * capacity, half_width)
    new_own = (dot(adder, arrived) / counts[:, None].astype(jnp.float32)).astype(jnp.bfloat16)

    new_all = lax.all_to_all(
        jnp.broadcast_to(new_own[None], (groups, new_rows, half_width)), "vocab", 0, 0, tiled=True
    ).reshape(columns_all, half_width)
    new_other = lax.ppermute(new_own, "dp", swap)
    new_wide = jnp.where(
        dp_index == 0,
        jnp.concatenate([new_own, new_other], 1),
        jnp.concatenate([new_other, new_own], 1),
    )
    direct = dot(hidden_states, new_wide, LAST)

    pre_half = dot(new_all, w_in)
    pre_units = pre_half + lax.ppermute(pre_half, "dp", swap)
    hidden_units = activate(pre_units).astype(jnp.bfloat16)

    share = dot(basis, hidden_units, LAST)
    share = share + lax.dynamic_update_slice(
        jnp.zeros((tokens, columns_all), jnp.float32), direct, (0, own_index * new_rows)
    )
    own_tokens = tokens // groups
    shares = lax.all_to_all(
        share.reshape(groups, own_tokens, columns_all), "vocab", 0, 0, tiled=True
    )
    logits = jnp.sum(shares, 0)
    row_top = jnp.max(logits, 1)
    log_totals = row_top + jnp.log(jnp.sum(jnp.exp(logits - row_top[:, None]), 1))
    own_targets = lax.dynamic_slice_in_dim(targets, own_index * own_tokens, own_tokens)
    hits = own_targets[:, None] == lax.broadcasted_iota(jnp.int32, (own_tokens, columns_all), 1)
    picked = jnp.sum(jnp.where(hits, logits, jnp.float32(0.0)), 1)
    loss_share = jnp.sum(log_totals - picked)
    dlogits = (jnp.exp(logits - log_totals[:, None]) - hits.astype(jnp.float32)).astype(
        jnp.bfloat16
    )

    high = lax.reduce_precision(loss_share, 8, 7)
    middle = lax.reduce_precision(loss_share - high, 8, 7)
    low = lax.reduce_precision(loss_share - high - middle, 8, 7)
    pieces = jnp.stack([high, middle, low]).astype(jnp.bfloat16)
    extra = jnp.zeros((16, columns_all), jnp.bfloat16).at[0, :3].set(pieces)
    packet = jnp.concatenate([dlogits, extra], 0)
    packets = lax.all_to_all(
        jnp.broadcast_to(packet[None], (groups * cores,) + packet.shape),
        ("vocab", "dp"),
        0,
        0,
        tiled=True,
    ).reshape(groups, cores, own_tokens + 16, columns_all)
    loss_value = (
        jnp.sum(packets[:, :, own_tokens, :3].astype(jnp.float32)) / (tokens * cores)
    ).reshape(1)
    dlogits_own = lax.dynamic_index_in_dim(packets, dp_index, 1, False)[:, :own_tokens].reshape(
        tokens, columns_all
    )
    dlogits_other = lax.dynamic_index_in_dim(packets, 1 - dp_index, 1, False)[
        :, :own_tokens
    ].reshape(tokens, columns_all)

    mixed_own = dot(dlogits_own, hidden_units).astype(jnp.bfloat16)
    mixed_other = dot(dlogits_other, hidden_units).astype(jnp.bfloat16)
    grad_out = dot(mixed_own, hidden_states, FIRST) + dot(mixed_other, hidden_other, FIRST)
    grad_units = dot(dlogits_own, basis, FIRST) + dot(dlogits_other, basis_other, FIRST)
    grad_pre = jax.vjp(activate, pre_units)[1](grad_units)[0].astype(jnp.bfloat16)
    grad_in = dot(new_all, grad_pre, FIRST)
    return (loss_value, grad_in, grad_out)


def solution(mesh):
    in_specs = (
        P(("groups", "dp"), None),
        P(("groups", "dp")),
        P("vocab", None),
        P(("groups", "vocab"), None),
        P(("groups", "vocab")),
        P("dp", "vocab"),
        P("vocab", None),
    )
    out_specs = (P("groups"), P(("groups", "dp"), "vocab"), P(("groups", "vocab"), None))
    return jax.shard_map(shards, mesh=mesh, in_specs=in_specs, out_specs=out_specs, check_vma=False)
```

time: 311 us -> 119 us (0.38)
  blocking collectives: 115 us -> 0 us
  waiting for transfers between devices: 137 us -> 49.6 us
  starting transfers between devices: 3.68 us -> 22.6 us
  matrix products: 17.6 us -> 29.4 us
  local copies, waits for them, and re-layouts: 16.4 us -> 5.76 us
  between operations: 15.7 us -> 8.08 us
    reduce_scatter x1 -> x0, waiting for transfers between devices: 64.3 us -> none  [shards(): lax.psum_scatter(lax.dot_general(hidden_units, basis, contract_last, pref...]
    all_gather x2 -> x0, blocking collectives: 62 us -> none  [the longest x1 31.5 us: shards(): new_all = lax.all_gather(own_half, 'vocab', axis=0, tiled=True)]
    psum x2 -> x0, waiting for transfers between devices: 48.4 us -> none  [the longest x1 34.6 us: shards(): grad_units, grad_out = lax.psum((units_partial, out_partial), 'dp')]
    all_to_all x1 -> x5, waiting for transfers between devices: 24.5 us -> 49.6 us  [the longest x1 13.8 us: shards(): lax.all_to_all(jnp.broadcast_to(new_own[None], (groups, new_rows, half_wi...]
    psum x2 -> x0, blocking collectives: 20.2 us -> none  [the longest x1 17.1 us: shards(): exp_totals, picked = lax.psum((exp_local, target_local), 'vocab')]
    pmax x1 -> x0, blocking collectives: 19.5 us -> none  [shards(): row_top = lax.pmax(jnp.max(logits, 1), 'vocab')]
    all_to_all x1 -> x5, starting transfers between devices: 3.56 us -> 21.7 us  [the longest x1 7.25 us: shards(): lax.all_to_all(asked.reshape(groups, capacity), 'vocab', 0, 0, tiled=True)]
    all_to_all x1 -> x0, blocking collectives: 13.5 us -> none  [shards(): lax.all_to_all(asked, 'vocab', split_axis=0, concat_axis=0, tiled=True)]
  transfers between devices with their start and end apart: 4 -> 9, of which waited for: 4 -> 5; matrix products, arithmetic and copies ran while one was open for 1% -> 25% of each run, Pallas kernels for 0% -> 0%
where the time goes in v1:
time: 119 us
  waiting for transfers between devices  49.6 us (42%)
  matrix products  29.4 us (25%)
  starting transfers between devices  22.6 us (19%)
  between operations  8.08 us (7%)
  local copies, waits for them, and re-layouts  5.76 us (5%)
  other arithmetic  3.18 us (3%)
    dot_general x11, matrix products, dot(): return lax.dot_general(a, b, dims, preferred_element_type=jnp.float32)  29.4 us
    all_to_all x1, waiting for transfers between devices, shards(): lax.all_to_all(jnp.broadcast_to(new_own[None], (groups, new_rows, half_wi...  13.8 us
    all_to_all x1, waiting for transfers between devices, shards(): lax.all_to_all(fetched.reshape(groups, capacity, half_width), 'vocab', 0,...  13.2 us
    all_to_all x1, waiting for transfers between devices, shards(): lax.all_to_all(jnp.broadcast_to(packet[None], (groups * cores,) + packet....  8.67 us
    all_to_all x1, waiting for transfers between devices, shards(): lax.all_to_all(share.reshape(groups, own_tokens, columns_all), 'vocab', 0...  7.55 us
    all_to_all x1, starting transfers between devices, shards(): lax.all_to_all(asked.reshape(groups, capacity), 'vocab', 0, 0, tiled=True)  7.25 us
    all_to_all x1, waiting for transfers between devices, shards(): lax.all_to_all(asked.reshape(groups, capacity), 'vocab', 0, 0, tiled=True)  6.39 us
    all_to_all x1, starting transfers between devices, shards(): lax.all_to_all(share.reshape(groups, own_tokens, columns_all), 'vocab', 0...  3.77 us
  transfers between devices with their start and end apart: 9, of which 5 were waited for; matrix products, arithmetic and copies ran while one was open for 25% of the time, Pallas kernels for 0%

profile of v1, /device:TPU:0, one launch (start us, length us, event | category | flops | bytes accessed | tf_op | source)
XLA Modules:
  0.0 118.7 jit_solution(15491122887567779857)
XLA Ops:
  0.7 0.9 copy.24
  2.6 7.3 %all-to-all-start = ((s32[8,1,16]{2,1,0:T(1,128)}), s32[8,1,16]{2,1,0:T(1,128)S(1)}, u32[]{:S(2)}, u32[]{:S(2)}) async-start(s32[8,1,16]{2,1,0:T(1,128)} %bitcast), calls=%async_computation | async-start | bytes 8192 | tf_op jit(solution)/shard_map/all_to_all | solution.py:54
  9.9 6.4 %all-to-all-done = s32[8,1,16]{2,1,0:T(1,128)S(1)} async-done(((s32[8,1,16]{2,1,0:T(1,128)}), s32[8,1,16]{2,1,0:T(1,128)S(1)}, u32[]{:S(2)}, u32[]{:S(2)}) %all-to-all-start) | async-done | bytes 544 | tf_op jit(solution)/shard_map/all_to_all | solution.py:54
  17.5 1.1 convolution_convert_fusion
  18.7 3.5 %all-to-all-start.1 = ((bf16[8,16,2048]{2,1,0:T(8,128)(2,1)}), bf16[8,16,2048]{2,1,0:T(8,128)(2,1)S(1)}, u32[]{:S(2)}, u32[]{:S(2)}) async-start(bf16[8,16,2048]{2,1,0:T(8,128)(2,1)} %bitcast.1), calls=%async_computation.1 | async-start | bytes 1048576 | tf_op jit(solution)/shard_map/all_to_all | solution.py:64
  22.2 13.2 %all-to-all-done.1 = bf16[8,16,2048]{2,1,0:T(8,128)(2,1)S(1)} async-done(((bf16[8,16,2048]{2,1,0:T(8,128)(2,1)}), bf16[8,16,2048]{2,1,0:T(8,128)(2,1)S(1)}, u32[]{:S(2)}, u32[]{:S(2)}) %all-to-all-start.1) | async-done | bytes 524320 | tf_op jit(solution)/shard_map/all_to_all | solution.py:64
  35.8 0.9 broadcast_in_dim.46
  36.6 3.7 %all-to-all-start.2 = ((bf16[8,16,2048]{2,1,0:T(8,128)(2,1)}), bf16[8,16,2048]{2,1,0:T(8,128)(2,1)S(1)}, u32[]{:S(2)}, u32[]{:S(2)}) async-start(bf16[8,16,2048]{2,1,0:T(8,128)(2,1)} %broadcast_in_dim.46), calls=%async_computation.2 | async-start | bytes 1048576 | tf_op jit(solution)/shard_map/all_to_all | solution.py:69
  40.3 13.8 %all-to-all-done.2 = bf16[8,16,2048]{2,1,0:T(8,128)(2,1)S(1)} async-done(((bf16[8,16,2048]{2,1,0:T(8,128)(2,1)}), bf16[8,16,2048]{2,1,0:T(8,128)(2,1)S(1)}, u32[]{:S(2)}, u32[]{:S(2)}) %all-to-all-start.2) | async-done | bytes 524320 | tf_op jit(solution)/shard_map/all_to_all | solution.py:69
  54.1 2.2 %fusion.59 = f32[128,512]{1,0:T(8,128)S(1)} fusion(bf16[128,2048]{1,0:T(8,128)(2,1)S(1)} %bitcast.36, bf16[2048,512]{1,0:T(8,128)(2,1)} %param.14), kind=kOutput, calls=%fused_computation.100 | convolution fusion | flops 268435456 | bytes 2883584 | tf_op jit(solution)/shard_map/dot_general | solution.py:15
  56.4 3.5 %convolution_convert_fusion.3 = bf16[256,512]{1,0:T(8,128)(2,1)S(1)} fusion(bf16[256,4096]{1,0:T(8,128)(2,1)S(1)} %copy-done.1, bf16[512,4096]{1,0:T(8,128)(2,1)} %param.15), kind=kOutput, calls=%fused_computation.6 | convolution fusion | flops 1073872896 | bytes 6553600 | tf_op jit(solution)/shard_map/dot_general | solution.py:15
  60.6 0.9 fusion.58
  61.6 1.6 %dynamic-slice_add_fusion = f32[256,16]{1,0:T(8,128)S(1)} fusion(f32[256,128]{1,0:T(8,128)} %fusion.58, s32[]{:T(128)S(6)} %select_n.103, bf16[256,4096]{1,0:T(8,128)(2,1)S(1)} %copy-done.1, bf16[16,2048]{1,0:T(8,128)(2,1)S(1)} %collective-permute-done.1, bf16[16,2048]{1,0:T(8,128)(2,1)S(1)} %fusion, pred[]{:T(512)S(6)} %eq.50), kind=kOutput, calls=%fused_computation.36 | convolution fusion | flops 34148352 | bytes 2260997 | tf_op jit(solution)/shard_map/dot_general | solution.py:15
  63.2 1.6 %add.107 = f32[256,128]{1,0:T(8,128)} dynamic-update-slice(f32[256,128]{1,0:T(8,128)} %fusion.58, f32[256,16]{1,0:T(8,128)S(1)} %dynamic-slice_add_fusion, s32[]{:T(128)} %constant.102.clone.1, s32[]{:T(128)S(6)} %select_n.103) | dynamic-update-slice | bytes 32772 | tf_op jit(solution)/shard_map/add | solution.py:85
  64.7 3.8 %all-to-all-start.3 = ((f32[8,32,128]{2,1,0:T(8,128)}), f32[8,32,128]{2,1,0:T(8,128)S(1)}, u32[]{:S(2)}, u32[]{:S(2)}) async-start(f32[8,32,128]{2,1,0:T(8,128)} %bitcast.5), calls=%async_computation.3 | async-start | bytes 262144 | tf_op jit(solution)/shard_map/all_to_all | solution.py:89
  68.6 7.5 %all-to-all-done.3 = f32[8,32,128]{2,1,0:T(8,128)S(1)} async-done(((f32[8,32,128]{2,1,0:T(8,128)}), f32[8,32,128]{2,1,0:T(8,128)S(1)}, u32[]{:S(2)}, u32[]{:S(2)}) %all-to-all-start.3) | async-done | bytes 131104 | tf_op jit(solution)/shard_map/all_to_all | solution.py:89
  82.5 0.7 fusion.39
  83.3 0.7 broadcast_in_dim.48
  84.0 3.5 %all-to-all-start.4 = ((bf16[16,48,128]{2,1,0:T(8,128)(2,1)}), bf16[16,48,128]{2,1,0:T(8,128)(2,1)S(1)}, u32[]{:S(2)}, u32[]{:S(2)}) async-start(bf16[16,48,128]{2,1,0:T(8,128)(2,1)} %broadcast_in_dim.48), calls=%async_computation.4 | async-start | bytes 393216 | tf_op jit(solution)/shard_map/all_to_all | solution.py:109
  87.8 8.7 %all-to-all-done.4 = bf16[16,48,128]{2,1,0:T(8,128)(2,1)S(1)} async-done(((bf16[16,48,128]{2,1,0:T(8,128)(2,1)}), bf16[16,48,128]{2,1,0:T(8,128)(2,1)S(1)}, u32[]{:S(2)}, u32[]{:S(2)}) %all-to-all-start.4) | async-done | bytes 196640 | tf_op jit(solution)/shard_map/all_to_all | solution.py:109
  96.7 6.5 %fusion.1 = f32[512,4096]{1,0:T(8,128)} fusion(bf16[256,4096]{1,0:T(8,128)(2,1)} %param.9, bf16[256,128]{1,0:T(8,128)(2,1)S(1)} %bitcast.42, f32[128,512]{1,0:T(8,128)S(1)} %add.103), kind=kOutput, calls=%fused_computation.7 | convolution fusion | flops 1108017152 | bytes 10813440 | tf_op jit(solution)/shard_map/dot_general | solution.py:15
  103.2 8.9 %convolution_add_fusion = f32[512,4096]{1,0:T(8,128)} fusion(f32[512,4096]{1,0:T(8,128)} %fusion.1, bf16[256,4096]{1,0:T(8,128)(2,1)} %collective-permute-done.3, bf16[256,128]{1,0:T(8,128)(2,1)S(1)} %bitcast.40, f32[128,512]{1,0:T(8,128)S(1)} %add.103), kind=kOutput, calls=%fused_computation | convolution fusion | flops 1110114304 | bytes 19202048 | tf_op jit(solution)/shard_map/dot_general | solution.py:15
  113.4 1.2 fusion.60
  114.5 3.0 %fusion.12 = f32[2048,512]{1,0:T(8,128)} fusion(bf16[128,2048]{1,0:T(8,128)(2,1)S(1)} %bitcast.37, f32[128,512]{1,0:T(8,128)S(1)} %add.103, f32[128,512]{1,0:T(8,128)S(1)} %fusion.60, bf16[256,128]{1,0:T(8,128)(2,1)S(1)} %bitcast.41, bf16[256,512]{1,0:T(8,128)(2,1)S(1)} %collective-permute-done.2), kind=kOutput, calls=%fused_computation.24 | convolution fusion | flops 303366144 | bytes 5570560 | tf_op jit(solution)/shard_map/dot_general | solution.py:15
  (46 shorter events, 5.6 us)
Async XLA Ops:
  0.6 16.9 %copy-start = (bf16[256,4096]{1,0:T(8,128)(2,1)S(1)}, bf16[256,4096]{1,0:T(8,128)(2,1)}, u32[]{:S(2)}) copy-start(bf16[256,4096]{1,0:T(8,128)(2,1)} %param.11) | copy-start | bytes 6291460
  0.6 21.6 %copy-start.4 = (s32[16]{0:T(128)S(1)}, s32[16]{0:T(128)}, u32[]{:S(2)}) copy-start(s32[16]{0:T(128)} %param.13) | copy-start | bytes 196
  2.6 13.6 %all-to-all-start = ((s32[8,1,16]{2,1,0:T(1,128)}), s32[8,1,16]{2,1,0:T(1,128)S(1)}, u32[]{:S(2)}, u32[]{:S(2)}) async-start(s32[8,1,16]{2,1,0:T(1,128)} %bitcast), calls=%async_computation | async-start | bytes 8192 | tf_op jit(solution)/shard_map/all_to_all | solution.py:54
  18.7 16.8 %all-to-all-start.1 = ((bf16[8,16,2048]{2,1,0:T(8,128)(2,1)}), bf16[8,16,2048]{2,1,0:T(8,128)(2,1)S(1)}, u32[]{:S(2)}, u32[]{:S(2)}) async-start(bf16[8,16,2048]{2,1,0:T(8,128)(2,1)} %bitcast.1), calls=%async_computation.1 | async-start | bytes 1048576 | tf_op jit(solution)/shard_map/all_to_all | solution.py:64
  36.6 17.5 %all-to-all-start.2 = ((bf16[8,16,2048]{2,1,0:T(8,128)(2,1)}), bf16[8,16,2048]{2,1,0:T(8,128)(2,1)S(1)}, u32[]{:S(2)}, u32[]{:S(2)}) async-start(bf16[8,16,2048]{2,1,0:T(8,128)(2,1)} %broadcast_in_dim.46), calls=%async_computation.2 | async-start | bytes 1048576 | tf_op jit(solution)/shard_map/all_to_all | solution.py:69
  40.3 62.9 %collective-permute-start.3 = (bf16[256,4096]{1,0:T(8,128)(2,1)}, bf16[256,4096]{1,0:T(8,128)(2,1)}, u32[]{:S(2)}, u32[]{:S(2)}) collective-permute-start(bf16[256,4096]{1,0:T(8,128)(2,1)} %param.9), channel_id=1, source_target_pairs={{0,1},{1,0},{2,3},{3,2},{4,5},{5,4},{6,7},{7,6},{8,9},{9,8},{10,11... | collective-permute-start | bytes 6291464 | tf_op jit(solution)/shard_map/ppermute | solution.py:55
  54.1 2.3 %copy-start.1 = (bf16[256,4096]{1,0:T(8,128)(2,1)S(1)}, bf16[256,4096]{1,0:T(8,128)(2,1)}, u32[]{:S(2)}) copy-start(bf16[256,4096]{1,0:T(8,128)(2,1)} %param.9) | copy-start | bytes 6291460
  56.3 4.1 %collective-permute-start = (f32[128,512]{1,0:T(8,128)S(1)}, f32[128,512]{1,0:T(8,128)S(1)}, u32[]{:S(2)}, u32[]{:S(2)}) collective-permute-start(f32[128,512]{1,0:T(8,128)S(1)} %fusion.59), channel_id=1, source_target_pairs={{0,1},{1,0},{2,3},{3,2},{4,5},{5,4},{6,7},{7,6},{8,9},{9,8},{10,11... | collective-permute-start | bytes 786440 | tf_op jit(solution)/shard_map/ppermute | solution.py:81
  59.9 0.7 copy-start.2
  59.9 1.6 %collective-permute-start.1 = (bf16[16,2048]{1,0:T(8,128)(2,1)S(1)}, bf16[16,2048]{1,0:T(8,128)(2,1)S(1)}, u32[]{:S(2)}, u32[]{:S(2)}) collective-permute-start(bf16[16,2048]{1,0:T(8,128)(2,1)S(1)} %fusion), channel_id=1, source_target_pairs={{0,1},{1,0},{2,3},{3,2},{4,5},{5,4},{6,7},{7,6},{8,9},{9,8},{10,11... | collective-permute-start | bytes 196616 | tf_op jit(solution)/shard_map/ppermute | solution.py:72
  60.6 7.9 %copy-start.3 = (s32[256]{0:T(256)S(1)}, s32[256]{0:T(256)}, u32[]{:S(2)}) copy-start(s32[256]{0:T(256)} %param.10) | copy-start | bytes 3076
  64.7 11.4 %all-to-all-start.3 = ((f32[8,32,128]{2,1,0:T(8,128)}), f32[8,32,128]{2,1,0:T(8,128)S(1)}, u32[]{:S(2)}, u32[]{:S(2)}) async-start(f32[8,32,128]{2,1,0:T(8,128)} %bitcast.5), calls=%async_computation.3 | async-start | bytes 262144 | tf_op jit(solution)/shard_map/all_to_all | solution.py:89
  84.0 12.5 %all-to-all-start.4 = ((bf16[16,48,128]{2,1,0:T(8,128)(2,1)}), bf16[16,48,128]{2,1,0:T(8,128)(2,1)S(1)}, u32[]{:S(2)}, u32[]{:S(2)}) async-start(bf16[16,48,128]{2,1,0:T(8,128)(2,1)} %broadcast_in_dim.48), calls=%async_computation.4 | async-start | bytes 393216 | tf_op jit(solution)/shard_map/all_to_all | solution.py:109
  87.6 27.0 %collective-permute-start.2 = (bf16[256,512]{1,0:T(8,128)(2,1)}, bf16[256,512]{1,0:T(8,128)(2,1)S(1)}, u32[]{:S(2)}, u32[]{:S(2)}) collective-permute-start(bf16[256,512]{1,0:T(8,128)(2,1)} %copy-done.2), channel_id=1, source_target_pairs={{0,1},{1,0},{2,3},{3,2},{4,5},{5,4},{6,7},{7,6},{8,9},{9,8},{10,11... | collective-permute-start | bytes 786440 | tf_op jit(solution)/shard_map/ppermute | solution.py:57

commit v2 on v1

v2 whole, which is shorter than its diff:
```python
import functools

import jax
import jax.numpy as jnp
from jax import lax
from jax.experimental import pallas as pl
from jax.experimental.pallas import tpu as pltpu
from jax.sharding import PartitionSpec as P

LAST = (((1,), (1,)), ((), ()))
FIRST = (((0,), (0,)), ((), ()))
PLAIN = (((1,), (0,)), ((), ()))
VMEM_LIMIT = 50 * 1024 * 1024


def activate(values):
    return jax.nn.gelu(values, approximate=True)


def dot(a, b, dims=PLAIN):
    return lax.dot_general(a, b, dims, preferred_element_type=jnp.float32)


def iota(shape, dim):
    return lax.broadcasted_iota(jnp.int32, shape, dim)


def cost(flops, moved):
    return pl.CostEstimate(flops=int(flops), bytes_accessed=int(moved), transcendentals=0)


def whole_call(body, outs, args, flops=1 << 24, moved=1 << 20):
    return pl.pallas_call(
        body,
        out_shape=outs,
        in_specs=[pl.BlockSpec(memory_space=pltpu.VMEM)] * len(args),
        out_specs=jax.tree.map(lambda _: pl.BlockSpec(memory_space=pltpu.VMEM), outs),
        compiler_params=pltpu.CompilerParams(vmem_limit_bytes=VMEM_LIMIT),
        cost_estimate=cost(flops, moved),
    )(*args)


def place_body(old_rows, groups, capacity, decomp_ref, asked_ref, adder_ref):
    new_rows, k_slots = decomp_ref.shape
    slots, places = new_rows * k_slots, groups * capacity
    lanes = max(groups, 128)
    ids = decomp_ref[...]
    flat = jnp.concatenate(
        [jnp.broadcast_to(ids[:, k : k + 1], (new_rows, lanes)) for k in range(k_slots)], 0
    )
    usable = flat >= 0
    owners = jnp.where(usable, flat // old_rows, groups)
    local = jnp.where(usable, flat - owners * old_rows, 0)
    onehot = (owners == iota((slots, lanes), 1)) & usable
    earlier = (iota((slots, slots), 1) < iota((slots, slots), 0)).astype(jnp.bfloat16)
    hits = jnp.where(onehot, 1.0, 0.0)
    before = dot(earlier, hits.astype(jnp.bfloat16))
    ranking = jnp.sum(before * hits, 1, keepdims=True).astype(jnp.int32)
    place = jnp.where(usable, owners * capacity + ranking, -1)[:, :1]
    taken = jnp.where(place == iota((slots, places), 1), 1.0, 0.0)
    wanted = (local[:, :128] + 1).astype(jnp.float32)
    asked = lax.dot_general(
        taken.T, wanted, PLAIN, precision=lax.Precision.HIGHEST, preferred_element_type=jnp.float32
    )
    asked_ref[...] = asked.astype(jnp.int32) - 1
    rows = groups * new_rows
    mine = (iota((rows, slots), 1) % new_rows) == (iota((rows, slots), 0) % new_rows)
    adder_ref[...] = dot(
        jnp.where(mine, 1.0, 0.0).astype(jnp.bfloat16), taken.astype(jnp.bfloat16)
    ).astype(jnp.bfloat16)


def share_body(pre_own_ref, pre_other_ref, basis_ref, direct_ref, pre_ref, units_ref, share_ref):
    pre = pre_own_ref[...] + pre_other_ref[...]
    pre_ref[...] = pre
    units = activate(pre).astype(jnp.bfloat16)
    units_ref[...] = units
    share_ref[...] = dot(basis_ref[...], units, LAST) + direct_ref[...]


def softmax_body(shares_ref, targets_ref, packets_ref):
    copies, rows, columns = packets_ref.shape
    tokens = shares_ref.shape[1]
    logits = shares_ref[0]
    for index in range(1, shares_ref.shape[0]):
        logits = logits + shares_ref[index]
    row_top = jnp.max(logits, 1, keepdims=True)
    log_totals = row_top + jnp.log(jnp.sum(jnp.exp(logits - row_top), 1, keepdims=True))
    hits = targets_ref[...] == iota((tokens, columns), 1)
    picked = jnp.sum(jnp.where(hits, logits, 0.0), 1, keepdims=True)
    loss = jnp.sum(log_totals - picked, 0, keepdims=True)
    dlogits = jnp.exp(logits - log_totals) - jnp.where(hits, 1.0, 0.0)
    high = lax.reduce_precision(loss, 8, 7)
    middle = lax.reduce_precision(loss - high, 8, 7)
    low = lax.reduce_precision(loss - high - middle, 8, 7)
    lane = iota((rows - tokens, columns), 1)
    extra = jnp.where(
        lane == 0, high, jnp.where(lane == 1, middle, jnp.where(lane == 2, low, 0.0))
    )
    packet = jnp.concatenate([dlogits, extra], 0).astype(jnp.bfloat16)
    for index in range(copies):
        packets_ref[index] = packet


def final_body(
    own_dl_ref,
    other_dl_ref,
    units_ref,
    pre_ref,
    own_basis_ref,
    other_basis_ref,
    own_hidden_ref,
    other_hidden_ref,
    new_ref,
    grad_in_ref,
    grad_out_ref,
    mixed_ref,
    grad_pre_ref,
):
    tokens = own_dl_ref.shape[0]

    @pl.when(pl.program_id(0) == 0)
    def _():
        units = units_ref[...]
        mixed_ref[:, :tokens] = dot(own_dl_ref[...], units).T.astype(jnp.bfloat16)
        mixed_ref[:, tokens:] = dot(other_dl_ref[...], units).T.astype(jnp.bfloat16)
        grad_units = dot(own_dl_ref[...], own_basis_ref[...], FIRST) + dot(
            other_dl_ref[...], other_basis_ref[...], FIRST
        )
        grad_pre_ref[...] = jax.vjp(activate, pre_ref[...])[1](grad_units)[0].astype(jnp.bfloat16)

    grad_out_ref[...] = dot(mixed_ref[:, :tokens], own_hidden_ref[...]) + dot(
        mixed_ref[:, tokens:], other_hidden_ref[...]
    )
    grad_in_ref[...] = dot(new_ref[...], grad_pre_ref[...], FIRST)


def final_call(own_dl, other_dl, units, pre, own_basis, other_basis, own_hidden, other_hidden, new):
    steps = 8
    tokens, width = own_hidden.shape
    columns, hidden = pre.shape
    half = new.shape[1]

    def fixed(array):
        return pl.BlockSpec(array.shape, lambda j: (0, 0))

    def cut(array):
        return pl.BlockSpec((array.shape[0], array.shape[1] // steps), lambda j: (0, j))

    return pl.pallas_call(
        final_body,
        grid=(steps,),
        out_shape=(
            jax.ShapeDtypeStruct((half, hidden), jnp.float32),
            jax.ShapeDtypeStruct((hidden, width), jnp.float32),
        ),
        in_specs=[
            fixed(own_dl),
            fixed(other_dl),
            fixed(units),
            fixed(pre),
            fixed(own_basis),
            fixed(other_basis),
            cut(own_hidden),
            cut(other_hidden),
            cut(new),
        ],
        out_specs=(
            pl.BlockSpec((half // steps, hidden), lambda j: (j, 0)),
            pl.BlockSpec((hidden, width // steps), lambda j: (0, j)),
        ),
        scratch_shapes=[
            pltpu.VMEM((hidden, 2 * tokens), jnp.bfloat16),
            pltpu.VMEM((columns, hidden), jnp.bfloat16),
        ],
        compiler_params=pltpu.CompilerParams(vmem_limit_bytes=VMEM_LIMIT),
        cost_estimate=cost(4 * tokens * hidden * width, 4 * (half + width) * hidden),
    )(own_dl, other_dl, units, pre, own_basis, other_basis, own_hidden, other_hidden, new)


def exchange(array, axes="vocab"):
    return lax.all_to_all(array, axes, 0, 0, tiled=True)


def shards(hidden_states, targets, old_embed, decomp, counts, w_in, w_out):
    new_rows, k_slots = decomp.shape
    old_rows, width = old_embed.shape
    groups = lax.axis_size("vocab")
    cores = lax.axis_size("dp")
    own_index = lax.axis_index("vocab")
    dp_index = lax.axis_index("dp")
    tokens = hidden_states.shape[0]
    half_width, hidden = w_in.shape
    columns = groups * new_rows
    capacity = max(2, new_rows * k_slots // groups)
    places = groups * capacity
    swap = [(0, 1), (1, 0)]
    shaped = jax.ShapeDtypeStruct

    asked, adder = whole_call(
        functools.partial(place_body, old_rows, groups, capacity),
        (shaped((places, 128), jnp.int32), shaped((columns, places), jnp.bfloat16)),
        (decomp,),
    )
    look = exchange(asked.reshape(groups, capacity, 128))
    hidden_other = lax.ppermute(hidden_states, "dp", swap)
    basis = dot(hidden_states, w_out, LAST).astype(jnp.bfloat16)
    basis_other = lax.ppermute(basis, "dp", swap)
    old_half = lax.dynamic_slice_in_dim(old_embed, dp_index * half_width, half_width, 1)
    scale = jnp.tile(counts.astype(jnp.float32), groups)[:, None]
    look, old_half, basis, scale, adder = lax.optimization_barrier(
        (look, old_half, basis, scale, adder)
    )

    select = look.reshape(places, 128)[:, :1] == iota((places, old_rows), 1)
    fetched = dot(select.astype(jnp.bfloat16), old_half).astype(jnp.bfloat16)
    arrived = exchange(fetched.reshape(groups, capacity, half_width)).reshape(places, half_width)

    new_copies = (dot(adder, arrived) / scale).astype(jnp.bfloat16)
    new_all = exchange(new_copies.reshape(groups, new_rows, half_width)).reshape(
        columns, half_width
    )
    new_own = new_copies[:new_rows]
    new_other = lax.ppermute(new_own, "dp", swap)
    new_wide = jnp.where(
        dp_index == 0,
        jnp.concatenate([new_own, new_other], 1),
        jnp.concatenate([new_other, new_own], 1),
    )
    direct = lax.dynamic_update_slice(
        jnp.zeros((tokens, columns), jnp.float32),
        dot(hidden_states, new_wide, LAST),
        (0, own_index * new_rows),
    )
    new_all, direct = lax.optimization_barrier((new_all, direct))

    pre_own = dot(new_all, w_in)
    pre_other = lax.ppermute(pre_own, "dp", swap)
    pre_units, hidden_units, share = whole_call(
        share_body,
        (
            shaped((columns, hidden), jnp.float32),
            shaped((columns, hidden), jnp.bfloat16),
            shaped((tokens, columns), jnp.float32),
        ),
        (pre_own, pre_other, basis, direct),
    )

    own_tokens = tokens // groups
    shares = exchange(share.reshape(groups, own_tokens, columns))
    own_targets = lax.dynamic_slice_in_dim(targets, own_index * own_tokens, own_tokens)
    packet_rows = (own_tokens + 16) // 16 * 16
    packets = whole_call(
        softmax_body,
        shaped((groups * cores, packet_rows, columns), jnp.bfloat16),
        (shares, own_targets[:, None]),
    )
    packets = exchange(packets, ("vocab", "dp")).reshape(groups, cores, packet_rows, columns)
    loss_value = (
        jnp.sum(packets[:, :, own_tokens, :3].astype(jnp.float32)) / (tokens * cores)
    ).reshape(1)

    def part(index):
        return lax.dynamic_index_in_dim(packets, index, 1, False)[:, :own_tokens].reshape(
            tokens, columns
        )

    grad_in, grad_out = final_call(
        part(dp_index),
        part(1 - dp_index),
        hidden_units,
        pre_units,
        basis,
        basis_other,
        hidden_states,
        hidden_other,
        new_all,
    )
    return (loss_value, grad_in, grad_out)


def solution(mesh):
    in_specs = (
        P(("groups", "dp"), None),
        P(("groups", "dp")),
        P("vocab", None),
        P(("groups", "vocab"), None),
        P(("groups", "vocab")),
        P("dp", "vocab"),
        P("vocab", None),
    )
    out_specs = (P("groups"), P(("groups", "dp"), "vocab"), P(("groups", "vocab"), None))
    return jax.shard_map(shards, mesh=mesh, in_specs=in_specs, out_specs=out_specs, check_vma=False)
```

time: 119 us -> 103 us (0.87)
  waiting for transfers between devices: 49.6 us -> 28.8 us
  matrix products: 29.4 us -> 11.1 us
  blocking collectives: 0 us -> 18.1 us
  Pallas kernels: 0 us -> 12.3 us
  between operations: 8.08 us -> 2.58 us
  starting transfers between devices: 22.6 us -> 19.5 us
  local copies, waits for them, and re-layouts: 5.76 us -> 7.98 us
  other arithmetic: 3.18 us -> 1.38 us
    all_to_all x5 -> x4, waiting for transfers between devices: 49.6 us -> 24.4 us  [exchange(): return lax.all_to_all(array, axes, 0, 0, tiled=True)]
    dot_general x11 -> x5, matrix products: 29.4 us -> 11.1 us  [dot(): return lax.dot_general(a, b, dims, preferred_element_type=jnp.float32)]
    all_to_all x0 -> x1, blocking collectives: none -> 18.1 us  [exchange(): return lax.all_to_all(array, axes, 0, 0, tiled=True)]
    pallas_call x0 -> x4, Pallas kernels: none -> 12.3 us  [the longest x1 9.16 us: final_call(): pl.pallas_call(final_body, grid=(steps,), out_shape=(jax.ShapeDtypeStruct...]
    all_to_all x5 -> x4, starting transfers between devices: 21.7 us -> 18.7 us  [exchange(): return lax.all_to_all(array, axes, 0, 0, tiled=True)]
    unnamed x12 -> x13, local copies, waits for them, and re-layouts: 1.13 us -> 4.07 us
    ppermute x1, waiting for transfers between devices: 0.01 us -> 2.9 us  [shards(): new_other = lax.ppermute(new_own, 'dp', swap)]
    add x1 -> x0, local copies, waits for them, and re-layouts: 1.59 us -> none  [shards(): share + lax.dynamic_update_slice(jnp.zeros((tokens, columns_all), jnp.flo...]
  transfers between devices with their start and end apart: 9 -> 8, of which waited for: 5 -> 6; matrix products, arithmetic and copies ran while one was open for 25% -> 13% of each run, Pallas kernels for 0% -> 2%
where the time goes in v2:
time: 103 us; the launch traced here: 102 us
  waiting for transfers between devices  28.8 us (28%)
  starting transfers between devices  19.5 us (19%)
  blocking collectives  18.1 us (18%)
  Pallas kernels  12.3 us (12%)
  matrix products  11.1 us (11%)
  local copies, waits for them, and re-layouts  7.98 us (8%)
  between operations  2.58 us (3%)
  other arithmetic  1.38 us (1%)
    all_to_all x4, waiting for transfers between devices, exchange(): return lax.all_to_all(array, axes, 0, 0, tiled=True)  24.4 us
    all_to_all x4, starting transfers between devices, exchange(): return lax.all_to_all(array, axes, 0, 0, tiled=True)  18.7 us
    all_to_all x1, blocking collectives, exchange(): return lax.all_to_all(array, axes, 0, 0, tiled=True)  18.1 us
    dot_general x5, matrix products, dot(): return lax.dot_general(a, b, dims, preferred_element_type=jnp.float32)  11.1 us
    pallas_call x1, Pallas kernels, final_call(): pl.pallas_call(final_body, grid=(steps,), out_shape=(jax.ShapeDtypeStruct...  9.16 us
    unnamed x13, local copies, waits for them, and re-layouts  4.07 us
    pallas_call x3, Pallas kernels, whole_call(): pl.pallas_call(body, out_shape=outs, in_specs=[pl.BlockSpec(memory_space=...  3.16 us
    ppermute x1, waiting for transfers between devices, shards(): new_other = lax.ppermute(new_own, 'dp', swap)  2.9 us
  transfers between devices with their start and end apart: 8, of which 6 were waited for; matrix products, arithmetic and copies ran while one was open for 13% of the time, Pallas kernels for 2%

profile of v2, /device:TPU:0, one launch (start us, length us, event | category | flops | bytes accessed | tf_op | source)
XLA Modules:
  0.0 101.8 jit_solution(8447896037599649799)
XLA Ops:
  0.6 0.9 copy.17.decomp_ref
  1.6 1.3 %shard_map.94 = (s32[128,128]{1,0:T(8,128)}, bf16[128,128]{1,0:T(8,128)(2,1)S(1)}) custom-call(s32[16,8]{1,0:T(8,128)S(1)} %copy.17.decomp_ref), custom_call_target="tpu_custom_call" | custom-call | flops 16777216 | bytes 1048576 | tf_op jit(solution)/shard_map/pallas_call | solution.py:33
  2.9 7.3 %all-to-all-start = ((s32[8,16,128]{2,1,0:T(8,128)}), s32[8,16,128]{2,1,0:T(8,128)S(1)}, u32[]{:S(2)}, u32[]{:S(2)}) async-start(s32[8,16,128]{2,1,0:T(8,128)} %bitcast), calls=%async_computation | async-start | bytes 131072 | tf_op jit(solution)/shard_map/all_to_all | solution.py:182
  10.1 4.1 %convolution_convert_fusion.1.basis_ref.own_basis_ref = bf16[256,512]{1,0:T(8,128)(2,1)S(1)} fusion(bf16[256,4096]{1,0:T(8,128)(2,1)} %own_hidden_ref.1, bf16[512,4096]{1,0:T(8,128)(2,1)} %param.13), kind=kOutput, calls=%fused_computation.3 | convolution fusion | flops 1073872896 | bytes 6553600 | tf_op jit(solution)/shard_map/dot_general | solution.py:21
  14.3 1.1 %constant_dynamic-slice_fusion = bf16[256,2048]{1,0:T(8,128)(2,1)} fusion(bf16[256,4096]{1,0:T(8,128)(2,1)S(1)} %copy-done, s32[]{:T(128)S(6)} %select_n.24), kind=kLoop, calls=%fused_computation.19 | loop fusion | bytes 2097156 | tf_op jit(solution)/shard_map/dynamic_slice | solution.py:209
  15.4 1.6 %all-to-all-done = s32[8,16,128]{2,1,0:T(8,128)S(1)} async-done(((s32[8,16,128]{2,1,0:T(8,128)}), s32[8,16,128]{2,1,0:T(8,128)S(1)}, u32[]{:S(2)}, u32[]{:S(2)}) %all-to-all-start) | async-done | bytes 65568 | tf_op jit(solution)/shard_map/all_to_all | solution.py:182
  17.1 1.6 %convolution_convert_fusion = bf16[128,2048]{1,0:T(8,128)(2,1)S(1)} fusion(bf16[256,2048]{1,0:T(8,128)(2,1)} %constant_dynamic-slice_fusion, s32[128]{0:T(128)S(1)} %slice_reduce_fusion), kind=kOutput, calls=%fused_computation.2 | convolution fusion | flops 134512640 | bytes 1573376 | tf_op jit(solution)/shard_map/dot_general | solution.py:21
  18.7 18.1 %all_to_all.25 = bf16[8,16,2048]{2,1,0:T(8,128)(2,1)S(1)} all-to-all(bf16[8,16,2048]{2,1,0:T(8,128)(2,1)S(1)} %bitcast.32), channel_id=1, replica_groups=mesh['groups'=2,'vocab'=8,'dp'=2] {'vocab'}, dimensions={0} | all-to-all | bytes 1048576 | tf_op jit(solution)/shard_map/all_to_all | solution.py:182
  36.9 1.1 %fusion = bf16[128,2048]{1,0:T(8,128)(2,1)} fusion(bf16[128,128]{1,0:T(8,128)(2,1)S(1)} %get-tuple-element.19, bf16[128,2048]{1,0:T(8,128)(2,1)S(1)} %bitcast.33, f32[128]{0:T(128)S(1)} %bitcast.35), kind=kOutput, calls=%fused_computation.1 | convolution fusion | flops 67633152 | bytes 1081856 | tf_op jit(solution)/shard_map/dot_general | solution.py:21
  37.9 3.6 %all-to-all-start.2 = ((bf16[8,16,2048]{2,1,0:T(8,128)(2,1)}), bf16[8,16,2048]{2,1,0:T(8,128)(2,1)S(1)}, u32[]{:S(2)}, u32[]{:S(2)}) async-start(bf16[8,16,2048]{2,1,0:T(8,128)(2,1)} %bitcast.5), calls=%async_computation.2 | async-start | bytes 1048576 | tf_op jit(solution)/shard_map/all_to_all | solution.py:182
  42.9 2.9 %collective-permute-done = bf16[16,2048]{1,0:T(8,128)(2,1)S(1)} collective-permute-done((bf16[16,2048]{1,0:T(8,128)(2,1)S(1)}, bf16[16,2048]{1,0:T(8,128)(2,1)S(1)}, u32[]{:S(2)}, u32[]{:S(2)}) %collective-permute-start) | collective-permute-done | bytes 65568 | tf_op jit(solution)/shard_map/ppermute | solution.py:224
  45.8 2.3 %convolution_bitcast_fusion = f32[256,16]{1,0:T(8,128)S(1)} fusion(bf16[256,4096]{1,0:T(8,128)(2,1)} %own_hidden_ref.1, bf16[16,2048]{1,0:T(8,128)(2,1)S(1)} %collective-permute-done, bf16[16,2048]{1,0:T(8,128)(2,1)S(1)} %slice.21, pred[]{:T(512)S(6)} %eq.16), kind=kOutput, calls=%fused_computation.4 | convolution fusion | flops 34144256 | bytes 2244609 | tf_op jit(solution)/shard_map/dot_general | solution.py:21
  48.8 6.9 %all-to-all-done.2 = bf16[8,16,2048]{2,1,0:T(8,128)(2,1)S(1)} async-done(((bf16[8,16,2048]{2,1,0:T(8,128)(2,1)}), bf16[8,16,2048]{2,1,0:T(8,128)(2,1)S(1)}, u32[]{:S(2)}, u32[]{:S(2)}) %all-to-all-start.2) | async-done | bytes 524320 | tf_op jit(solution)/shard_map/all_to_all | solution.py:182
  55.6 2.0 %fusion.10.pre_own_ref = f32[128,512]{1,0:T(8,128)S(1)} fusion(bf16[128,2048]{1,0:T(8,128)(2,1)S(1)} %bitcast.28, bf16[2048,512]{1,0:T(8,128)(2,1)} %param.12), kind=kOutput, calls=%fused_computation.22 | convolution fusion | flops 268435456 | bytes 2883584 | tf_op jit(solution)/shard_map/dot_general | solution.py:21
  57.7 1.5 %collective-permute-done.1.pre_other_ref = f32[128,512]{1,0:T(8,128)S(1)} collective-permute-done((f32[128,512]{1,0:T(8,128)S(1)}, f32[128,512]{1,0:T(8,128)S(1)}, u32[]{:S(2)}, u32[]{:S(2)}) %collective-permute-start.1) | collective-permute-done | bytes 262176 | tf_op jit(solution)/shard_map/ppermute | solution.py:238
  59.3 1.0 shard_map.95
  60.9 3.6 %all-to-all-start.3 = ((f32[8,32,128]{2,1,0:T(8,128)}), f32[8,32,128]{2,1,0:T(8,128)S(1)}, u32[]{:S(2)}, u32[]{:S(2)}) async-start(f32[8,32,128]{2,1,0:T(8,128)} %bitcast.8), calls=%async_computation.3 | async-start | bytes 262144 | tf_op jit(solution)/shard_map/all_to_all | solution.py:182
  64.7 7.2 %all-to-all-done.3.shares_ref = f32[8,32,128]{2,1,0:T(8,128)S(1)} async-done(((f32[8,32,128]{2,1,0:T(8,128)}), f32[8,32,128]{2,1,0:T(8,128)S(1)}, u32[]{:S(2)}, u32[]{:S(2)}) %all-to-all-start.3) | async-done | bytes 131104 | tf_op jit(solution)/shard_map/all_to_all | solution.py:182
  72.8 4.2 %all-to-all-start.4 = ((bf16[16,48,128]{2,1,0:T(8,128)(2,1)}), bf16[16,48,128]{2,1,0:T(8,128)(2,1)}, u32[]{:S(2)}, u32[]{:S(2)}) async-start(bf16[16,48,128]{2,1,0:T(8,128)(2,1)} %shard_map.96), calls=%async_computation.4 | async-start | bytes 393216 | tf_op jit(solution)/shard_map/all_to_all | solution.py:182
  77.2 8.8 %all-to-all-done.4 = bf16[16,48,128]{2,1,0:T(8,128)(2,1)} async-done(((bf16[16,48,128]{2,1,0:T(8,128)(2,1)}), bf16[16,48,128]{2,1,0:T(8,128)(2,1)}, u32[]{:S(2)}, u32[]{:S(2)}) %all-to-all-start.4) | async-done | bytes 196640 | tf_op jit(solution)/shard_map/all_to_all | solution.py:182
  86.0 1.0 dynamic-slice_bitcast_fusion
  86.9 1.4 %fusion.8 = f32[]{:T(128)} fusion(bf16[8,2,48,128]{3,2,1,0:T(8,128)(2,1)} %bitcast.10), kind=kLoop, calls=%fused_computation.18 | loop fusion | flops 95 | bytes 100 | tf_op jit(solution)/shard_map/reduce_sum | solution.py:260
  89.0 1.6 %copy-done.1 = bf16[256,4096]{1,0:T(8,128)(2,1)S(1)} copy-done((bf16[256,4096]{1,0:T(8,128)(2,1)S(1)}, bf16[256,4096]{1,0:T(8,128)(2,1)}, u32[]{:S(2)}) %copy-start.1) | copy-done | bytes 2097176
  91.5 9.2 %shard_map.97 = (f32[2048,512]{1,0:T(8,128)}, f32[512,4096]{1,0:T(8,128)}) custom-call(bf16[256,128]{1,0:T(8,128)(2,1)S(1)} %bitcast.31, bf16[256,128]{1,0:T(8,128)(2,1)S(1)} %bitcast.30, bf16[128,512]{1,0:T(8,128)(2,1)S(1)} %copy-done.3, f32[128,512]{1,0:T(8,128)S(1)} %get-tuple-element.28.pre_ref, ...), custom_call_target="tpu_custom_call" | custom-call | flops 2147483648 | bytes 12582912 | tf_op jit(solution)/shard_map/pallas_call | solution.py:150
  (29 shorter events, 5.2 us)
Async XLA Ops:
  0.6 13.6 %copy-start = (bf16[256,4096]{1,0:T(8,128)(2,1)S(1)}, bf16[256,4096]{1,0:T(8,128)(2,1)}, u32[]{:S(2)}) copy-start(bf16[256,4096]{1,0:T(8,128)(2,1)} %param.9) | copy-start | bytes 6291460
  2.9 14.2 %all-to-all-start = ((s32[8,16,128]{2,1,0:T(8,128)}), s32[8,16,128]{2,1,0:T(8,128)S(1)}, u32[]{:S(2)}, u32[]{:S(2)}) async-start(s32[8,16,128]{2,1,0:T(8,128)} %bitcast), calls=%async_computation | async-start | bytes 131072 | tf_op jit(solution)/shard_map/all_to_all | solution.py:182
  14.2 1.1 %copy-start.5 = (s32[16]{0:T(128)S(1)}, s32[16]{0:T(128)}, u32[]{:S(2)}) copy-start(s32[16]{0:T(128)} %param.11) | copy-start | bytes 196
  37.9 17.7 %all-to-all-start.2 = ((bf16[8,16,2048]{2,1,0:T(8,128)(2,1)}), bf16[8,16,2048]{2,1,0:T(8,128)(2,1)S(1)}, u32[]{:S(2)}, u32[]{:S(2)}) async-start(bf16[8,16,2048]{2,1,0:T(8,128)(2,1)} %bitcast.5), calls=%async_computation.2 | async-start | bytes 1048576 | tf_op jit(solution)/shard_map/all_to_all | solution.py:182
  41.6 47.4 %collective-permute-start.3 = (bf16[256,4096]{1,0:T(8,128)(2,1)}, bf16[256,4096]{1,0:T(8,128)(2,1)}, u32[]{:S(2)}, u32[]{:S(2)}) collective-permute-start(bf16[256,4096]{1,0:T(8,128)(2,1)} %own_hidden_ref.1), channel_id=1, source_target_pairs={{0,1},{1,0},{2,3},{3,2},{4,5},{5,4},{6,7},{7,6},{8,9},{9,8},{10,11... | collective-permute-start | bytes 6291464 | tf_op jit(solution)/shard_map/ppermute | solution.py:206
  42.4 3.4 %collective-permute-start = (bf16[16,2048]{1,0:T(8,128)(2,1)S(1)}, bf16[16,2048]{1,0:T(8,128)(2,1)S(1)}, u32[]{:S(2)}, u32[]{:S(2)}) collective-permute-start(bf16[16,2048]{1,0:T(8,128)(2,1)S(1)} %slice.21), channel_id=1, source_target_pairs={{0,1},{1,0},{2,3},{3,2},{4,5},{5,4},{6,7},{7,6},{8,9},{9,8},{10,11... | collective-permute-start | bytes 196616 | tf_op jit(solution)/shard_map/ppermute | solution.py:224
  48.8 15.8 %copy-start.4 = (s32[256]{0:T(256)S(1)}, s32[256]{0:T(256)}, u32[]{:S(2)}) copy-start(s32[256]{0:T(256)} %param.8) | copy-start | bytes 3076
  57.7 1.6 %collective-permute-start.1 = (f32[128,512]{1,0:T(8,128)S(1)}, f32[128,512]{1,0:T(8,128)S(1)}, u32[]{:S(2)}, u32[]{:S(2)}) collective-permute-start(f32[128,512]{1,0:T(8,128)S(1)} %fusion.10.pre_own_ref), channel_id=1, source_target_pairs={{0,1},{1,0},{2,3},{3,2},{4,5},{5,4},{6,7},{7,6},{8,9},{9,8},{10,11... | collective-permute-start | bytes 786440 | tf_op jit(solution)/shard_map/ppermute | solution.py:238
  60.2 0.7 copy-start.2
  60.9 11.0 %all-to-all-start.3 = ((f32[8,32,128]{2,1,0:T(8,128)}), f32[8,32,128]{2,1,0:T(8,128)S(1)}, u32[]{:S(2)}, u32[]{:S(2)}) async-start(f32[8,32,128]{2,1,0:T(8,128)} %bitcast.8), calls=%async_computation.3 | async-start | bytes 262144 | tf_op jit(solution)/shard_map/all_to_all | solution.py:182
  72.8 13.2 %all-to-all-start.4 = ((bf16[16,48,128]{2,1,0:T(8,128)(2,1)}), bf16[16,48,128]{2,1,0:T(8,128)(2,1)}, u32[]{:S(2)}, u32[]{:S(2)}) async-start(bf16[16,48,128]{2,1,0:T(8,128)(2,1)} %shard_map.96), calls=%async_computation.4 | async-start | bytes 393216 | tf_op jit(solution)/shard_map/all_to_all | solution.py:182
  76.9 12.0 %collective-permute-start.2 = (bf16[256,512]{1,0:T(8,128)(2,1)S(1)}, bf16[256,512]{1,0:T(8,128)(2,1)S(1)}, u32[]{:S(2)}, u32[]{:S(2)}) collective-permute-start(bf16[256,512]{1,0:T(8,128)(2,1)S(1)} %convolution_convert_fusion.1.basis_ref.own_basis_ref), channel_id=1, source_target_pairs={{0,1},{1,0},{2,3},{3,2},{4,5},{5,4},{6,7},{7,6},{8,9},{9,8},{10,11... | collective-permute-start | bytes 786440 | tf_op jit(solution)/shard_map/ppermute | solution.py:208
  89.0 1.6 %copy-start.1 = (bf16[256,4096]{1,0:T(8,128)(2,1)S(1)}, bf16[256,4096]{1,0:T(8,128)(2,1)}, u32[]{:S(2)}) copy-start(bf16[256,4096]{1,0:T(8,128)(2,1)} %own_hidden_ref.1) | copy-start | bytes 6291460
  90.6 0.9 copy-start.3

commit v3 on v2

v3 whole, which is shorter than its diff:
```python
import functools

import jax
import jax.numpy as jnp
from jax import lax
from jax.experimental import pallas as pl
from jax.experimental.pallas import tpu as pltpu
from jax.sharding import PartitionSpec as P

LAST = (((1,), (1,)), ((), ()))
FIRST = (((0,), (0,)), ((), ()))
PLAIN = (((1,), (0,)), ((), ()))
MIB = 1024 * 1024


def activate(values):
    return jax.nn.gelu(values, approximate=True)


def dot(a, b, dims=PLAIN):
    return lax.dot_general(a, b, dims, preferred_element_type=jnp.float32)


def iota(shape, dim):
    return lax.broadcasted_iota(jnp.int32, shape, dim)


def cost(flops, moved):
    return pl.CostEstimate(flops=int(flops), bytes_accessed=int(moved), transcendentals=0)


def whole_call(body, outs, args, flops=1 << 24, moved=1 << 20):
    held = sum(4 * x.size for x in args) + sum(4 * x.size for x in jax.tree.leaves(outs))
    return pl.pallas_call(
        body,
        out_shape=outs,
        in_specs=[pl.BlockSpec(memory_space=pltpu.VMEM)] * len(args),
        out_specs=jax.tree.map(lambda _: pl.BlockSpec(memory_space=pltpu.VMEM), outs),
        compiler_params=pltpu.CompilerParams(vmem_limit_bytes=min(8 * MIB + 2 * held, 60 * MIB)),
        cost_estimate=cost(flops, moved),
    )(*args)


def place_body(old_rows, groups, capacity, decomp_ref, asked_ref, adder_ref):
    k_slots, new_rows = decomp_ref.shape
    slots, places = new_rows * k_slots, groups * capacity
    ids = decomp_ref[...]
    flat = jnp.concatenate([ids[k : k + 1] for k in range(k_slots)], 1)
    usable = flat >= 0
    owners = jnp.where(usable, flat // old_rows, groups)
    local = jnp.where(usable, flat - owners * old_rows, 0)
    hits = jnp.where(owners == iota((groups, slots), 0), 1.0, 0.0)
    earlier = (iota((slots, slots), 0) < iota((slots, slots), 1)).astype(jnp.bfloat16)
    before = dot(hits.astype(jnp.bfloat16), earlier)
    ranking = jnp.sum(before * hits, 0, keepdims=True).astype(jnp.int32)
    place = jnp.where(usable, owners * capacity + ranking, -1)
    taken = place == iota((places, slots), 0)
    asked = jnp.sum(jnp.where(taken, local + 1, 0), 1, keepdims=True) - 1
    asked_ref[...] = jnp.broadcast_to(asked, asked_ref.shape)
    rows = groups * new_rows
    mine = (iota((rows, slots), 1) % new_rows) == (iota((rows, slots), 0) % new_rows)
    adder_ref[...] = dot(
        jnp.where(mine, 1.0, 0.0).astype(jnp.bfloat16),
        jnp.where(taken, 1.0, 0.0).astype(jnp.bfloat16),
        LAST,
    ).astype(jnp.bfloat16)


def fetch_body(look_ref, old_ref, rows_ref):
    places, lanes = look_ref.shape
    old_rows = old_ref.shape[0]
    look = look_ref[...][:, :1]
    select = jnp.where(look == iota((places, old_rows), 1), 1.0, 0.0).astype(jnp.bfloat16)
    rows_ref[...] = dot(select, old_ref[...]).astype(jnp.bfloat16)


def add_body(adder_ref, rows_ref, scale_ref, new_ref):
    new_ref[...] = (dot(adder_ref[...], rows_ref[...]) / scale_ref[...]).astype(jnp.bfloat16)


def pre_body(new_ref, w_ref, pre_ref):
    pre_ref[...] = dot(new_ref[...], w_ref[...])


def share_body(pre_own_ref, pre_other_ref, basis_ref, direct_ref, pre_ref, units_ref, share_ref):
    pre = pre_own_ref[...] + pre_other_ref[...]
    pre_ref[...] = pre
    units = activate(pre).astype(jnp.bfloat16)
    units_ref[...] = units
    share_ref[...] = dot(basis_ref[...], units, LAST) + direct_ref[...]


def softmax_body(shares_ref, targets_ref, packets_ref):
    copies, rows, columns = packets_ref.shape
    tokens = shares_ref.shape[1]
    logits = shares_ref[0]
    for index in range(1, shares_ref.shape[0]):
        logits = logits + shares_ref[index]
    row_top = jnp.max(logits, 1, keepdims=True)
    log_totals = row_top + jnp.log(jnp.sum(jnp.exp(logits - row_top), 1, keepdims=True))
    hits = targets_ref[...] == iota((tokens, columns), 1)
    picked = jnp.sum(jnp.where(hits, logits, 0.0), 1, keepdims=True)
    loss = jnp.sum(log_totals - picked, 0, keepdims=True)
    dlogits = jnp.exp(logits - log_totals) - jnp.where(hits, 1.0, 0.0)
    high = lax.reduce_precision(loss, 8, 7)
    middle = lax.reduce_precision(loss - high, 8, 7)
    low = lax.reduce_precision(loss - high - middle, 8, 7)
    lane = iota((rows - tokens, columns), 1)
    extra = jnp.where(
        lane == 0, high, jnp.where(lane == 1, middle, jnp.where(lane == 2, low, 0.0))
    )
    packet = jnp.concatenate([dlogits, extra], 0).astype(jnp.bfloat16)
    for index in range(copies):
        packets_ref[index] = packet


def copy_body(count, *refs):
    sources, outs, sems = refs[:count], refs[count : 2 * count], refs[2 * count]
    copies = []
    for index, (source, out) in enumerate(zip(sources, outs, strict=True)):
        if source.shape != out.shape:
            wide = out.shape[1]
            offset = pl.multiple_of(lax.axis_index("dp") * wide, wide)
            source = source.at[:, pl.ds(offset, wide)]
        copies.append(pltpu.make_async_copy(source, out, sems.at[index]))
    for copy in copies:
        copy.start()
    for copy in copies:
        copy.wait()


def prefetch(arrays, shapes):
    return pl.pallas_call(
        functools.partial(copy_body, len(arrays)),
        out_shape=tuple(
            pltpu.VMEM(shape, array.dtype) for array, shape in zip(arrays, shapes, strict=True)
        ),
        in_specs=[pl.BlockSpec(memory_space=pl.ANY)] * len(arrays),
        out_specs=tuple(pl.BlockSpec(memory_space=pltpu.VMEM) for _ in arrays),
        scratch_shapes=[pltpu.SemaphoreType.DMA((len(arrays),))],
        compiler_params=pltpu.CompilerParams(vmem_limit_bytes=8 * MIB),
        cost_estimate=cost(0, sum(2 * a.size for a in arrays)),
    )(*arrays)


def final_body(
    own_tokens,
    packets_ref,
    own_dl_ref,
    other_dl_ref,
    units_ref,
    pre_ref,
    own_basis_ref,
    other_basis_ref,
    own_hidden_ref,
    other_hidden_ref,
    new_ref,
    loss_ref,
    grad_in_ref,
    grad_out_ref,
    in_blocks,
    out_blocks,
    sems,
):
    groups, cores, _, columns = packets_ref.shape
    steps = out_blocks.shape[0]
    own = lax.axis_index("dp")
    tokens = groups * own_tokens

    def dlogits(core):
        return jnp.concatenate([packets_ref[g, core, :own_tokens] for g in range(groups)], 0)

    if own_tokens % 16 == 0:
        own_dl, other_dl = dlogits(own), dlogits(1 - own)
    else:
        own_dl, other_dl = own_dl_ref[...], other_dl_ref[...]
    units = units_ref[...]
    own_mixed = dot(own_dl, units).T.astype(jnp.bfloat16)
    other_mixed = dot(other_dl, units).T.astype(jnp.bfloat16)
    copies = []
    wide = out_blocks.shape[2]
    for j in range(steps):
        part = pl.ds(j * wide, wide)
        out_blocks[j] = dot(own_mixed, own_hidden_ref[:, part]) + dot(
            other_mixed, other_hidden_ref[:, part]
        )
        copies.append(
            pltpu.make_async_copy(out_blocks.at[j], grad_out_ref.at[:, part], sems.at[j])
        )
        copies[-1].start()
    grad_units = dot(own_dl, own_basis_ref[...], FIRST) + dot(
        other_dl, other_basis_ref[...], FIRST
    )
    grad_pre = jax.vjp(activate, pre_ref[...])[1](grad_units)[0].astype(jnp.bfloat16)
    high = in_blocks.shape[1]
    for j in range(steps):
        part = pl.ds(j * high, high)
        in_blocks[j] = dot(new_ref[:, part], grad_pre, FIRST)
        copies.append(
            pltpu.make_async_copy(in_blocks.at[j], grad_in_ref.at[part], sems.at[steps + j])
        )
        copies[-1].start()
    loss = jnp.zeros((16, columns), jnp.float32)
    first = own_tokens // 16 * 16
    for g in range(groups):
        for c in range(cores):
            loss = loss + packets_ref[g, c, first : first + 16].astype(jnp.float32)
    loss = jnp.where(iota(loss.shape, 0) == own_tokens - first, loss, 0.0)
    loss = jnp.sum(jnp.sum(loss, 0, keepdims=True), 1, keepdims=True)
    loss_ref[...] = loss / (tokens * cores)
    for copy in copies:
        copy.wait()


def final_call(
    own_tokens, packets, units, pre, own_basis, other_basis, own_hidden, other_hidden, new
):
    steps = 8
    tokens, width = own_hidden.shape
    hidden = pre.shape[1]
    half = new.shape[1]
    vmem = pl.BlockSpec(memory_space=pltpu.VMEM)
    anywhere = pl.BlockSpec(memory_space=pl.ANY)
    if own_tokens % 16 == 0:
        parts = (jnp.zeros((8, 128), jnp.bfloat16),) * 2
    else:
        own = lax.axis_index("dp")
        parts = tuple(
            lax.dynamic_index_in_dim(packets, core, 1, False)[:, :own_tokens].reshape(tokens, -1)
            for core in (own, 1 - own)
        )
    args = (packets, *parts, units, pre, own_basis, other_basis, own_hidden, other_hidden, new)
    return pl.pallas_call(
        functools.partial(final_body, own_tokens),
        out_shape=(
            jax.ShapeDtypeStruct((1, 1), jnp.float32),
            jax.ShapeDtypeStruct((half, hidden), jnp.float32),
            jax.ShapeDtypeStruct((hidden, width), jnp.float32),
        ),
        in_specs=[vmem] * len(args),
        out_specs=(vmem, anywhere, anywhere),
        scratch_shapes=[
            pltpu.VMEM((steps, half // steps, hidden), jnp.float32),
            pltpu.VMEM((steps, hidden, width // steps), jnp.float32),
            pltpu.SemaphoreType.DMA((2 * steps,)),
        ],
        compiler_params=pltpu.CompilerParams(vmem_limit_bytes=40 * MIB),
        cost_estimate=cost(4 * tokens * hidden * width, 4 * (half + width) * hidden),
    )(*args)


def exchange(array, axes="vocab"):
    return lax.all_to_all(array, axes, 0, 0, tiled=True)


def shards(hidden_states, targets, old_embed, decomp, counts, w_in, w_out):
    new_rows, k_slots = decomp.shape
    old_rows, width = old_embed.shape
    groups = lax.axis_size("vocab")
    cores = lax.axis_size("dp")
    own_index = lax.axis_index("vocab")
    dp_index = lax.axis_index("dp")
    tokens = hidden_states.shape[0]
    half_width, hidden = w_in.shape
    columns = groups * new_rows
    capacity = max(2, new_rows * k_slots // groups)
    places = groups * capacity
    swap = [(0, 1), (1, 0)]
    shaped = jax.ShapeDtypeStruct

    asked, adder = whole_call(
        functools.partial(place_body, old_rows, groups, capacity),
        (shaped((places, 128), jnp.int32), shaped((columns, places), jnp.bfloat16)),
        (decomp.T,),
    )
    look = exchange(asked.reshape(groups, capacity, 128))
    hidden_other = lax.ppermute(hidden_states, "dp", swap)
    basis = dot(hidden_states, w_out, LAST).astype(jnp.bfloat16)
    basis_other = lax.ppermute(basis, "dp", swap)
    old_half, w_held, hidden_held = prefetch(
        (old_embed, w_in, hidden_states),
        ((old_rows, half_width), w_in.shape, hidden_states.shape),
    )
    scale = jnp.tile(counts.astype(jnp.float32), groups)[:, None]
    own_tokens = tokens // groups
    own_targets = lax.dynamic_slice_in_dim(targets, own_index * own_tokens, own_tokens)[:, None]
    look, old_half, basis, scale, own_targets = lax.optimization_barrier(
        (look, old_half, basis, scale, own_targets)
    )

    fetched = whole_call(
        fetch_body,
        shaped((places, half_width), jnp.bfloat16),
        (look.reshape(places, 128), old_half),
    )
    arrived = exchange(fetched.reshape(groups, capacity, half_width)).reshape(places, half_width)

    new_copies = whole_call(
        add_body, shaped((columns, half_width), jnp.bfloat16), (adder, arrived, scale)
    )
    new_all = exchange(new_copies.reshape(groups, new_rows, half_width)).reshape(
        columns, half_width
    )
    new_own = new_copies[:new_rows]
    new_other = lax.ppermute(new_own, "dp", swap)
    new_wide = jnp.where(
        dp_index == 0,
        jnp.concatenate([new_own, new_other], 1),
        jnp.concatenate([new_other, new_own], 1),
    )
    direct = lax.dynamic_update_slice(
        jnp.zeros((tokens, columns), jnp.float32),
        dot(hidden_held, new_wide, LAST),
        (0, own_index * new_rows),
    )
    (other_held,) = prefetch((hidden_other,), (hidden_other.shape,))
    new_all, direct, other_held, basis_other = lax.optimization_barrier(
        (new_all, direct, other_held, basis_other)
    )

    pre_own = whole_call(pre_body, shaped((columns, hidden), jnp.float32), (new_all, w_held))
    pre_other = lax.ppermute(pre_own, "dp", swap)
    pre_units, hidden_units, share = whole_call(
        share_body,
        (
            shaped((columns, hidden), jnp.float32),
            shaped((columns, hidden), jnp.bfloat16),
            shaped((tokens, columns), jnp.float32),
        ),
        (pre_own, pre_other, basis, direct),
    )

    shares = exchange(share.reshape(groups, own_tokens, columns))
    packet_rows = (own_tokens + 16) // 16 * 16
    packets = whole_call(
        softmax_body,
        shaped((groups * cores, packet_rows, columns), jnp.bfloat16),
        (shares, own_targets),
    )
    packets = exchange(packets, ("vocab", "dp")).reshape(groups, cores, packet_rows, columns)
    loss_value, grad_in, grad_out = final_call(
        own_tokens,
        packets,
        hidden_units,
        pre_units,
        basis,
        basis_other,
        hidden_held,
        other_held,
        new_all,
    )
    loss_value = loss_value.reshape(1)
    return (loss_value, grad_in, grad_out)


def solution(mesh):
    in_specs = (
        P(("groups", "dp"), None),
        P(("groups", "dp")),
        P("vocab", None),
        P(("groups", "vocab"), None),
        P(("groups", "vocab")),
        P("dp", "vocab"),
        P("vocab", None),
    )
    out_specs = (P("groups"), P(("groups", "dp"), "vocab"), P(("groups", "vocab"), None))
    return jax.shard_map(shards, mesh=mesh, in_specs=in_specs, out_specs=out_specs, check_vma=False)
```

time: 103 us -> 97.6 us (0.948)
  blocking collectives: 18.1 us -> 11.6 us
  matrix products: 11.1 us -> 4.91 us
  local copies, waits for them, and re-layouts: 7.98 us -> 12.9 us
  waiting for transfers between devices: 28.8 us -> 32.5 us
  between operations: 2.58 us -> 0.82 us
  starting transfers between devices: 19.5 us -> 21.2 us
  other arithmetic: 1.38 us -> 0.01 us
    unnamed x13 -> x26, local copies, waits for them, and re-layouts: 4.07 us -> 11 us
    all_to_all x1, blocking collectives: 18.1 us -> 11.6 us  [exchange(): return lax.all_to_all(array, axes, 0, 0, tiled=True)]
    dot_general x5 -> x2, matrix products: 11.1 us -> 4.91 us  [dot(): return lax.dot_general(a, b, dims, preferred_element_type=jnp.float32)]
    all_to_all x4, waiting for transfers between devices: 24.4 us -> 30.3 us  [exchange(): return lax.all_to_all(array, axes, 0, 0, tiled=True)]
    ppermute x1, waiting for transfers between devices: 2.9 us -> 0.74 us  [shards(): new_other = lax.ppermute(new_own, 'dp', swap)]
    all_to_all x4, starting transfers between devices: 18.7 us -> 20.6 us  [exchange(): return lax.all_to_all(array, axes, 0, 0, tiled=True)]
    pallas_call x3 -> x6, Pallas kernels: 3.16 us -> 4.84 us  [whole_call(): pl.pallas_call(body, out_shape=outs, in_specs=[pl.BlockSpec(memory_space=...]
    reduce_sum x1 -> x0, other arithmetic: 1.38 us -> none  [shards(): jnp.sum(packets[:, :, own_tokens, :3].astype(jnp.float32))]
  transfers between devices with their start and end apart: 8 -> 8, of which waited for: 6 -> 5; matrix products, arithmetic and copies ran while one was open for 13% -> 7% of each run, Pallas kernels for 2% -> 5%
where the time goes in v3:
time: 97.6 us; the launch traced here: 96.9 us
  waiting for transfers between devices  32.5 us (33%)
  starting transfers between devices  21.2 us (22%)
  local copies, waits for them, and re-layouts  12.9 us (13%)
  Pallas kernels  12.9 us (13%)
  blocking collectives  11.6 us (12%)
  matrix products  4.91 us (5%)
    all_to_all x4, waiting for transfers between devices, exchange(): return lax.all_to_all(array, axes, 0, 0, tiled=True)  30.3 us
    all_to_all x4, starting transfers between devices, exchange(): return lax.all_to_all(array, axes, 0, 0, tiled=True)  20.6 us
    all_to_all x1, blocking collectives, exchange(): return lax.all_to_all(array, axes, 0, 0, tiled=True)  11.6 us
    unnamed x26, local copies, waits for them, and re-layouts  11 us
    pallas_call x1, Pallas kernels, final_call(): pl.pallas_call(functools.partial(final_body, own_tokens), out_shape=(jax....  5.94 us
    dot_general x2, matrix products, dot(): return lax.dot_general(a, b, dims, preferred_element_type=jnp.float32)  4.91 us
    pallas_call x6, Pallas kernels, whole_call(): pl.pallas_call(body, out_shape=outs, in_specs=[pl.BlockSpec(memory_space=...  4.84 us
    pallas_call x2, Pallas kernels, prefetch(): pl.pallas_call(functools.partial(copy_body, len(arrays)), out_shape=tuple...  2.17 us
  transfers between devices with their start and end apart: 8, of which 5 were waited for; matrix products, arithmetic and copies ran while one was open for 7% of the time, Pallas kernels for 5%

profile of v3, /device:TPU:0, one launch (start us, length us, event | category | flops | bytes accessed | tf_op | source)
XLA Modules:
  0.0 96.9 jit_solution(7923101308449079769)
XLA Ops:
  1.3 1.0 shard_map.94
  2.3 7.3 %all-to-all-start = ((s32[8,16,128]{2,1,0:T(8,128)}), s32[8,16,128]{2,1,0:T(8,128)S(1)}, u32[]{:S(2)}, u32[]{:S(2)}) async-start(s32[8,16,128]{2,1,0:T(8,128)} %bitcast.1), calls=%async_computation | async-start | bytes 131072 | tf_op jit(solution)/shard_map/all_to_all | solution.py:253
  9.6 4.2 %convolution_convert_fusion.basis_ref.own_basis_ref = bf16[256,512]{1,0:T(8,128)(2,1)S(1)} fusion(bf16[256,4096]{1,0:T(8,128)(2,1)} %refs_2_.1, bf16[512,4096]{1,0:T(8,128)(2,1)} %param.13), kind=kOutput, calls=%fused_computation | convolution fusion | flops 1073872896 | bytes 6553600 | tf_op jit(solution)/shard_map/dot_general | solution.py:21
  14.0 1.6 %copy-done.2 = bf16[2048,512]{1,0:T(8,128)(2,1)S(1)} copy-done((bf16[2048,512]{1,0:T(8,128)(2,1)S(1)}, bf16[2048,512]{1,0:T(8,128)(2,1)}, u32[]{:S(2)}) %copy-start.2) | copy-done | bytes 2097176
  15.6 1.6 %copy-done.3 = bf16[256,4096]{1,0:T(8,128)(2,1)S(1)} copy-done((bf16[256,4096]{1,0:T(8,128)(2,1)S(1)}, bf16[256,4096]{1,0:T(8,128)(2,1)}, u32[]{:S(2)}) %copy-start.3) | copy-done | bytes 2097176
  17.6 1.3 %copy-done.4 = bf16[2048,512]{1,0:T(8,128)(2,1)} copy-done((bf16[2048,512]{1,0:T(8,128)(2,1)}, bf16[2048,512]{1,0:T(8,128)(2,1)S(1)}, u32[]{:S(2)}) %copy-start.4) | copy-done | bytes 2097176
  19.0 1.3 %copy-done.8 = bf16[256,4096]{1,0:T(8,128)(2,1)} copy-done((bf16[256,4096]{1,0:T(8,128)(2,1)}, bf16[256,4096]{1,0:T(8,128)(2,1)S(1)}, u32[]{:S(2)}) %copy-start.8) | copy-done | bytes 2097176
  20.4 1.2 %shard_map.96 = bf16[128,2048]{1,0:T(8,128)(2,1)} custom-call(s32[128,128]{1,0:T(8,128)S(1)} %bitcast.18, bf16[256,2048]{1,0:T(8,128)(2,1)S(1)} %get-tuple-element.27.old_ref), custom_call_target="tpu_custom_call" | custom-call | flops 16777216 | bytes 1048576 | tf_op jit(solution)/shard_map/pallas_call | solution.py:34
  21.5 6.1 %all-to-all-start.1 = ((bf16[8,16,2048]{2,1,0:T(8,128)(2,1)}), bf16[8,16,2048]{2,1,0:T(8,128)(2,1)S(1)}, u32[]{:S(2)}, u32[]{:S(2)}) async-start(bf16[8,16,2048]{2,1,0:T(8,128)(2,1)} %bitcast.4), calls=%async_computation.1 | async-start | bytes 1048576 | tf_op jit(solution)/shard_map/all_to_all | solution.py:253
  27.7 14.9 %all-to-all-done.1 = bf16[8,16,2048]{2,1,0:T(8,128)(2,1)S(1)} async-done(((bf16[8,16,2048]{2,1,0:T(8,128)(2,1)}), bf16[8,16,2048]{2,1,0:T(8,128)(2,1)S(1)}, u32[]{:S(2)}, u32[]{:S(2)}) %all-to-all-start.1) | async-done | bytes 524320 | tf_op jit(solution)/shard_map/all_to_all | solution.py:253
  42.6 1.1 %shard_map.97 = bf16[128,2048]{1,0:T(8,128)(2,1)} custom-call(bf16[128,128]{1,0:T(8,128)(2,1)S(1)} %get-tuple-element.23.adder_ref, bf16[128,2048]{1,0:T(8,128)(2,1)S(1)} %bitcast.15, f32[128,1]{1,0:T(8,128)S(1)} %copy.10.scale_ref), custom_call_target="tpu_custom_call" | custom-call | flops 16777216 | bytes 1048576 | tf_op jit(solution)/shard_map/pallas_call | solution.py:34
  43.7 3.6 %all-to-all-start.2 = ((bf16[8,16,2048]{2,1,0:T(8,128)(2,1)}), bf16[8,16,2048]{2,1,0:T(8,128)(2,1)S(1)}, u32[]{:S(2)}, u32[]{:S(2)}) async-start(bf16[8,16,2048]{2,1,0:T(8,128)(2,1)} %bitcast.6), calls=%async_computation.2 | async-start | bytes 1048576 | tf_op jit(solution)/shard_map/all_to_all | solution.py:253
  47.3 0.8 slice.4
  50.8 1.7 %shard_map.98.other_hidden_ref = bf16[256,4096]{1,0:T(8,128)(2,1)S(1)} custom-call(bf16[256,4096]{1,0:T(8,128)(2,1)} %collective-permute-done.1.refs_0_), custom_call_target="tpu_custom_call" | custom-call | bytes 2097152 | tf_op jit(solution)/shard_map/pallas_call | solution.py:133
  52.5 1.3 %copy-done.6 = bf16[256,4096]{1,0:T(8,128)(2,1)} copy-done((bf16[256,4096]{1,0:T(8,128)(2,1)}, bf16[256,4096]{1,0:T(8,128)(2,1)S(1)}, u32[]{:S(2)}) %copy-start.6) | copy-done | bytes 2097176
  53.9 8.1 %all-to-all-done.2 = bf16[8,16,2048]{2,1,0:T(8,128)(2,1)S(1)} async-done(((bf16[8,16,2048]{2,1,0:T(8,128)(2,1)}), bf16[8,16,2048]{2,1,0:T(8,128)(2,1)S(1)}, u32[]{:S(2)}, u32[]{:S(2)}) %all-to-all-start.2) | async-done | bytes 524320 | tf_op jit(solution)/shard_map/all_to_all | solution.py:253
  62.5 1.5 %collective-permute-done.3.pre_other_ref = f32[128,512]{1,0:T(8,128)S(1)} collective-permute-done((f32[128,512]{1,0:T(8,128)S(1)}, f32[128,512]{1,0:T(8,128)S(1)}, u32[]{:S(2)}, u32[]{:S(2)}) %collective-permute-start.3) | collective-permute-done | bytes 262176 | tf_op jit(solution)/shard_map/ppermute | solution.py:322
  64.1 1.0 shard_map.100
  65.0 3.6 %all-to-all-start.3 = ((f32[8,32,128]{2,1,0:T(8,128)}), f32[8,32,128]{2,1,0:T(8,128)S(1)}, u32[]{:S(2)}, u32[]{:S(2)}) async-start(f32[8,32,128]{2,1,0:T(8,128)} %bitcast.8), calls=%async_computation.3 | async-start | bytes 262144 | tf_op jit(solution)/shard_map/all_to_all | solution.py:253
  68.7 7.3 %all-to-all-done.3.shares_ref = f32[8,32,128]{2,1,0:T(8,128)S(1)} async-done(((f32[8,32,128]{2,1,0:T(8,128)}), f32[8,32,128]{2,1,0:T(8,128)S(1)}, u32[]{:S(2)}, u32[]{:S(2)}) %all-to-all-start.3) | async-done | bytes 131104 | tf_op jit(solution)/shard_map/all_to_all | solution.py:253
  76.2 11.6 %all_to_all.25 = bf16[16,48,128]{2,1,0:T(8,128)(2,1)S(1)} all-to-all(bf16[16,48,128]{2,1,0:T(8,128)(2,1)S(1)} %shard_map.101), channel_id=1, replica_groups=mesh['groups'=2,'vocab'=8,'dp'=2] {'vocab','dp'}, dimensions={0} | all-to-all | bytes 393216 | tf_op jit(solution)/shard_map/all_to_all | solution.py:253
  87.8 1.6 %copy-done.7 = bf16[256,4096]{1,0:T(8,128)(2,1)S(1)} copy-done((bf16[256,4096]{1,0:T(8,128)(2,1)S(1)}, bf16[256,4096]{1,0:T(8,128)(2,1)}, u32[]{:S(2)}) %copy-start.7) | copy-done | bytes 2097176
  89.4 1.6 %copy-done.10 = bf16[256,4096]{1,0:T(8,128)(2,1)S(1)} copy-done((bf16[256,4096]{1,0:T(8,128)(2,1)S(1)}, bf16[256,4096]{1,0:T(8,128)(2,1)}, u32[]{:S(2)}) %copy-start.10) | copy-done | bytes 2097176
  91.0 5.9 %shard_map.102 = (f32[1,1]{1,0:T(1,128)}, f32[2048,512]{1,0:T(8,128)}, f32[512,4096]{1,0:T(8,128)}) custom-call(bf16[8,2,48,128]{3,2,1,0:T(8,128)(2,1)S(1)} %bitcast.19, bf16[8,128]{1,0:T(8,128)(2,1)S(1)} %broadcast_in_dim.11.own_dl_ref.other_dl_ref, bf16[8,128]{1,0:T(8,128)(2,1)S(1)} %broadcast_in_dim.11.own_dl_ref.other_dl_ref, ...), custom_call_target="tpu_custom_call" | custom-call | flops 2147483648 | bytes 12582912 | tf_op jit(solution)/shard_map/pallas_call | solution.py:233
  (40 shorter events, 4.9 us)
Async XLA Ops:
  0.6 19.6 %copy-start = (s32[256]{0:T(256)S(1)}, s32[256]{0:T(256)}, u32[]{:S(2)}) copy-start(s32[256]{0:T(256)} %param.8) | copy-start | bytes 3076
  0.6 0.7 copy-start.11
  2.3 18.1 %all-to-all-start = ((s32[8,16,128]{2,1,0:T(8,128)}), s32[8,16,128]{2,1,0:T(8,128)S(1)}, u32[]{:S(2)}, u32[]{:S(2)}) async-start(s32[8,16,128]{2,1,0:T(8,128)} %bitcast.1), calls=%async_computation | async-start | bytes 131072 | tf_op jit(solution)/shard_map/all_to_all | solution.py:253
  9.5 4.4 %copy-start.12 = (s32[16]{0:T(128)S(1)}, s32[16]{0:T(128)}, u32[]{:S(2)}) copy-start(s32[16]{0:T(128)} %param.11) | copy-start | bytes 196
  9.6 4.5 %copy-start.1 = (bf16[256,4096]{1,0:T(8,128)(2,1)S(1)}, bf16[256,4096]{1,0:T(8,128)(2,1)}, u32[]{:S(2)}) copy-start(bf16[256,4096]{1,0:T(8,128)(2,1)} %refs_0_.1) | copy-start | bytes 6291460
  9.6 41.2 %collective-permute-start.1 = (bf16[256,4096]{1,0:T(8,128)(2,1)}, bf16[256,4096]{1,0:T(8,128)(2,1)}, u32[]{:S(2)}, u32[]{:S(2)}) collective-permute-start(bf16[256,4096]{1,0:T(8,128)(2,1)} %refs_2_.1), channel_id=1, source_target_pairs={{0,1},{1,0},{2,3},{3,2},{4,5},{5,4},{6,7},{7,6},{8,9},{9,8},{10,11... | collective-permute-start | bytes 6291464 | tf_op jit(solution)/shard_map/ppermute | solution.py:277
  14.0 1.6 %copy-start.2 = (bf16[2048,512]{1,0:T(8,128)(2,1)S(1)}, bf16[2048,512]{1,0:T(8,128)(2,1)}, u32[]{:S(2)}) copy-start(bf16[2048,512]{1,0:T(8,128)(2,1)} %refs_1_.1) | copy-start | bytes 6291460
  15.6 1.6 %copy-start.3 = (bf16[256,4096]{1,0:T(8,128)(2,1)S(1)}, bf16[256,4096]{1,0:T(8,128)(2,1)}, u32[]{:S(2)}) copy-start(bf16[256,4096]{1,0:T(8,128)(2,1)} %refs_2_.1) | copy-start | bytes 6291460
  17.6 1.3 %copy-start.4 = (bf16[2048,512]{1,0:T(8,128)(2,1)}, bf16[2048,512]{1,0:T(8,128)(2,1)S(1)}, u32[]{:S(2)}) copy-start(bf16[2048,512]{1,0:T(8,128)(2,1)S(1)} %get-tuple-element.31.w_ref) | copy-start | bytes 6291460
  19.0 1.3 %copy-start.8 = (bf16[256,4096]{1,0:T(8,128)(2,1)}, bf16[256,4096]{1,0:T(8,128)(2,1)S(1)}, u32[]{:S(2)}) copy-start(bf16[256,4096]{1,0:T(8,128)(2,1)S(1)} %get-tuple-element.29.own_hidden_ref) | copy-start | bytes 6291460
  21.5 27.9 %copy-start.9 = (bf16[256,4096]{1,0:T(8,128)(2,1)S(1)}, bf16[256,4096]{1,0:T(8,128)(2,1)}, u32[]{:S(2)}) copy-start(bf16[256,4096]{1,0:T(8,128)(2,1)} %copy-done.8) | copy-start | bytes 6291460
  21.5 21.1 %all-to-all-start.1 = ((bf16[8,16,2048]{2,1,0:T(8,128)(2,1)}), bf16[8,16,2048]{2,1,0:T(8,128)(2,1)S(1)}, u32[]{:S(2)}, u32[]{:S(2)}) async-start(bf16[8,16,2048]{2,1,0:T(8,128)(2,1)} %bitcast.4), calls=%async_computation.1 | async-start | bytes 1048576 | tf_op jit(solution)/shard_map/all_to_all | solution.py:253
  43.7 18.3 %all-to-all-start.2 = ((bf16[8,16,2048]{2,1,0:T(8,128)(2,1)}), bf16[8,16,2048]{2,1,0:T(8,128)(2,1)S(1)}, u32[]{:S(2)}, u32[]{:S(2)}) async-start(bf16[8,16,2048]{2,1,0:T(8,128)(2,1)} %bitcast.6), calls=%async_computation.2 | async-start | bytes 1048576 | tf_op jit(solution)/shard_map/all_to_all | solution.py:253
  48.2 1.3 %collective-permute-start = (bf16[16,2048]{1,0:T(8,128)(2,1)S(1)}, bf16[16,2048]{1,0:T(8,128)(2,1)S(1)}, u32[]{:S(2)}, u32[]{:S(2)}) collective-permute-start(bf16[16,2048]{1,0:T(8,128)(2,1)S(1)} %slice.4), channel_id=1, source_target_pairs={{0,1},{1,0},{2,3},{3,2},{4,5},{5,4},{6,7},{7,6},{8,9},{9,8},{10,11... | collective-permute-start | bytes 196616 | tf_op jit(solution)/shard_map/ppermute | solution.py:305
  48.2 5.7 %collective-permute-start.2 = (bf16[256,512]{1,0:T(8,128)(2,1)S(1)}, bf16[256,512]{1,0:T(8,128)(2,1)S(1)}, u32[]{:S(2)}, u32[]{:S(2)}) collective-permute-start(bf16[256,512]{1,0:T(8,128)(2,1)S(1)} %convolution_convert_fusion.basis_ref.own_basis_ref), channel_id=1, source_target_pairs={{0,1},{1,0},{2,3},{3,2},{4,5},{5,4},{6,7},{7,6},{8,9},{9,8},{10,11... | collective-permute-start | bytes 786440 | tf_op jit(solution)/shard_map/ppermute | solution.py:279
  50.8 11.2 %copy-start.5 = (bf16[2048,512]{1,0:T(8,128)(2,1)S(1)}, bf16[2048,512]{1,0:T(8,128)(2,1)}, u32[]{:S(2)}) copy-start(bf16[2048,512]{1,0:T(8,128)(2,1)} %copy-done.4) | copy-start | bytes 6291460
  52.5 1.3 %copy-start.6 = (bf16[256,4096]{1,0:T(8,128)(2,1)}, bf16[256,4096]{1,0:T(8,128)(2,1)S(1)}, u32[]{:S(2)}) copy-start(bf16[256,4096]{1,0:T(8,128)(2,1)S(1)} %shard_map.98.other_hidden_ref) | copy-start | bytes 6291460
  62.5 1.6 %collective-permute-start.3 = (f32[128,512]{1,0:T(8,128)S(1)}, f32[128,512]{1,0:T(8,128)S(1)}, u32[]{:S(2)}, u32[]{:S(2)}) collective-permute-start(f32[128,512]{1,0:T(8,128)S(1)} %shard_map.99.pre_own_ref), channel_id=1, source_target_pairs={{0,1},{1,0},{2,3},{3,2},{4,5},{5,4},{6,7},{7,6},{8,9},{9,8},{10,11... | collective-permute-start | bytes 786440 | tf_op jit(solution)/shard_map/ppermute | solution.py:322
  65.0 11.0 %all-to-all-start.3 = ((f32[8,32,128]{2,1,0:T(8,128)}), f32[8,32,128]{2,1,0:T(8,128)S(1)}, u32[]{:S(2)}, u32[]{:S(2)}) async-start(f32[8,32,128]{2,1,0:T(8,128)} %bitcast.8), calls=%async_computation.3 | async-start | bytes 262144 | tf_op jit(solution)/shard_map/all_to_all | solution.py:253
  87.8 1.6 %copy-start.7 = (bf16[256,4096]{1,0:T(8,128)(2,1)S(1)}, bf16[256,4096]{1,0:T(8,128)(2,1)}, u32[]{:S(2)}) copy-start(bf16[256,4096]{1,0:T(8,128)(2,1)} %copy-done.6) | copy-start | bytes 6291460
  89.4 1.6 %copy-start.10 = (bf16[256,4096]{1,0:T(8,128)(2,1)S(1)}, bf16[256,4096]{1,0:T(8,128)(2,1)}, u32[]{:S(2)}) copy-start(bf16[256,4096]{1,0:T(8,128)(2,1)} %copy-done.8) | copy-start | bytes 6291460

commit v4 on v3

--- a/solution.py
+++ b/solution.py
@@ -114,35 +114,6 @@
         packets_ref[index] = packet
 
 
-def copy_body(count, *refs):
-    sources, outs, sems = refs[:count], refs[count : 2 * count], refs[2 * count]
-    copies = []
-    for index, (source, out) in enumerate(zip(sources, outs, strict=True)):
-        if source.shape != out.shape:
-            wide = out.shape[1]
-            offset = pl.multiple_of(lax.axis_index("dp") * wide, wide)
-            source = source.at[:, pl.ds(offset, wide)]
-        copies.append(pltpu.make_async_copy(source, out, sems.at[index]))
-    for copy in copies:
-        copy.start()
-    for copy in copies:
-        copy.wait()
-
-
-def prefetch(arrays, shapes):
-    return pl.pallas_call(
-        functools.partial(copy_body, len(arrays)),
-        out_shape=tuple(
-            pltpu.VMEM(shape, array.dtype) for array, shape in zip(arrays, shapes, strict=True)
-        ),
-        in_specs=[pl.BlockSpec(memory_space=pl.ANY)] * len(arrays),
-        out_specs=tuple(pl.BlockSpec(memory_space=pltpu.VMEM) for _ in arrays),
-        scratch_shapes=[pltpu.SemaphoreType.DMA((len(arrays),))],
-        compiler_params=pltpu.CompilerParams(vmem_limit_bytes=8 * MIB),
-        cost_estimate=cost(0, sum(2 * a.size for a in arrays)),
-    )(*arrays)
-
-
 def final_body(
     own_tokens,
     packets_ref,
@@ -152,12 +123,13 @@
     pre_ref,
     own_basis_ref,
     other_basis_ref,
+    new_ref,
     own_hidden_ref,
     other_hidden_ref,
-    new_ref,
     loss_ref,
     grad_in_ref,
     grad_out_ref,
+    hidden_blocks,
     in_blocks,
     out_blocks,
     sems,
@@ -166,6 +138,21 @@
     steps = out_blocks.shape[0]
     own = lax.axis_index("dp")
     tokens = groups * own_tokens
+    wide = out_blocks.shape[2]
+    high = in_blocks.shape[1]
+
+    arriving = []
+    for j in range(steps):
+        part = pl.ds(j * wide, wide)
+        for core, source in enumerate((own_hidden_ref, other_hidden_ref)):
+            arriving.append(
+                pltpu.make_async_copy(
+                    source.at[:, part],
+                    hidden_blocks.at[j, pl.ds(core * tokens, tokens)],
+                    sems.at[2 * steps + 2 * j + core],
+                )
+            )
+            arriving[-1].start()
 
     def dlogits(core):
         return jnp.concatenate([packets_ref[g, core, :own_tokens] for g in range(groups)], 0)
@@ -174,32 +161,34 @@
         own_dl, other_dl = dlogits(own), dlogits(1 - own)
     else:
         own_dl, other_dl = own_dl_ref[...], other_dl_ref[...]
-    units = units_ref[...]
-    own_mixed = dot(own_dl, units).T.astype(jnp.bfloat16)
-    other_mixed = dot(other_dl, units).T.astype(jnp.bfloat16)
-    copies = []
-    wide = out_blocks.shape[2]
-    for j in range(steps):
-        part = pl.ds(j * wide, wide)
-        out_blocks[j] = dot(own_mixed, own_hidden_ref[:, part]) + dot(
-            other_mixed, other_hidden_ref[:, part]
-        )
-        copies.append(
-            pltpu.make_async_copy(out_blocks.at[j], grad_out_ref.at[:, part], sems.at[j])
-        )
-        copies[-1].start()
+    leaving = []
+
     grad_units = dot(own_dl, own_basis_ref[...], FIRST) + dot(
         other_dl, other_basis_ref[...], FIRST
     )
     grad_pre = jax.vjp(activate, pre_ref[...])[1](grad_units)[0].astype(jnp.bfloat16)
-    high = in_blocks.shape[1]
     for j in range(steps):
         part = pl.ds(j * high, high)
         in_blocks[j] = dot(new_ref[:, part], grad_pre, FIRST)
-        copies.append(
+        leaving.append(
             pltpu.make_async_copy(in_blocks.at[j], grad_in_ref.at[part], sems.at[steps + j])
         )
-        copies[-1].start()
+        leaving[-1].start()
+
+    units_t = units_ref[...].T
+    mixed = jnp.concatenate(
+        [dot(units_t, dl, LAST).astype(jnp.bfloat16) for dl in (own_dl, other_dl)], 1
+    )
+    for j in range(steps):
+        part = pl.ds(j * wide, wide)
+        arriving[2 * j].wait()
+        arriving[2 * j + 1].wait()
+        out_blocks[j] = dot(mixed, hidden_blocks[j])
+        leaving.append(
+            pltpu.make_async_copy(out_blocks.at[j], grad_out_ref.at[:, part], sems.at[j])
+        )
+        leaving[-1].start()
+
     loss = jnp.zeros((16, columns), jnp.float32)
     first = own_tokens // 16 * 16
     for g in range(groups):
@@ -208,7 +197,7 @@
     loss = jnp.where(iota(loss.shape, 0) == own_tokens - first, loss, 0.0)
     loss = jnp.sum(jnp.sum(loss, 0, keepdims=True), 1, keepdims=True)
     loss_ref[...] = loss / (tokens * cores)
-    for copy in copies:
+    for copy in leaving:
         copy.wait()
 
 
@@ -220,7 +209,7 @@
     hidden = pre.shape[1]
     half = new.shape[1]
     vmem = pl.BlockSpec(memory_space=pltpu.VMEM)
-    anywhere = pl.BlockSpec(memory_space=pl.ANY)
+    hbm = pl.BlockSpec(memory_space=pltpu.HBM)
     if own_tokens % 16 == 0:
         parts = (jnp.zeros((8, 128), jnp.bfloat16),) * 2
     else:
@@ -229,7 +218,7 @@
             lax.dynamic_index_in_dim(packets, core, 1, False)[:, :own_tokens].reshape(tokens, -1)
             for core in (own, 1 - own)
         )
-    args = (packets, *parts, units, pre, own_basis, other_basis, own_hidden, other_hidden, new)
+    args = (packets, *parts, units, pre, own_basis, other_basis, new)
     return pl.pallas_call(
         functools.partial(final_body, own_tokens),
         out_shape=(
@@ -237,16 +226,17 @@
             jax.ShapeDtypeStruct((half, hidden), jnp.float32),
             jax.ShapeDtypeStruct((hidden, width), jnp.float32),
         ),
-        in_specs=[vmem] * len(args),
-        out_specs=(vmem, anywhere, anywhere),
+        in_specs=[vmem] * len(args) + [hbm] * 2,
+        out_specs=(vmem, hbm, hbm),
         scratch_shapes=[
+            pltpu.VMEM((steps, 2 * tokens, width // steps), jnp.bfloat16),
             pltpu.VMEM((steps, half // steps, hidden), jnp.float32),
             pltpu.VMEM((steps, hidden, width // steps), jnp.float32),
-            pltpu.SemaphoreType.DMA((2 * steps,)),
+            pltpu.SemaphoreType.DMA((4 * steps,)),
         ],
-        compiler_params=pltpu.CompilerParams(vmem_limit_bytes=40 * MIB),
+        compiler_params=pltpu.CompilerParams(vmem_limit_bytes=44 * MIB),
         cost_estimate=cost(4 * tokens * hidden * width, 4 * (half + width) * hidden),
-    )(*args)
+    )(*args, own_hidden, other_hidden)
 
 
 def exchange(array, axes="vocab"):
@@ -277,10 +267,7 @@
     hidden_other = lax.ppermute(hidden_states, "dp", swap)
     basis = dot(hidden_states, w_out, LAST).astype(jnp.bfloat16)
     basis_other = lax.ppermute(basis, "dp", swap)
-    old_half, w_held, hidden_held = prefetch(
-        (old_embed, w_in, hidden_states),
-        ((old_rows, half_width), w_in.shape, hidden_states.shape),
-    )
+    old_half = lax.dynamic_slice_in_dim(old_embed, dp_index * half_width, half_width, 1)
     scale = jnp.tile(counts.astype(jnp.float32), groups)[:, None]
     own_tokens = tokens // groups
     own_targets = lax.dynamic_slice_in_dim(targets, own_index * own_tokens, own_tokens)[:, None]
@@ -310,15 +297,14 @@
     )
     direct = lax.dynamic_update_slice(
         jnp.zeros((tokens, columns), jnp.float32),
-        dot(hidden_held, new_wide, LAST),
+        dot(hidden_states, new_wide, LAST),
         (0, own_index * new_rows),
     )
-    (other_held,) = prefetch((hidden_other,), (hidden_other.shape,))
-    new_all, direct, other_held, basis_other = lax.optimization_barrier(
-        (new_all, direct, other_held, basis_other)
-    )
-
-    pre_own = whole_call(pre_body, shaped((columns, hidden), jnp.float32), (new_all, w_held))
+    new_all, direct, hidden_other, basis_other = lax.optimization_barrier(
+        (new_all, direct, hidden_other, basis_other)
+    )
+
+    pre_own = whole_call(pre_body, shaped((columns, hidden), jnp.float32), (new_all, w_in))
     pre_other = lax.ppermute(pre_own, "dp", swap)
     pre_units, hidden_units, share = whole_call(
         share_body,
@@ -345,8 +331,8 @@
         pre_units,
         basis,
         basis_other,
-        hidden_held,
-        other_held,
+        hidden_states,
+        hidden_other,
         new_all,
     )
     loss_value = loss_value.reshape(1)

time: 97.6 us -> 94.8 us (0.971)
  local copies, waits for them, and re-layouts: 12.9 us -> 10 us
  waiting for transfers between devices: 32.5 us -> 35 us
  Pallas kernels: 12.9 us -> 10.6 us
  starting transfers between devices: 21.2 us -> 19.7 us
  matrix products: 4.91 us -> 6.37 us
    unnamed x26 -> x18, local copies, waits for them, and re-layouts: 11 us -> 6.91 us
    all_to_all x4, waiting for transfers between devices: 30.3 us -> 32.8 us  [exchange(): return lax.all_to_all(array, axes, 0, 0, tiled=True)]
    pallas_call x2 -> x0, Pallas kernels: 2.17 us -> none  [prefetch(): pl.pallas_call(functools.partial(copy_body, len(arrays)), out_shape=tuple...]
    all_to_all x4, starting transfers between devices: 20.6 us -> 19.1 us  [exchange(): return lax.all_to_all(array, axes, 0, 0, tiled=True)]
    dot_general x2, matrix products: 4.91 us -> 6.37 us  [dot(): return lax.dot_general(a, b, dims, preferred_element_type=jnp.float32)]
  transfers between devices with their start and end apart: 8 -> 8, of which waited for: 5 -> 6; matrix products, arithmetic and copies ran while one was open for 7% -> 10% of each run, Pallas kernels for 5% -> 2%
where the time goes in v4:
time: 94.8 us; the launch traced here: 94.1 us
  waiting for transfers between devices  35 us (37%)
  starting transfers between devices  19.7 us (21%)
  blocking collectives  11.6 us (12%)
  Pallas kernels  10.6 us (11%)
  local copies, waits for them, and re-layouts  10 us (11%)
  matrix products  6.37 us (7%)
    all_to_all x4, waiting for transfers between devices, exchange(): return lax.all_to_all(array, axes, 0, 0, tiled=True)  32.8 us
    all_to_all x4, starting transfers between devices, exchange(): return lax.all_to_all(array, axes, 0, 0, tiled=True)  19.1 us
    all_to_all x1, blocking collectives, exchange(): return lax.all_to_all(array, axes, 0, 0, tiled=True)  11.6 us
    unnamed x18, local copies, waits for them, and re-layouts  6.91 us
    pallas_call x1, Pallas kernels, final_call(): pl.pallas_call(functools.partial(final_body, own_tokens), out_shape=(jax....  6.62 us
    dot_general x2, matrix products, dot(): return lax.dot_general(a, b, dims, preferred_element_type=jnp.float32)  6.37 us
    pallas_call x6, Pallas kernels, whole_call(): pl.pallas_call(body, out_shape=outs, in_specs=[pl.BlockSpec(memory_space=...  4 us
  transfers between devices with their start and end apart: 8, of which 6 were waited for; matrix products, arithmetic and copies ran while one was open for 10% of the time, Pallas kernels for 2%

profile of v4, /device:TPU:0, one launch (start us, length us, event | category | flops | bytes accessed | tf_op | source)
XLA Modules:
  0.0 94.1 jit_solution(451989038504179838)
XLA Ops:
  0.7 0.8 copy-done.6
  1.5 1.0 %shard_map.94 = (s32[128,128]{1,0:T(8,128)}, bf16[128,128]{1,0:T(8,128)(2,1)S(1)}) custom-call(s32[8,16]{1,0:T(8,128)S(1)} %bitcast.23), custom_call_target="tpu_custom_call" | custom-call | flops 16777216 | bytes 1048576 | tf_op jit(solution)/shard_map/pallas_call | solution.py:34
  2.4 7.3 %all-to-all-start = ((s32[8,16,128]{2,1,0:T(8,128)}), s32[8,16,128]{2,1,0:T(8,128)S(1)}, u32[]{:S(2)}, u32[]{:S(2)}) async-start(s32[8,16,128]{2,1,0:T(8,128)} %bitcast.1), calls=%async_computation | async-start | bytes 131072 | tf_op jit(solution)/shard_map/all_to_all | solution.py:243
  9.7 4.1 %convolution_convert_fusion.basis_ref.own_basis_ref = bf16[256,512]{1,0:T(8,128)(2,1)S(1)} fusion(bf16[256,4096]{1,0:T(8,128)(2,1)} %own_hidden_ref.1, bf16[512,4096]{1,0:T(8,128)(2,1)} %param.13), kind=kOutput, calls=%fused_computation | convolution fusion | flops 1073872896 | bytes 6553600 | tf_op jit(solution)/shard_map/dot_general | solution.py:21
  15.2 1.4 %all-to-all-done = s32[8,16,128]{2,1,0:T(8,128)S(1)} async-done(((s32[8,16,128]{2,1,0:T(8,128)}), s32[8,16,128]{2,1,0:T(8,128)S(1)}, u32[]{:S(2)}, u32[]{:S(2)}) %all-to-all-start) | async-done | bytes 65568 | tf_op jit(solution)/shard_map/all_to_all | solution.py:243
  17.0 0.8 copy-done.1
  17.7 4.6 %all-to-all-start.1 = ((bf16[8,16,2048]{2,1,0:T(8,128)(2,1)}), bf16[8,16,2048]{2,1,0:T(8,128)(2,1)S(1)}, u32[]{:S(2)}, u32[]{:S(2)}) async-start(bf16[8,16,2048]{2,1,0:T(8,128)(2,1)} %bitcast.17), calls=%async_computation.1 | async-start | bytes 1048576 | tf_op jit(solution)/shard_map/all_to_all | solution.py:243
  22.4 15.0 %all-to-all-done.1 = bf16[8,16,2048]{2,1,0:T(8,128)(2,1)S(1)} async-done(((bf16[8,16,2048]{2,1,0:T(8,128)(2,1)}), bf16[8,16,2048]{2,1,0:T(8,128)(2,1)S(1)}, u32[]{:S(2)}, u32[]{:S(2)}) %all-to-all-start.1) | async-done | bytes 524320 | tf_op jit(solution)/shard_map/all_to_all | solution.py:243
  37.5 1.1 %shard_map.96 = bf16[128,2048]{1,0:T(8,128)(2,1)} custom-call(bf16[128,128]{1,0:T(8,128)(2,1)S(1)} %get-tuple-element.20.adder_ref, bf16[128,2048]{1,0:T(8,128)(2,1)S(1)} %bitcast.18, f32[128,1]{1,0:T(8,128)S(1)} %copy.10.scale_ref), custom_call_target="tpu_custom_call" | custom-call | flops 16777216 | bytes 1048576 | tf_op jit(solution)/shard_map/pallas_call | solution.py:34
  38.5 3.6 %all-to-all-start.2 = ((bf16[8,16,2048]{2,1,0:T(8,128)(2,1)}), bf16[8,16,2048]{2,1,0:T(8,128)(2,1)S(1)}, u32[]{:S(2)}, u32[]{:S(2)}) async-start(bf16[8,16,2048]{2,1,0:T(8,128)(2,1)} %bitcast.6), calls=%async_computation.2 | async-start | bytes 1048576 | tf_op jit(solution)/shard_map/all_to_all | solution.py:243
  42.2 0.8 slice.4
  43.5 0.7 collective-permute-done
  44.3 2.3 %convolution_bitcast_fusion = f32[256,16]{1,0:T(8,128)S(1)} fusion(bf16[256,4096]{1,0:T(8,128)(2,1)} %own_hidden_ref.1, bf16[16,2048]{1,0:T(8,128)(2,1)S(1)} %collective-permute-done, bf16[16,2048]{1,0:T(8,128)(2,1)S(1)} %slice.4, pred[]{:T(512)S(6)} %eq.3), kind=kOutput, calls=%fused_computation.1 | convolution fusion | flops 34144256 | bytes 2244609 | tf_op jit(solution)/shard_map/dot_general | solution.py:21
  47.2 9.7 %all-to-all-done.2 = bf16[8,16,2048]{2,1,0:T(8,128)(2,1)S(1)} async-done(((bf16[8,16,2048]{2,1,0:T(8,128)(2,1)}), bf16[8,16,2048]{2,1,0:T(8,128)(2,1)S(1)}, u32[]{:S(2)}, u32[]{:S(2)}) %all-to-all-start.2) | async-done | bytes 524320 | tf_op jit(solution)/shard_map/all_to_all | solution.py:243
  56.9 1.6 %copy-done.2 = bf16[2048,512]{1,0:T(8,128)(2,1)S(1)} copy-done((bf16[2048,512]{1,0:T(8,128)(2,1)S(1)}, bf16[2048,512]{1,0:T(8,128)(2,1)}, u32[]{:S(2)}) %copy-start.2) | copy-done | bytes 2097176
  59.0 1.5 %collective-permute-done.3.pre_other_ref = f32[128,512]{1,0:T(8,128)S(1)} collective-permute-done((f32[128,512]{1,0:T(8,128)S(1)}, f32[128,512]{1,0:T(8,128)S(1)}, u32[]{:S(2)}, u32[]{:S(2)}) %collective-permute-start.3) | collective-permute-done | bytes 262176 | tf_op jit(solution)/shard_map/ppermute | solution.py:308
  60.5 1.0 %shard_map.98 = (f32[128,512]{1,0:T(8,128)S(1)}, bf16[128,512]{1,0:T(8,128)(2,1)S(1)}, f32[256,128]{1,0:T(8,128)}) custom-call(f32[128,512]{1,0:T(8,128)S(1)} %shard_map.97.pre_own_ref, f32[128,512]{1,0:T(8,128)S(1)} %collective-permute-done.3.pre_other_ref, bf16[256,512]{1,0:T(8,128)(2,1)S(1)} %convolution_convert_fusion.basis_ref.own_basis_ref, ...), custom_call_target="tpu_custom_call" | custom-call | flops 16777216 | bytes 1048576 | tf_op jit(solution)/shard_map/pallas_call | solution.py:34
  62.1 3.6 %all-to-all-start.3 = ((f32[8,32,128]{2,1,0:T(8,128)}), f32[8,32,128]{2,1,0:T(8,128)S(1)}, u32[]{:S(2)}, u32[]{:S(2)}) async-start(f32[8,32,128]{2,1,0:T(8,128)} %bitcast.9), calls=%async_computation.3 | async-start | bytes 262144 | tf_op jit(solution)/shard_map/all_to_all | solution.py:243
  65.8 0.7 copy.12.targets_ref
  66.5 6.6 %all-to-all-done.3.shares_ref = f32[8,32,128]{2,1,0:T(8,128)S(1)} async-done(((f32[8,32,128]{2,1,0:T(8,128)}), f32[8,32,128]{2,1,0:T(8,128)S(1)}, u32[]{:S(2)}, u32[]{:S(2)}) %all-to-all-start.3) | async-done | bytes 131104 | tf_op jit(solution)/shard_map/all_to_all | solution.py:243
  73.3 11.6 %all_to_all.25 = bf16[16,48,128]{2,1,0:T(8,128)(2,1)S(1)} all-to-all(bf16[16,48,128]{2,1,0:T(8,128)(2,1)S(1)} %shard_map.99), channel_id=1, replica_groups=mesh['groups'=2,'vocab'=8,'dp'=2] {'vocab','dp'}, dimensions={0} | all-to-all | bytes 393216 | tf_op jit(solution)/shard_map/all_to_all | solution.py:243
  84.9 1.6 %copy-done.3 = bf16[256,4096]{1,0:T(8,128)(2,1)S(1)} copy-done((bf16[256,4096]{1,0:T(8,128)(2,1)S(1)}, bf16[256,4096]{1,0:T(8,128)(2,1)}, u32[]{:S(2)}) %copy-start.3) | copy-done | bytes 2097176
  86.5 0.9 copy-done.5
  87.4 6.6 %shard_map.100 = (f32[1,1]{1,0:T(1,128)}, f32[2048,512]{1,0:T(8,128)}, f32[512,4096]{1,0:T(8,128)}) custom-call(bf16[8,2,48,128]{3,2,1,0:T(8,128)(2,1)S(1)} %bitcast.22, bf16[8,128]{1,0:T(8,128)(2,1)S(1)} %broadcast_in_dim.11.own_dl_ref.other_dl_ref, bf16[8,128]{1,0:T(8,128)(2,1)S(1)} %broadcast_in_dim.11.own_dl_ref.other_dl_ref, ...), custom_call_target="tpu_custom_call" | custom-call | flops 2147483648 | bytes 12582912 | tf_op jit(solution)/shard_map/pallas_call | solution.py:222
  (31 shorter events, 4.3 us)
Async XLA Ops:
  0.6 13.2 %copy-start = (bf16[256,4096]{1,0:T(8,128)(2,1)S(1)}, bf16[256,4096]{1,0:T(8,128)(2,1)}, u32[]{:S(2)}) copy-start(bf16[256,4096]{1,0:T(8,128)(2,1)} %param.9) | copy-start | bytes 6291460
  0.6 0.8 copy-start.6
  2.4 14.2 %all-to-all-start = ((s32[8,16,128]{2,1,0:T(8,128)}), s32[8,16,128]{2,1,0:T(8,128)S(1)}, u32[]{:S(2)}, u32[]{:S(2)}) async-start(s32[8,16,128]{2,1,0:T(8,128)} %bitcast.1), calls=%async_computation | async-start | bytes 131072 | tf_op jit(solution)/shard_map/all_to_all | solution.py:243
  9.7 47.2 %collective-permute-start.1 = (bf16[256,4096]{1,0:T(8,128)(2,1)}, bf16[256,4096]{1,0:T(8,128)(2,1)}, u32[]{:S(2)}, u32[]{:S(2)}) collective-permute-start(bf16[256,4096]{1,0:T(8,128)(2,1)} %own_hidden_ref.1), channel_id=1, source_target_pairs={{0,1},{1,0},{2,3},{3,2},{4,5},{5,4},{6,7},{7,6},{8,9},{9,8},{10,11... | collective-permute-start | bytes 6291464 | tf_op jit(solution)/shard_map/ppermute | solution.py:267
  13.8 0.7 copy-start.8
  13.8 0.7 copy-start.7
  16.9 0.8 copy-start.1
  17.7 19.7 %all-to-all-start.1 = ((bf16[8,16,2048]{2,1,0:T(8,128)(2,1)}), bf16[8,16,2048]{2,1,0:T(8,128)(2,1)S(1)}, u32[]{:S(2)}, u32[]{:S(2)}) async-start(bf16[8,16,2048]{2,1,0:T(8,128)(2,1)} %bitcast.17), calls=%async_computation.1 | async-start | bytes 1048576 | tf_op jit(solution)/shard_map/all_to_all | solution.py:243
  38.5 18.3 %all-to-all-start.2 = ((bf16[8,16,2048]{2,1,0:T(8,128)(2,1)}), bf16[8,16,2048]{2,1,0:T(8,128)(2,1)S(1)}, u32[]{:S(2)}, u32[]{:S(2)}) async-start(bf16[8,16,2048]{2,1,0:T(8,128)(2,1)} %bitcast.6), calls=%async_computation.2 | async-start | bytes 1048576 | tf_op jit(solution)/shard_map/all_to_all | solution.py:243
  43.0 1.3 %collective-permute-start = (bf16[16,2048]{1,0:T(8,128)(2,1)S(1)}, bf16[16,2048]{1,0:T(8,128)(2,1)S(1)}, u32[]{:S(2)}, u32[]{:S(2)}) collective-permute-start(bf16[16,2048]{1,0:T(8,128)(2,1)S(1)} %slice.4), channel_id=1, source_target_pairs={{0,1},{1,0},{2,3},{3,2},{4,5},{5,4},{6,7},{7,6},{8,9},{9,8},{10,11... | collective-permute-start | bytes 196616 | tf_op jit(solution)/shard_map/ppermute | solution.py:292
  43.0 4.2 %collective-permute-start.2 = (bf16[256,512]{1,0:T(8,128)(2,1)S(1)}, bf16[256,512]{1,0:T(8,128)(2,1)S(1)}, u32[]{:S(2)}, u32[]{:S(2)}) collective-permute-start(bf16[256,512]{1,0:T(8,128)(2,1)S(1)} %convolution_convert_fusion.basis_ref.own_basis_ref), channel_id=1, source_target_pairs={{0,1},{1,0},{2,3},{3,2},{4,5},{5,4},{6,7},{7,6},{8,9},{9,8},{10,11... | collective-permute-start | bytes 786440 | tf_op jit(solution)/shard_map/ppermute | solution.py:269
  56.9 1.6 %copy-start.2 = (bf16[2048,512]{1,0:T(8,128)(2,1)S(1)}, bf16[2048,512]{1,0:T(8,128)(2,1)}, u32[]{:S(2)}) copy-start(bf16[2048,512]{1,0:T(8,128)(2,1)} %w_ref.1) | copy-start | bytes 6291460
  58.9 1.6 %collective-permute-start.3 = (f32[128,512]{1,0:T(8,128)S(1)}, f32[128,512]{1,0:T(8,128)S(1)}, u32[]{:S(2)}, u32[]{:S(2)}) collective-permute-start(f32[128,512]{1,0:T(8,128)S(1)} %shard_map.97.pre_own_ref), channel_id=1, source_target_pairs={{0,1},{1,0},{2,3},{3,2},{4,5},{5,4},{6,7},{7,6},{8,9},{9,8},{10,11... | collective-permute-start | bytes 786440 | tf_op jit(solution)/shard_map/ppermute | solution.py:308
  61.5 0.7 copy-start.4
  62.1 11.0 %all-to-all-start.3 = ((f32[8,32,128]{2,1,0:T(8,128)}), f32[8,32,128]{2,1,0:T(8,128)S(1)}, u32[]{:S(2)}, u32[]{:S(2)}) async-start(f32[8,32,128]{2,1,0:T(8,128)} %bitcast.9), calls=%async_computation.3 | async-start | bytes 262144 | tf_op jit(solution)/shard_map/all_to_all | solution.py:243
  84.9 1.6 %copy-start.3 = (bf16[256,4096]{1,0:T(8,128)(2,1)S(1)}, bf16[256,4096]{1,0:T(8,128)(2,1)}, u32[]{:S(2)}) copy-start(bf16[256,4096]{1,0:T(8,128)(2,1)} %own_hidden_ref.1) | copy-start | bytes 6291460
  86.5 0.9 copy-start.5

commit v5 on v4

--- a/solution.py
+++ b/solution.py
@@ -41,7 +41,7 @@
     )(*args)
 
 
-def place_body(old_rows, groups, capacity, decomp_ref, asked_ref, adder_ref):
+def slot_places(decomp_ref, old_rows, groups, capacity):
     k_slots, new_rows = decomp_ref.shape
     slots, places = new_rows * k_slots, groups * capacity
     ids = decomp_ref[...]
@@ -54,32 +54,127 @@
     before = dot(hits.astype(jnp.bfloat16), earlier)
     ranking = jnp.sum(before * hits, 0, keepdims=True).astype(jnp.int32)
     place = jnp.where(usable, owners * capacity + ranking, -1)
-    taken = place == iota((places, slots), 0)
-    asked = jnp.sum(jnp.where(taken, local + 1, 0), 1, keepdims=True) - 1
-    asked_ref[...] = jnp.broadcast_to(asked, asked_ref.shape)
-    rows = groups * new_rows
-    mine = (iota((rows, slots), 1) % new_rows) == (iota((rows, slots), 0) % new_rows)
+    return place == iota((places, slots), 0), local
+
+
+def copies_body(ids_ref, copies_ref):
+    k_slots, new_rows = ids_ref.shape
+    ids = ids_ref[...]
+    rest = copies_ref.shape[2] - new_rows
+    if rest:
+        ids = jnp.concatenate([ids, jnp.zeros((k_slots, rest), jnp.int32)], 1)
+    for index in range(copies_ref.shape[0]):
+        copies_ref[index] = ids
+
+
+def column_body(
+    old_rows, groups, capacity, decomp_ref, counts_ref, targets_ref, adder_ref, scale_ref, own_ref
+):
+    taken, _ = slot_places(decomp_ref, old_rows, groups, capacity)
+    new_rows, slots = decomp_ref.shape[1], taken.shape[1]
+    mine = (iota((new_rows, slots), 1) % new_rows) == iota((new_rows, slots), 0)
     adder_ref[...] = dot(
         jnp.where(mine, 1.0, 0.0).astype(jnp.bfloat16),
         jnp.where(taken, 1.0, 0.0).astype(jnp.bfloat16),
         LAST,
     ).astype(jnp.bfloat16)
-
-
-def fetch_body(look_ref, old_ref, rows_ref):
-    places, lanes = look_ref.shape
+    square = (new_rows, new_rows)
+    diagonal = iota(square, 0) == iota(square, 1)
+    scale = jnp.sum(jnp.where(diagonal, counts_ref[...], 0), 1, keepdims=True)
+    scale_ref[...] = scale.astype(jnp.float32)
+    own_tokens, tokens = own_ref.shape[0], targets_ref.shape[1]
+    first = lax.axis_index("vocab") * own_tokens
+    chosen = iota((own_tokens, tokens), 1) == iota((own_tokens, tokens), 0) + first
+    own_ref[...] = jnp.sum(jnp.where(chosen, targets_ref[...], 0), 1, keepdims=True)
+
+
+def fetch_body(capacity, new_rows, look_ref, old_ref, rows_ref, blocks, sems):
+    senders, k_slots, _ = look_ref.shape
     old_rows = old_ref.shape[0]
-    look = look_ref[...][:, :1]
-    select = jnp.where(look == iota((places, old_rows), 1), 1.0, 0.0).astype(jnp.bfloat16)
-    rows_ref[...] = dot(select, old_ref[...]).astype(jnp.bfloat16)
+    slots = k_slots * new_rows
+    steps, _, wide = blocks.shape
+    flat = jnp.concatenate([look_ref[:, k, :new_rows] for k in range(k_slots)], 1)
+    local = flat - lax.axis_index("vocab") * old_rows
+    mine = (local >= 0) & (local < old_rows)
+    earlier = (iota((slots, slots), 0) < iota((slots, slots), 1)).astype(jnp.bfloat16)
+    before = dot(jnp.where(mine, 1.0, 0.0).astype(jnp.bfloat16), earlier).astype(jnp.int32)
+    place = jnp.where(mine, before, -1)
+    wanted = local + 1
+    asked = []
+    for r in range(senders):
+        taken = place[r : r + 1] == iota((capacity, slots), 0)
+        asked.append(jnp.sum(jnp.where(taken, wanted[r : r + 1], 0), 1, keepdims=True) - 1)
+    asked = jnp.concatenate(asked, 0)
+    select = jnp.where(asked == iota((asked.shape[0], old_rows), 1), 1.0, 0.0).astype(jnp.bfloat16)
+    leaving = []
+    for j in range(steps):
+        part = pl.ds(j * wide, wide)
+        blocks[j] = dot(select, old_ref[:, part]).astype(jnp.bfloat16)
+        leaving.append(pltpu.make_async_copy(blocks.at[j], rows_ref.at[:, part], sems.at[j]))
+        leaving[-1].start()
+    for copy in leaving:
+        copy.wait()
+
+
+def fetch_call(capacity, new_rows, look, old_half):
+    steps = 4
+    places, width = look.shape[0] * capacity, old_half.shape[1]
+    return pl.pallas_call(
+        functools.partial(fetch_body, capacity, new_rows),
+        out_shape=pltpu.HBM((places, width), jnp.bfloat16),
+        in_specs=[pl.BlockSpec(memory_space=pltpu.VMEM)] * 2,
+        out_specs=pl.BlockSpec(memory_space=pltpu.HBM),
+        scratch_shapes=[
+            pltpu.VMEM((steps, places, width // steps), jnp.bfloat16),
+            pltpu.SemaphoreType.DMA((steps,)),
+        ],
+        compiler_params=pltpu.CompilerParams(vmem_limit_bytes=12 * MIB),
+        cost_estimate=cost(1 << 24, 1 << 21),
+    )(look, old_half)
 
 
 def add_body(adder_ref, rows_ref, scale_ref, new_ref):
     new_ref[...] = (dot(adder_ref[...], rows_ref[...]) / scale_ref[...]).astype(jnp.bfloat16)
 
 
-def pre_body(new_ref, w_ref, pre_ref):
+def direct_body(hidden_ref, own_ref, other_ref, direct_ref):
+    new_rows, half = own_ref.shape
+    tokens, columns = direct_ref.shape
+    core = lax.axis_index("dp")
+    own_part = pl.ds(pl.multiple_of(core * half, half), half)
+    other_part = pl.ds(pl.multiple_of((1 - core) * half, half), half)
+    part = dot(hidden_ref[:, own_part], own_ref[...], LAST) + dot(
+        hidden_ref[:, other_part], other_ref[...], LAST
+    )
+    wide = jnp.concatenate([part, jnp.zeros((tokens, columns - new_rows), jnp.float32)], 1)
+    direct_ref[...] = pltpu.roll(wide, lax.axis_index("vocab") * new_rows, 1)
+
+
+def pre_body(count, *refs):
+    blocks, (w_ref, new_ref, pre_ref) = refs[:count], refs[count:]
+    rows = blocks[0].shape[0]
+    for k, block in enumerate(blocks):
+        index = lax.axis_index("vocab") ^ k if count > 1 else 0
+        new_ref[pl.ds(pl.multiple_of(index * rows, rows), rows)] = block[...]
     pre_ref[...] = dot(new_ref[...], w_ref[...])
+
+
+def copy_body(source_ref, out_ref, sem):
+    copy = pltpu.make_async_copy(source_ref, out_ref, sem)
+    copy.start()
+    copy.wait()
+
+
+def held(array):
+    return pl.pallas_call(
+        copy_body,
+        out_shape=pltpu.VMEM(array.shape, array.dtype),
+        in_specs=[pl.BlockSpec(memory_space=pltpu.HBM)],
+        out_specs=pl.BlockSpec(memory_space=pltpu.VMEM),
+        scratch_shapes=[pltpu.SemaphoreType.DMA],
+        compiler_params=pltpu.CompilerParams(vmem_limit_bytes=8 * MIB),
+        cost_estimate=cost(0, 2 * array.size),
+    )(in_hbm(array))
 
 
 def share_body(pre_own_ref, pre_other_ref, basis_ref, direct_ref, pre_ref, units_ref, share_ref):
@@ -112,6 +207,10 @@
     packet = jnp.concatenate([dlogits, extra], 0).astype(jnp.bfloat16)
     for index in range(copies):
         packets_ref[index] = packet
+
+
+def in_hbm(array):
+    return pltpu.with_memory_space_constraint(array, pltpu.HBM)
 
 
 def final_body(
@@ -167,7 +266,7 @@
         other_dl, other_basis_ref[...], FIRST
     )
     grad_pre = jax.vjp(activate, pre_ref[...])[1](grad_units)[0].astype(jnp.bfloat16)
-    for j in range(steps):
+    for j in range(in_blocks.shape[0]):
         part = pl.ds(j * high, high)
         in_blocks[j] = dot(new_ref[:, part], grad_pre, FIRST)
         leaving.append(
@@ -202,9 +301,8 @@
 
 
 def final_call(
-    own_tokens, packets, units, pre, own_basis, other_basis, own_hidden, other_hidden, new
+    own_tokens, packets, units, pre, own_basis, other_basis, own_hidden, other_hidden, new, steps=8
 ):
-    steps = 8
     tokens, width = own_hidden.shape
     hidden = pre.shape[1]
     half = new.shape[1]
@@ -236,7 +334,7 @@
         ],
         compiler_params=pltpu.CompilerParams(vmem_limit_bytes=44 * MIB),
         cost_estimate=cost(4 * tokens * hidden * width, 4 * (half + width) * hidden),
-    )(*args, own_hidden, other_hidden)
+    )(*args, in_hbm(own_hidden), in_hbm(other_hidden))
 
 
 def exchange(array, axes="vocab"):
@@ -258,53 +356,65 @@
     swap = [(0, 1), (1, 0)]
     shaped = jax.ShapeDtypeStruct
 
-    asked, adder = whole_call(
-        functools.partial(place_body, old_rows, groups, capacity),
-        (shaped((places, 128), jnp.int32), shaped((columns, places), jnp.bfloat16)),
-        (decomp.T,),
-    )
-    look = exchange(asked.reshape(groups, capacity, 128))
+    sizes = (old_rows, groups, capacity)
+    ids = whole_call(
+        copies_body, shaped((groups, k_slots, max(new_rows, 128)), jnp.int32), (decomp.T,)
+    )
+    look = exchange(ids)
+    ids, hidden_states = lax.optimization_barrier((ids, hidden_states))
     hidden_other = lax.ppermute(hidden_states, "dp", swap)
+    old_half = lax.dynamic_slice_in_dim(old_embed, dp_index * half_width, half_width, 1)
+    own_tokens = tokens // groups
+    adder, scale, own_targets = whole_call(
+        functools.partial(column_body, *sizes),
+        (
+            shaped((new_rows, places), jnp.bfloat16),
+            shaped((new_rows, 1), jnp.float32),
+            shaped((own_tokens, 1), jnp.int32),
+        ),
+        (decomp.T, counts[None], targets[None]),
+    )
+    look, old_half, adder, scale, own_targets = lax.optimization_barrier(
+        (look, old_half, adder, scale, own_targets)
+    )
+
+    fetched = fetch_call(capacity, new_rows, look, old_half)
+    arrived = exchange(fetched.reshape(groups, capacity, half_width)).reshape(places, half_width)
     basis = dot(hidden_states, w_out, LAST).astype(jnp.bfloat16)
     basis_other = lax.ppermute(basis, "dp", swap)
-    old_half = lax.dynamic_slice_in_dim(old_embed, dp_index * half_width, half_width, 1)
-    scale = jnp.tile(counts.astype(jnp.float32), groups)[:, None]
-    own_tokens = tokens // groups
-    own_targets = lax.dynamic_slice_in_dim(targets, own_index * own_tokens, own_tokens)[:, None]
-    look, old_half, basis, scale, own_targets = lax.optimization_barrier(
-        (look, old_half, basis, scale, own_targets)
-    )
-
-    fetched = whole_call(
-        fetch_body,
-        shaped((places, half_width), jnp.bfloat16),
-        (look.reshape(places, 128), old_half),
-    )
-    arrived = exchange(fetched.reshape(groups, capacity, half_width)).reshape(places, half_width)
-
-    new_copies = whole_call(
-        add_body, shaped((columns, half_width), jnp.bfloat16), (adder, arrived, scale)
-    )
-    new_all = exchange(new_copies.reshape(groups, new_rows, half_width)).reshape(
-        columns, half_width
-    )
-    new_own = new_copies[:new_rows]
+    arrived, basis, basis_other, hidden_other = lax.optimization_barrier(
+        (arrived, basis, basis_other, hidden_other)
+    )
+
+    new_own = whole_call(
+        add_body, shaped((new_rows, half_width), jnp.bfloat16), (adder, arrived, scale)
+    )
+    if groups in (2, 4, 8):
+        steps = range(groups - 1, 0, -1)
+        blocks = [
+            lax.ppermute(new_own, "vocab", [(i, i ^ k) for i in range(groups)]) for k in steps
+        ]
+        blocks = [new_own] + blocks[::-1]
+    else:
+        copies = jnp.broadcast_to(new_own[None], (groups, new_rows, half_width))
+        blocks = [exchange(copies).reshape(columns, half_width)]
     new_other = lax.ppermute(new_own, "dp", swap)
-    new_wide = jnp.where(
-        dp_index == 0,
-        jnp.concatenate([new_own, new_other], 1),
-        jnp.concatenate([new_other, new_own], 1),
-    )
-    direct = lax.dynamic_update_slice(
-        jnp.zeros((tokens, columns), jnp.float32),
-        dot(hidden_states, new_wide, LAST),
-        (0, own_index * new_rows),
-    )
-    new_all, direct, hidden_other, basis_other = lax.optimization_barrier(
-        (new_all, direct, hidden_other, basis_other)
-    )
-
-    pre_own = whole_call(pre_body, shaped((columns, hidden), jnp.float32), (new_all, w_in))
+    direct = whole_call(
+        direct_body,
+        shaped((tokens, columns), jnp.float32),
+        (hidden_states, new_own, new_other),
+    )
+    w_held = held(w_in)
+    blocks, direct, w_held = lax.optimization_barrier((blocks, direct, w_held))
+
+    new_all, pre_own = whole_call(
+        functools.partial(pre_body, len(blocks)),
+        (
+            shaped((columns, half_width), jnp.bfloat16),
+            shaped((columns, hidden), jnp.float32),
+        ),
+        (*blocks, w_held),
+    )
     pre_other = lax.ppermute(pre_own, "dp", swap)
     pre_units, hidden_units, share = whole_call(
         share_body,

time: 94.8 us -> 82.6 us (0.87)
  waiting for transfers between devices: 35 us -> 20 us
  blocking collectives: 11.6 us -> 21.8 us
  local copies, waits for them, and re-layouts: 10 us -> 0.93 us
  starting transfers between devices: 19.7 us -> 22.1 us
  matrix products: 6.37 us -> 4.11 us
  Pallas kernels: 10.6 us -> 12.3 us
    all_to_all x4 -> x2, waiting for transfers between devices: 32.8 us -> 14.5 us  [exchange(): return lax.all_to_all(array, axes, 0, 0, tiled=True)]
    ppermute x0 -> x7, starting transfers between devices: none -> 11.2 us  [shards(): lax.ppermute(new_own, 'vocab', [(i, i ^ k) for i in range(groups)])]
    all_to_all x1 -> x2, blocking collectives: 11.6 us -> 21.8 us  [exchange(): return lax.all_to_all(array, axes, 0, 0, tiled=True)]
    all_to_all x4 -> x2, starting transfers between devices: 19.1 us -> 10.3 us  [exchange(): return lax.all_to_all(array, axes, 0, 0, tiled=True)]
    unnamed x18 -> x12, local copies, waits for them, and re-layouts: 6.91 us -> 0.85 us
    pallas_call x0 -> x2, Pallas kernels: none -> 2.99 us  [the longest x1 1.6 us: held(): pl.pallas_call(copy_body, out_shape=pltpu.VMEM(array.shape, array.dtype),...]
    ppermute x0 -> x7, waiting for transfers between devices: none -> 2.48 us  [shards(): lax.ppermute(new_own, 'vocab', [(i, i ^ k) for i in range(groups)])]
    dot_general x2 -> x1, matrix products: 6.37 us -> 4.11 us  [dot(): return lax.dot_general(a, b, dims, preferred_element_type=jnp.float32)]
  transfers between devices with their start and end apart: 8 -> 13, of which waited for: 6 -> 6; matrix products, arithmetic and copies ran while one was open for 10% -> 5% of each run, Pallas kernels for 2% -> 5%
where the time goes in v5:
time: 82.6 us; the launch traced here: 82.1 us
  starting transfers between devices  22.1 us (27%)
  blocking collectives  21.8 us (26%)
  waiting for transfers between devices  20 us (24%)
  Pallas kernels  12.3 us (15%)
  matrix products  4.11 us (5%)
  local copies, waits for them, and re-layouts  0.93 us (1%)
    all_to_all x2, blocking collectives, exchange(): return lax.all_to_all(array, axes, 0, 0, tiled=True)  21.8 us
    all_to_all x2, waiting for transfers between devices, exchange(): return lax.all_to_all(array, axes, 0, 0, tiled=True)  14.5 us
    ppermute x7, starting transfers between devices, shards(): lax.ppermute(new_own, 'vocab', [(i, i ^ k) for i in range(groups)])  11.2 us
    all_to_all x2, starting transfers between devices, exchange(): return lax.all_to_all(array, axes, 0, 0, tiled=True)  10.3 us
    pallas_call x1, Pallas kernels, final_call(): pl.pallas_call(functools.partial(final_body, own_tokens), out_shape=(jax....  6.46 us
    dot_general x1, matrix products, dot(): return lax.dot_general(a, b, dims, preferred_element_type=jnp.float32)  4.11 us
    pallas_call x7, Pallas kernels, whole_call(): pl.pallas_call(body, out_shape=outs, in_specs=[pl.BlockSpec(memory_space=...  2.88 us
    ppermute x7, waiting for transfers between devices, shards(): lax.ppermute(new_own, 'vocab', [(i, i ^ k) for i in range(groups)])  2.48 us
  transfers between devices with their start and end apart: 13, of which 6 were waited for; matrix products, arithmetic and copies ran while one was open for 5% of the time, Pallas kernels for 5%

profile of v5, /device:TPU:0, one launch (start us, length us, event | category | flops | bytes accessed | tf_op | source)
XLA Modules:
  0.0 82.1 jit_solution(16569072220338087199)
XLA Ops:
  0.7 0.8 %copy-done.2 = s32[16,8]{0,1:T(8,128)S(1)} copy-done((s32[16,8]{0,1:T(8,128)S(1)}, s32[16,8]{0,1:T(8,128)}, u32[]{:S(2)}) %copy-start.2) | copy-done | bytes 536
  1.5 0.6 shard_map.94
  2.1 0.5 collective-permute-start.1
  2.6 6.8 %all-to-all-start = ((s32[8,8,128]{2,1,0:T(8,128)}), s32[8,8,128]{2,1,0:T(8,128)S(1)}, u32[]{:S(2)}, u32[]{:S(2)}) async-start(s32[8,8,128]{2,1,0:T(8,128)} %shard_map.94), calls=%async_computation | async-start | bytes 65536 | tf_op jit(solution)/shard_map/all_to_all | solution.py:341
  9.8 6.2 %all-to-all-done.look_ref = s32[8,8,128]{2,1,0:T(8,128)S(1)} async-done(((s32[8,8,128]{2,1,0:T(8,128)}), s32[8,8,128]{2,1,0:T(8,128)S(1)}, u32[]{:S(2)}, u32[]{:S(2)}) %all-to-all-start) | async-done | bytes 32800 | tf_op jit(solution)/shard_map/all_to_all | solution.py:341
  16.1 1.4 %shard_map.96 = bf16[128,2048]{1,0:T(8,128)(2,1)} custom-call(s32[8,8,128]{2,1,0:T(8,128)S(1)} %all-to-all-done.look_ref, bf16[256,2048]{1,0:T(8,128)(2,1)S(1)} %constant_dynamic-slice_fusion.old_ref), custom_call_target="tpu_custom_call" | custom-call | flops 16777216 | bytes 2097152 | tf_op jit(solution)/shard_map/pallas_call | solution.py:122
  17.5 3.5 %all-to-all-start.1 = ((bf16[8,16,2048]{2,1,0:T(8,128)(2,1)}), bf16[8,16,2048]{2,1,0:T(8,128)(2,1)S(1)}, u32[]{:S(2)}, u32[]{:S(2)}) async-start(bf16[8,16,2048]{2,1,0:T(8,128)(2,1)} %bitcast.17), calls=%async_computation.1 | async-start | bytes 1048576 | tf_op jit(solution)/shard_map/all_to_all | solution.py:341
  21.0 4.1 %convolution_convert_fusion.basis_ref.own_basis_ref = bf16[256,512]{1,0:T(8,128)(2,1)S(1)} fusion(bf16[256,4096]{1,0:T(8,128)(2,1)} %own_hidden_ref, bf16[512,4096]{1,0:T(8,128)(2,1)} %param.13), kind=kOutput, calls=%fused_computation | convolution fusion | flops 1073872896 | bytes 6553600 | tf_op jit(solution)/shard_map/dot_general | solution.py:21
  25.2 1.5 %collective-permute-done.other_basis_ref = bf16[256,512]{1,0:T(8,128)(2,1)S(1)} collective-permute-done((bf16[256,512]{1,0:T(8,128)(2,1)S(1)}, bf16[256,512]{1,0:T(8,128)(2,1)S(1)}, u32[]{:S(2)}, u32[]{:S(2)}) %collective-permute-start) | collective-permute-done | bytes 262176 | tf_op jit(solution)/shard_map/ppermute | solution.py:384
  26.7 8.2 %all-to-all-done.1 = bf16[8,16,2048]{2,1,0:T(8,128)(2,1)S(1)} async-done(((bf16[8,16,2048]{2,1,0:T(8,128)(2,1)}), bf16[8,16,2048]{2,1,0:T(8,128)(2,1)S(1)}, u32[]{:S(2)}, u32[]{:S(2)}) %all-to-all-start.1) | async-done | bytes 524320 | tf_op jit(solution)/shard_map/all_to_all | solution.py:341
  35.2 2.4 %collective-permute-start.8 = (bf16[16,2048]{1,0:T(8,128)(2,1)S(1)}, bf16[16,2048]{1,0:T(8,128)(2,1)S(1)}, u32[]{:S(2)}, u32[]{:S(2)}) collective-permute-start(bf16[16,2048]{1,0:T(8,128)(2,1)S(1)} %shard_map.97.own_ref.refs_0_), channel_id=1, source_target_pairs={{0,14},{2,12},{4,10},{6,8},{8,6},{10,4},{12,2},{14,0},{1,15},{3,13... | collective-permute-start | bytes 196616 | tf_op jit(solution)/shard_map/ppermute | solution.py:395
  37.6 2.3 %collective-permute-start.7 = (bf16[16,2048]{1,0:T(8,128)(2,1)S(1)}, bf16[16,2048]{1,0:T(8,128)(2,1)S(1)}, u32[]{:S(2)}, u32[]{:S(2)}) collective-permute-start(bf16[16,2048]{1,0:T(8,128)(2,1)S(1)} %shard_map.97.own_ref.refs_0_), channel_id=1, source_target_pairs={{0,12},{2,14},{4,8},{6,10},{8,4},{10,6},{12,0},{14,2},{1,13},{3,15... | collective-permute-start | bytes 196616 | tf_op jit(solution)/shard_map/ppermute | solution.py:395
  40.0 3.0 %collective-permute-start.5 = (bf16[16,2048]{1,0:T(8,128)(2,1)S(1)}, bf16[16,2048]{1,0:T(8,128)(2,1)S(1)}, u32[]{:S(2)}, u32[]{:S(2)}) collective-permute-start(bf16[16,2048]{1,0:T(8,128)(2,1)S(1)} %shard_map.97.own_ref.refs_0_), channel_id=1, source_target_pairs={{0,8},{2,10},{4,12},{6,14},{8,0},{10,2},{12,4},{14,6},{1,9},{3,11}... | collective-permute-start | bytes 196616 | tf_op jit(solution)/shard_map/ppermute | solution.py:395
  43.0 3.0 %collective-permute-start.3 = (bf16[16,2048]{1,0:T(8,128)(2,1)S(1)}, bf16[16,2048]{1,0:T(8,128)(2,1)S(1)}, u32[]{:S(2)}, u32[]{:S(2)}) collective-permute-start(bf16[16,2048]{1,0:T(8,128)(2,1)S(1)} %shard_map.97.own_ref.refs_0_), channel_id=1, source_target_pairs={{0,4},{2,6},{4,0},{6,2},{8,12},{10,14},{12,8},{14,10},{1,5},{3,7},... | collective-permute-start | bytes 196616 | tf_op jit(solution)/shard_map/ppermute | solution.py:395
  46.0 0.4 collective-permute-start.2
  46.4 1.6 %shard_map.99.refs_8_ = bf16[2048,512]{1,0:T(8,128)(2,1)S(1)} custom-call(bf16[2048,512]{1,0:T(8,128)(2,1)} %source_ref.1), custom_call_target="tpu_custom_call" | custom-call | bytes 2097152 | tf_op jit(solution)/shard_map/pallas_call | solution.py:169
  48.0 0.7 shard_map.98.direct_ref
  48.8 1.0 %collective-permute-done.6.refs_5_ = bf16[16,2048]{1,0:T(8,128)(2,1)S(1)} collective-permute-done((bf16[16,2048]{1,0:T(8,128)(2,1)S(1)}, bf16[16,2048]{1,0:T(8,128)(2,1)S(1)}, u32[]{:S(2)}, u32[]{:S(2)}) %collective-permute-start.6) | collective-permute-done | bytes 65568 | tf_op jit(solution)/shard_map/ppermute | solution.py:395
  49.8 1.5 %collective-permute-done.3.refs_2_ = bf16[16,2048]{1,0:T(8,128)(2,1)S(1)} collective-permute-done((bf16[16,2048]{1,0:T(8,128)(2,1)S(1)}, bf16[16,2048]{1,0:T(8,128)(2,1)S(1)}, u32[]{:S(2)}, u32[]{:S(2)}) %collective-permute-start.3) | collective-permute-done | bytes 65568 | tf_op jit(solution)/shard_map/ppermute | solution.py:395
  51.2 0.5 shard_map.100
  51.8 1.5 %collective-permute-done.10.pre_other_ref = f32[128,512]{1,0:T(8,128)S(1)} collective-permute-done((f32[128,512]{1,0:T(8,128)S(1)}, f32[128,512]{1,0:T(8,128)S(1)}, u32[]{:S(2)}, u32[]{:S(2)}) %collective-permute-start.10) | collective-permute-done | bytes 262176 | tf_op jit(solution)/shard_map/ppermute | solution.py:418
  53.6 10.3 %all_to_all.20.shares_ref = f32[8,32,128]{2,1,0:T(8,128)S(1)} all-to-all(f32[8,32,128]{2,1,0:T(8,128)S(1)} %bitcast.12), channel_id=1, replica_groups=mesh['groups'=2,'vocab'=8,'dp'=2] {'vocab'}, dimensions={0} | all-to-all | bytes 262144 | tf_op jit(solution)/shard_map/all_to_all | solution.py:341
  64.1 11.6 %all_to_all.21 = bf16[16,48,128]{2,1,0:T(8,128)(2,1)S(1)} all-to-all(bf16[16,48,128]{2,1,0:T(8,128)(2,1)S(1)} %shard_map.102), channel_id=1, replica_groups=mesh['groups'=2,'vocab'=8,'dp'=2] {'vocab','dp'}, dimensions={0} | all-to-all | bytes 393216 | tf_op jit(solution)/shard_map/all_to_all | solution.py:341
  75.7 6.5 %shard_map.103 = (f32[1,1]{1,0:T(1,128)}, f32[2048,512]{1,0:T(8,128)}, f32[512,4096]{1,0:T(8,128)}) custom-call(bf16[8,2,48,128]{3,2,1,0:T(8,128)(2,1)S(1)} %bitcast.11, bf16[8,128]{1,0:T(8,128)(2,1)S(1)} %broadcast_in_dim.11.own_dl_ref.other_dl_ref, bf16[8,128]{1,0:T(8,128)(2,1)S(1)} %broadcast_in_dim.11.own_dl_ref.other_dl_ref, ...), custom_call_target="tpu_custom_call" | custom-call | flops 2147483648 | bytes 12582912 | tf_op jit(solution)/shard_map/pallas_call | solution.py:320
  (29 shorter events, 1.4 us)
Async XLA Ops:
  0.6 8.7 %copy-start = (bf16[256,4096]{1,0:T(8,128)(2,1)S(1)}, bf16[256,4096]{1,0:T(8,128)(2,1)}, u32[]{:S(2)}) copy-start(bf16[256,4096]{1,0:T(8,128)(2,1)} %param.9) | copy-start | bytes 6291460
  0.6 8.8 %copy-start.5 = (s32[16]{0:T(128)S(1)}, s32[16]{0:T(128)}, u32[]{:S(2)}) copy-start(s32[16]{0:T(128)} %param.11) | copy-start | bytes 196
  0.7 8.8 %copy-start.4 = (s32[256]{0:T(256)S(1)}, s32[256]{0:T(256)}, u32[]{:S(2)}) copy-start(s32[256]{0:T(256)} %param.8) | copy-start | bytes 3076
  0.7 0.8 %copy-start.2 = (s32[16,8]{0,1:T(8,128)S(1)}, s32[16,8]{0,1:T(8,128)}, u32[]{:S(2)}) copy-start(s32[16,8]{0,1:T(8,128)} %param.10) | copy-start | bytes 1540
  1.5 8.0 %copy-start.3 = (s32[16,8]{0,1:T(8,128)S(1)}, s32[16,8]{0,1:T(8,128)}, u32[]{:S(2)}) copy-start(s32[16,8]{0,1:T(8,128)} %param.10) | copy-start | bytes 1540
  2.1 32.8 %collective-permute-start.1 = (bf16[256,4096]{1,0:T(8,128)(2,1)}, bf16[256,4096]{1,0:T(8,128)(2,1)}, u32[]{:S(2)}, u32[]{:S(2)}) collective-permute-start(bf16[256,4096]{1,0:T(8,128)(2,1)} %own_hidden_ref), channel_id=1, source_target_pairs={{0,1},{1,0},{2,3},{3,2},{4,5},{5,4},{6,7},{7,6},{8,9},{9,8},{10,11... | collective-permute-start | bytes 6291464 | tf_op jit(solution)/shard_map/ppermute | solution.py:365
  2.6 13.5 %all-to-all-start = ((s32[8,8,128]{2,1,0:T(8,128)}), s32[8,8,128]{2,1,0:T(8,128)S(1)}, u32[]{:S(2)}, u32[]{:S(2)}) async-start(s32[8,8,128]{2,1,0:T(8,128)} %shard_map.94), calls=%async_computation | async-start | bytes 65536 | tf_op jit(solution)/shard_map/all_to_all | solution.py:341
  17.5 17.5 %all-to-all-start.1 = ((bf16[8,16,2048]{2,1,0:T(8,128)(2,1)}), bf16[8,16,2048]{2,1,0:T(8,128)(2,1)S(1)}, u32[]{:S(2)}, u32[]{:S(2)}) async-start(bf16[8,16,2048]{2,1,0:T(8,128)(2,1)} %bitcast.17), calls=%async_computation.1 | async-start | bytes 1048576 | tf_op jit(solution)/shard_map/all_to_all | solution.py:341
  25.1 1.6 %collective-permute-start = (bf16[256,512]{1,0:T(8,128)(2,1)S(1)}, bf16[256,512]{1,0:T(8,128)(2,1)S(1)}, u32[]{:S(2)}, u32[]{:S(2)}) collective-permute-start(bf16[256,512]{1,0:T(8,128)(2,1)S(1)} %convolution_convert_fusion.basis_ref.own_basis_ref), channel_id=1, source_target_pairs={{0,1},{1,0},{2,3},{3,2},{4,5},{5,4},{6,7},{7,6},{8,9},{9,8},{10,11... | collective-permute-start | bytes 786440 | tf_op jit(solution)/shard_map/ppermute | solution.py:384
  35.1 12.9 %copy-start.1 = (bf16[256,4096]{1,0:T(8,128)(2,1)S(1)}, bf16[256,4096]{1,0:T(8,128)(2,1)}, u32[]{:S(2)}) copy-start(bf16[256,4096]{1,0:T(8,128)(2,1)} %own_hidden_ref) | copy-start | bytes 6291460
  35.1 7.8 %collective-permute-start.9 = (bf16[16,2048]{1,0:T(8,128)(2,1)S(1)}, bf16[16,2048]{1,0:T(8,128)(2,1)S(1)}, u32[]{:S(2)}, u32[]{:S(2)}) collective-permute-start(bf16[16,2048]{1,0:T(8,128)(2,1)S(1)} %shard_map.97.own_ref.refs_0_), channel_id=1, source_target_pairs={{0,1},{1,0},{2,3},{3,2},{4,5},{5,4},{6,7},{7,6},{8,9},{9,8},{10,11... | collective-permute-start | bytes 196616 | tf_op jit(solution)/shard_map/ppermute | solution.py:401
  35.2 7.8 %collective-permute-start.8 = (bf16[16,2048]{1,0:T(8,128)(2,1)S(1)}, bf16[16,2048]{1,0:T(8,128)(2,1)S(1)}, u32[]{:S(2)}, u32[]{:S(2)}) collective-permute-start(bf16[16,2048]{1,0:T(8,128)(2,1)S(1)} %shard_map.97.own_ref.refs_0_), channel_id=1, source_target_pairs={{0,14},{2,12},{4,10},{6,8},{8,6},{10,4},{12,2},{14,0},{1,15},{3,13... | collective-permute-start | bytes 196616 | tf_op jit(solution)/shard_map/ppermute | solution.py:395
  37.6 8.4 %collective-permute-start.7 = (bf16[16,2048]{1,0:T(8,128)(2,1)S(1)}, bf16[16,2048]{1,0:T(8,128)(2,1)S(1)}, u32[]{:S(2)}, u32[]{:S(2)}) collective-permute-start(bf16[16,2048]{1,0:T(8,128)(2,1)S(1)} %shard_map.97.own_ref.refs_0_), channel_id=1, source_target_pairs={{0,12},{2,14},{4,8},{6,10},{8,4},{10,6},{12,0},{14,2},{1,13},{3,15... | collective-permute-start | bytes 196616 | tf_op jit(solution)/shard_map/ppermute | solution.py:395
  40.0 9.8 %collective-permute-start.6 = (bf16[16,2048]{1,0:T(8,128)(2,1)S(1)}, bf16[16,2048]{1,0:T(8,128)(2,1)S(1)}, u32[]{:S(2)}, u32[]{:S(2)}) collective-permute-start(bf16[16,2048]{1,0:T(8,128)(2,1)S(1)} %shard_map.97.own_ref.refs_0_), channel_id=1, source_target_pairs={{0,10},{2,8},{4,14},{6,12},{8,2},{10,0},{12,6},{14,4},{1,11},{3,9}... | collective-permute-start | bytes 196616 | tf_op jit(solution)/shard_map/ppermute | solution.py:395
  40.0 9.8 %collective-permute-start.5 = (bf16[16,2048]{1,0:T(8,128)(2,1)S(1)}, bf16[16,2048]{1,0:T(8,128)(2,1)S(1)}, u32[]{:S(2)}, u32[]{:S(2)}) collective-permute-start(bf16[16,2048]{1,0:T(8,128)(2,1)S(1)} %shard_map.97.own_ref.refs_0_), channel_id=1, source_target_pairs={{0,8},{2,10},{4,12},{6,14},{8,0},{10,2},{12,4},{14,6},{1,9},{3,11}... | collective-permute-start | bytes 196616 | tf_op jit(solution)/shard_map/ppermute | solution.py:395
  42.9 6.8 %collective-permute-start.4 = (bf16[16,2048]{1,0:T(8,128)(2,1)S(1)}, bf16[16,2048]{1,0:T(8,128)(2,1)S(1)}, u32[]{:S(2)}, u32[]{:S(2)}) collective-permute-start(bf16[16,2048]{1,0:T(8,128)(2,1)S(1)} %shard_map.97.own_ref.refs_0_), channel_id=1, source_target_pairs={{0,6},{2,4},{4,2},{6,0},{8,14},{10,12},{12,10},{14,8},{1,7},{3,5},... | collective-permute-start | bytes 196616 | tf_op jit(solution)/shard_map/ppermute | solution.py:395
  43.0 8.3 %collective-permute-start.3 = (bf16[16,2048]{1,0:T(8,128)(2,1)S(1)}, bf16[16,2048]{1,0:T(8,128)(2,1)S(1)}, u32[]{:S(2)}, u32[]{:S(2)}) collective-permute-start(bf16[16,2048]{1,0:T(8,128)(2,1)S(1)} %shard_map.97.own_ref.refs_0_), channel_id=1, source_target_pairs={{0,4},{2,6},{4,0},{6,2},{8,12},{10,14},{12,8},{14,10},{1,5},{3,7},... | collective-permute-start | bytes 196616 | tf_op jit(solution)/shard_map/ppermute | solution.py:395
  46.0 5.2 %collective-permute-start.2 = (bf16[16,2048]{1,0:T(8,128)(2,1)S(1)}, bf16[16,2048]{1,0:T(8,128)(2,1)S(1)}, u32[]{:S(2)}, u32[]{:S(2)}) collective-permute-start(bf16[16,2048]{1,0:T(8,128)(2,1)S(1)} %shard_map.97.own_ref.refs_0_), channel_id=1, source_target_pairs={{0,2},{2,0},{4,6},{6,4},{8,10},{10,8},{12,14},{14,12},{1,3},{3,1},... | collective-permute-start | bytes 196616 | tf_op jit(solution)/shard_map/ppermute | solution.py:395
  51.7 1.6 %collective-permute-start.10 = (f32[128,512]{1,0:T(8,128)S(1)}, f32[128,512]{1,0:T(8,128)S(1)}, u32[]{:S(2)}, u32[]{:S(2)}) collective-permute-start(f32[128,512]{1,0:T(8,128)S(1)} %get-tuple-element.52.pre_own_ref), channel_id=1, source_target_pairs={{0,1},{1,0},{2,3},{3,2},{4,5},{5,4},{6,7},{7,6},{8,9},{9,8},{10,11... | collective-permute-start | bytes 786440 | tf_op jit(solution)/shard_map/ppermute | solution.py:418

commit v6 on v5

--- a/solution.py
+++ b/solution.py
@@ -215,27 +215,16 @@
 
 def final_body(
     own_tokens,
-    packets_ref,
-    own_dl_ref,
-    other_dl_ref,
-    units_ref,
-    pre_ref,
-    own_basis_ref,
-    other_basis_ref,
-    new_ref,
-    own_hidden_ref,
-    other_hidden_ref,
-    loss_ref,
-    grad_in_ref,
-    grad_out_ref,
-    hidden_blocks,
-    in_blocks,
-    out_blocks,
-    sems,
+    own_packets_ref,
+    other_packets_ref,
+    *refs,
 ):
-    groups, cores, _, columns = packets_ref.shape
+    dlogits_refs, refs = refs[:-14], refs[-14:]
+    units_ref, pre_ref, own_basis_ref, other_basis_ref, new_ref = refs[:5]
+    own_hidden_ref, other_hidden_ref, loss_ref, grad_in_ref, grad_out_ref = refs[5:10]
+    hidden_blocks, in_blocks, out_blocks, sems = refs[10:]
+    groups, _, columns = own_packets_ref.shape
     steps = out_blocks.shape[0]
-    own = lax.axis_index("dp")
     tokens = groups * own_tokens
     wide = out_blocks.shape[2]
     high = in_blocks.shape[1]
@@ -243,23 +232,20 @@
     arriving = []
     for j in range(steps):
         part = pl.ds(j * wide, wide)
-        for core, source in enumerate((own_hidden_ref, other_hidden_ref)):
-            arriving.append(
-                pltpu.make_async_copy(
-                    source.at[:, part],
-                    hidden_blocks.at[j, pl.ds(core * tokens, tokens)],
-                    sems.at[2 * steps + 2 * j + core],
-                )
+        arriving.append(
+            pltpu.make_async_copy(
+                other_hidden_ref.at[:, part], hidden_blocks.at[j], sems.at[2 * steps + j]
             )
-            arriving[-1].start()
-
-    def dlogits(core):
-        return jnp.concatenate([packets_ref[g, core, :own_tokens] for g in range(groups)], 0)
+        )
+        arriving[-1].start()
+
+    def dlogits(packets_ref):
+        return jnp.concatenate([packets_ref[g, :own_tokens] for g in range(groups)], 0)
 
     if own_tokens % 16 == 0:
-        own_dl, other_dl = dlogits(own), dlogits(1 - own)
+        own_dl, other_dl = dlogits(own_packets_ref), dlogits(other_packets_ref)
     else:
-        own_dl, other_dl = own_dl_ref[...], other_dl_ref[...]
+        own_dl, other_dl = (ref[...] for ref in dlogits_refs)
     leaving = []
 
     grad_units = dot(own_dl, own_basis_ref[...], FIRST) + dot(
@@ -280,9 +266,10 @@
     )
     for j in range(steps):
         part = pl.ds(j * wide, wide)
-        arriving[2 * j].wait()
-        arriving[2 * j + 1].wait()
-        out_blocks[j] = dot(mixed, hidden_blocks[j])
+        arriving[j].wait()
+        out_blocks[j] = dot(
+            mixed, jnp.concatenate([own_hidden_ref[:, part], hidden_blocks[j]], 0)
+        )
         leaving.append(
             pltpu.make_async_copy(out_blocks.at[j], grad_out_ref.at[:, part], sems.at[j])
         )
@@ -290,12 +277,12 @@
 
     loss = jnp.zeros((16, columns), jnp.float32)
     first = own_tokens // 16 * 16
-    for g in range(groups):
-        for c in range(cores):
-            loss = loss + packets_ref[g, c, first : first + 16].astype(jnp.float32)
+    for packets_ref in (own_packets_ref, other_packets_ref):
+        for g in range(groups):
+            loss = loss + packets_ref[g, first : first + 16].astype(jnp.float32)
     loss = jnp.where(iota(loss.shape, 0) == own_tokens - first, loss, 0.0)
     loss = jnp.sum(jnp.sum(loss, 0, keepdims=True), 1, keepdims=True)
-    loss_ref[...] = loss / (tokens * cores)
+    loss_ref[...] = loss / (2 * tokens)
     for copy in leaving:
         copy.wait()
 
@@ -309,14 +296,10 @@
     vmem = pl.BlockSpec(memory_space=pltpu.VMEM)
     hbm = pl.BlockSpec(memory_space=pltpu.HBM)
     if own_tokens % 16 == 0:
-        parts = (jnp.zeros((8, 128), jnp.bfloat16),) * 2
+        parts = ()
     else:
-        own = lax.axis_index("dp")
-        parts = tuple(
-            lax.dynamic_index_in_dim(packets, core, 1, False)[:, :own_tokens].reshape(tokens, -1)
-            for core in (own, 1 - own)
-        )
-    args = (packets, *parts, units, pre, own_basis, other_basis, new)
+        parts = tuple(p[:, :own_tokens].reshape(tokens, -1) for p in packets)
+    args = (*packets, *parts, units, pre, own_basis, other_basis, new)
     return pl.pallas_call(
         functools.partial(final_body, own_tokens),
         out_shape=(
@@ -324,28 +307,27 @@
             jax.ShapeDtypeStruct((half, hidden), jnp.float32),
             jax.ShapeDtypeStruct((hidden, width), jnp.float32),
         ),
-        in_specs=[vmem] * len(args) + [hbm] * 2,
+        in_specs=[vmem] * len(args) + [vmem, hbm],
         out_specs=(vmem, hbm, hbm),
         scratch_shapes=[
-            pltpu.VMEM((steps, 2 * tokens, width // steps), jnp.bfloat16),
+            pltpu.VMEM((steps, tokens, width // steps), jnp.bfloat16),
             pltpu.VMEM((steps, half // steps, hidden), jnp.float32),
             pltpu.VMEM((steps, hidden, width // steps), jnp.float32),
-            pltpu.SemaphoreType.DMA((4 * steps,)),
+            pltpu.SemaphoreType.DMA((3 * steps,)),
         ],
         compiler_params=pltpu.CompilerParams(vmem_limit_bytes=44 * MIB),
         cost_estimate=cost(4 * tokens * hidden * width, 4 * (half + width) * hidden),
-    )(*args, in_hbm(own_hidden), in_hbm(other_hidden))
-
-
-def exchange(array, axes="vocab"):
-    return lax.all_to_all(array, axes, 0, 0, tiled=True)
+    )(*args, own_hidden, in_hbm(other_hidden))
+
+
+def exchange(array):
+    return lax.all_to_all(array, "vocab", 0, 0, tiled=True)
 
 
 def shards(hidden_states, targets, old_embed, decomp, counts, w_in, w_out):
     new_rows, k_slots = decomp.shape
     old_rows, width = old_embed.shape
     groups = lax.axis_size("vocab")
-    cores = lax.axis_size("dp")
     own_index = lax.axis_index("vocab")
     dp_index = lax.axis_index("dp")
     tokens = hidden_states.shape[0]
@@ -430,13 +412,14 @@
     packet_rows = (own_tokens + 16) // 16 * 16
     packets = whole_call(
         softmax_body,
-        shaped((groups * cores, packet_rows, columns), jnp.bfloat16),
+        shaped((groups, packet_rows, columns), jnp.bfloat16),
         (shares, own_targets),
     )
-    packets = exchange(packets, ("vocab", "dp")).reshape(groups, cores, packet_rows, columns)
+    packets = exchange(packets)
+    packets_other = lax.ppermute(packets, "dp", swap)
     loss_value, grad_in, grad_out = final_call(
         own_tokens,
-        packets,
+        (packets, packets_other),
         hidden_units,
         pre_units,
         basis,

time: 82.6 us -> 81.8 us (level)
  blocking collectives: 21.8 us -> 19.8 us
  waiting for transfers between devices: 20 us -> 21.3 us
    all_to_all x2, blocking collectives: 21.8 us -> 19.8 us  [exchange(): return lax.all_to_all(array, 'vocab', 0, 0, tiled=True)]
    ppermute x0 -> x1, waiting for transfers between devices: none -> 1.3 us  [shards(): packets_other = lax.ppermute(packets, 'dp', swap)]
  transfers between devices with their start and end apart: 13 -> 14, of which waited for: 6 -> 7; matrix products, arithmetic and copies ran while one was open for 5% -> 5% of each run, Pallas kernels for 5% -> 5%
where the time goes in v6:
time: 81.8 us; the launch traced here: 81.4 us
  starting transfers between devices  22.1 us (27%)
  waiting for transfers between devices  21.3 us (26%)
  blocking collectives  19.8 us (24%)
  Pallas kernels  12.3 us (15%)
  matrix products  4.11 us (5%)
  local copies, waits for them, and re-layouts  0.92 us (1%)
    all_to_all x2, blocking collectives, exchange(): return lax.all_to_all(array, 'vocab', 0, 0, tiled=True)  19.8 us
    all_to_all x2, waiting for transfers between devices, exchange(): return lax.all_to_all(array, 'vocab', 0, 0, tiled=True)  14.5 us
    ppermute x7, starting transfers between devices, shards(): lax.ppermute(new_own, 'vocab', [(i, i ^ k) for i in range(groups)])  11.2 us
    all_to_all x2, starting transfers between devices, exchange(): return lax.all_to_all(array, 'vocab', 0, 0, tiled=True)  10.3 us
    pallas_call x1, Pallas kernels, final_call(): pl.pallas_call(functools.partial(final_body, own_tokens), out_shape=(jax....  6.48 us
    dot_general x1, matrix products, dot(): return lax.dot_general(a, b, dims, preferred_element_type=jnp.float32)  4.11 us
    pallas_call x7, Pallas kernels, whole_call(): pl.pallas_call(body, out_shape=outs, in_specs=[pl.BlockSpec(memory_space=...  2.87 us
    ppermute x7, waiting for transfers between devices, shards(): lax.ppermute(new_own, 'vocab', [(i, i ^ k) for i in range(groups)])  2.48 us
  transfers between devices with their start and end apart: 14, of which 7 were waited for; matrix products, arithmetic and copies ran while one was open for 5% of the time, Pallas kernels for 5%

profile of v6, /device:TPU:0, one launch (start us, length us, event | category | flops | bytes accessed | tf_op | source)
XLA Modules:
  0.0 81.4 jit_solution(12180670384262803320)
XLA Ops:
  0.7 0.8 %copy-done.2 = s32[16,8]{0,1:T(8,128)S(1)} copy-done((s32[16,8]{0,1:T(8,128)S(1)}, s32[16,8]{0,1:T(8,128)}, u32[]{:S(2)}) %copy-start.2) | copy-done | bytes 536
  1.5 0.6 shard_map.94
  2.1 0.5 collective-permute-start.1
  2.6 6.8 %all-to-all-start = ((s32[8,8,128]{2,1,0:T(8,128)}), s32[8,8,128]{2,1,0:T(8,128)S(1)}, u32[]{:S(2)}, u32[]{:S(2)}) async-start(s32[8,8,128]{2,1,0:T(8,128)} %shard_map.94), calls=%async_computation | async-start | bytes 65536 | tf_op jit(solution)/shard_map/all_to_all | solution.py:324
  9.8 6.2 %all-to-all-done.look_ref = s32[8,8,128]{2,1,0:T(8,128)S(1)} async-done(((s32[8,8,128]{2,1,0:T(8,128)}), s32[8,8,128]{2,1,0:T(8,128)S(1)}, u32[]{:S(2)}, u32[]{:S(2)}) %all-to-all-start) | async-done | bytes 32800 | tf_op jit(solution)/shard_map/all_to_all | solution.py:324
  16.1 1.4 %shard_map.96 = bf16[128,2048]{1,0:T(8,128)(2,1)} custom-call(s32[8,8,128]{2,1,0:T(8,128)S(1)} %all-to-all-done.look_ref, bf16[256,2048]{1,0:T(8,128)(2,1)S(1)} %constant_dynamic-slice_fusion.old_ref), custom_call_target="tpu_custom_call" | custom-call | flops 16777216 | bytes 2097152 | tf_op jit(solution)/shard_map/pallas_call | solution.py:122
  17.5 3.5 %all-to-all-start.1 = ((bf16[8,16,2048]{2,1,0:T(8,128)(2,1)}), bf16[8,16,2048]{2,1,0:T(8,128)(2,1)S(1)}, u32[]{:S(2)}, u32[]{:S(2)}) async-start(bf16[8,16,2048]{2,1,0:T(8,128)(2,1)} %bitcast.15), calls=%async_computation.1 | async-start | bytes 1048576 | tf_op jit(solution)/shard_map/all_to_all | solution.py:324
  21.0 4.1 %convolution_convert_fusion.basis_ref.refs_2_ = bf16[256,512]{1,0:T(8,128)(2,1)S(1)} fusion(bf16[256,4096]{1,0:T(8,128)(2,1)} %refs_5_, bf16[512,4096]{1,0:T(8,128)(2,1)} %param.13), kind=kOutput, calls=%fused_computation | convolution fusion | flops 1073872896 | bytes 6553600 | tf_op jit(solution)/shard_map/dot_general | solution.py:21
  25.2 1.5 %collective-permute-done.refs_3_ = bf16[256,512]{1,0:T(8,128)(2,1)S(1)} collective-permute-done((bf16[256,512]{1,0:T(8,128)(2,1)S(1)}, bf16[256,512]{1,0:T(8,128)(2,1)S(1)}, u32[]{:S(2)}, u32[]{:S(2)}) %collective-permute-start) | collective-permute-done | bytes 262176 | tf_op jit(solution)/shard_map/ppermute | solution.py:366
  26.7 8.2 %all-to-all-done.1 = bf16[8,16,2048]{2,1,0:T(8,128)(2,1)S(1)} async-done(((bf16[8,16,2048]{2,1,0:T(8,128)(2,1)}), bf16[8,16,2048]{2,1,0:T(8,128)(2,1)S(1)}, u32[]{:S(2)}, u32[]{:S(2)}) %all-to-all-start.1) | async-done | bytes 524320 | tf_op jit(solution)/shard_map/all_to_all | solution.py:324
  35.2 2.4 %collective-permute-start.8 = (bf16[16,2048]{1,0:T(8,128)(2,1)S(1)}, bf16[16,2048]{1,0:T(8,128)(2,1)S(1)}, u32[]{:S(2)}, u32[]{:S(2)}) collective-permute-start(bf16[16,2048]{1,0:T(8,128)(2,1)S(1)} %shard_map.97.own_ref.refs_0_), channel_id=1, source_target_pairs={{0,14},{2,12},{4,10},{6,8},{8,6},{10,4},{12,2},{14,0},{1,15},{3,13... | collective-permute-start | bytes 196616 | tf_op jit(solution)/shard_map/ppermute | solution.py:377
  37.6 2.3 %collective-permute-start.7 = (bf16[16,2048]{1,0:T(8,128)(2,1)S(1)}, bf16[16,2048]{1,0:T(8,128)(2,1)S(1)}, u32[]{:S(2)}, u32[]{:S(2)}) collective-permute-start(bf16[16,2048]{1,0:T(8,128)(2,1)S(1)} %shard_map.97.own_ref.refs_0_), channel_id=1, source_target_pairs={{0,12},{2,14},{4,8},{6,10},{8,4},{10,6},{12,0},{14,2},{1,13},{3,15... | collective-permute-start | bytes 196616 | tf_op jit(solution)/shard_map/ppermute | solution.py:377
  40.0 3.0 %collective-permute-start.5 = (bf16[16,2048]{1,0:T(8,128)(2,1)S(1)}, bf16[16,2048]{1,0:T(8,128)(2,1)S(1)}, u32[]{:S(2)}, u32[]{:S(2)}) collective-permute-start(bf16[16,2048]{1,0:T(8,128)(2,1)S(1)} %shard_map.97.own_ref.refs_0_), channel_id=1, source_target_pairs={{0,8},{2,10},{4,12},{6,14},{8,0},{10,2},{12,4},{14,6},{1,9},{3,11}... | collective-permute-start | bytes 196616 | tf_op jit(solution)/shard_map/ppermute | solution.py:377
  43.0 3.0 %collective-permute-start.3 = (bf16[16,2048]{1,0:T(8,128)(2,1)S(1)}, bf16[16,2048]{1,0:T(8,128)(2,1)S(1)}, u32[]{:S(2)}, u32[]{:S(2)}) collective-permute-start(bf16[16,2048]{1,0:T(8,128)(2,1)S(1)} %shard_map.97.own_ref.refs_0_), channel_id=1, source_target_pairs={{0,4},{2,6},{4,0},{6,2},{8,12},{10,14},{12,8},{14,10},{1,5},{3,7},... | collective-permute-start | bytes 196616 | tf_op jit(solution)/shard_map/ppermute | solution.py:377
  46.4 1.6 %shard_map.99.refs_8_ = bf16[2048,512]{1,0:T(8,128)(2,1)S(1)} custom-call(bf16[2048,512]{1,0:T(8,128)(2,1)} %source_ref.1), custom_call_target="tpu_custom_call" | custom-call | bytes 2097152 | tf_op jit(solution)/shard_map/pallas_call | solution.py:169
  48.0 0.7 shard_map.98.direct_ref
  48.8 1.0 %collective-permute-done.6.refs_5_ = bf16[16,2048]{1,0:T(8,128)(2,1)S(1)} collective-permute-done((bf16[16,2048]{1,0:T(8,128)(2,1)S(1)}, bf16[16,2048]{1,0:T(8,128)(2,1)S(1)}, u32[]{:S(2)}, u32[]{:S(2)}) %collective-permute-start.6) | collective-permute-done | bytes 65568 | tf_op jit(solution)/shard_map/ppermute | solution.py:377
  49.8 1.5 %collective-permute-done.3.refs_2_ = bf16[16,2048]{1,0:T(8,128)(2,1)S(1)} collective-permute-done((bf16[16,2048]{1,0:T(8,128)(2,1)S(1)}, bf16[16,2048]{1,0:T(8,128)(2,1)S(1)}, u32[]{:S(2)}, u32[]{:S(2)}) %collective-permute-start.3) | collective-permute-done | bytes 65568 | tf_op jit(solution)/shard_map/ppermute | solution.py:377
  51.2 0.5 shard_map.100
  51.8 1.5 %collective-permute-done.10.pre_other_ref = f32[128,512]{1,0:T(8,128)S(1)} collective-permute-done((f32[128,512]{1,0:T(8,128)S(1)}, f32[128,512]{1,0:T(8,128)S(1)}, u32[]{:S(2)}, u32[]{:S(2)}) %collective-permute-start.10) | collective-permute-done | bytes 262176 | tf_op jit(solution)/shard_map/ppermute | solution.py:400
  53.6 10.3 %all_to_all.20.shares_ref = f32[8,32,128]{2,1,0:T(8,128)S(1)} all-to-all(f32[8,32,128]{2,1,0:T(8,128)S(1)} %bitcast.10), channel_id=1, replica_groups=mesh['groups'=2,'vocab'=8,'dp'=2] {'vocab'}, dimensions={0} | all-to-all | bytes 262144 | tf_op jit(solution)/shard_map/all_to_all | solution.py:324
  64.1 9.6 %all_to_all.21.own_packets_ref = bf16[8,48,128]{2,1,0:T(8,128)(2,1)S(1)} all-to-all(bf16[8,48,128]{2,1,0:T(8,128)(2,1)S(1)} %shard_map.102), channel_id=1, replica_groups=mesh['groups'=2,'vocab'=8,'dp'=2] {'vocab'}, dimensions={0} | all-to-all | bytes 196608 | tf_op jit(solution)/shard_map/all_to_all | solution.py:324
  73.6 1.3 %collective-permute-done.11.other_packets_ref = bf16[8,48,128]{2,1,0:T(8,128)(2,1)S(1)} collective-permute-done((bf16[8,48,128]{2,1,0:T(8,128)(2,1)S(1)}, bf16[8,48,128]{2,1,0:T(8,128)(2,1)S(1)}, u32[]{:S(2)}, u32[]{:S(2)}) %collective-permute-start.11) | collective-permute-done | bytes 98336 | tf_op jit(solution)/shard_map/ppermute | solution.py:419
  74.9 6.5 %shard_map.103 = (f32[1,1]{1,0:T(1,128)}, f32[2048,512]{1,0:T(8,128)}, f32[512,4096]{1,0:T(8,128)}) custom-call(bf16[8,48,128]{2,1,0:T(8,128)(2,1)S(1)} %all_to_all.21.own_packets_ref, bf16[8,48,128]{2,1,0:T(8,128)(2,1)S(1)} %collective-permute-done.11.other_packets_ref, bf16[128,512]{1,0:T(8,128)(2,1)S(1)} %get-tuple-element.57.refs_0_, ...), custom_call_target="tpu_custom_call" | custom-call | flops 2147483648 | bytes 12582912 | tf_op jit(solution)/shard_map/pallas_call | solution.py:303
  (30 shorter events, 1.8 us)
Async XLA Ops:
  0.6 8.7 %copy-start = (bf16[256,4096]{1,0:T(8,128)(2,1)S(1)}, bf16[256,4096]{1,0:T(8,128)(2,1)}, u32[]{:S(2)}) copy-start(bf16[256,4096]{1,0:T(8,128)(2,1)} %param.9) | copy-start | bytes 6291460
  0.6 8.8 %copy-start.5 = (s32[16]{0:T(128)S(1)}, s32[16]{0:T(128)}, u32[]{:S(2)}) copy-start(s32[16]{0:T(128)} %param.11) | copy-start | bytes 196
  0.7 8.8 %copy-start.4 = (s32[256]{0:T(256)S(1)}, s32[256]{0:T(256)}, u32[]{:S(2)}) copy-start(s32[256]{0:T(256)} %param.8) | copy-start | bytes 3076
  0.7 0.8 %copy-start.2 = (s32[16,8]{0,1:T(8,128)S(1)}, s32[16,8]{0,1:T(8,128)}, u32[]{:S(2)}) copy-start(s32[16,8]{0,1:T(8,128)} %param.10) | copy-start | bytes 1540
  1.5 8.0 %copy-start.3 = (s32[16,8]{0,1:T(8,128)S(1)}, s32[16,8]{0,1:T(8,128)}, u32[]{:S(2)}) copy-start(s32[16,8]{0,1:T(8,128)} %param.10) | copy-start | bytes 1540
  2.1 32.8 %collective-permute-start.1 = (bf16[256,4096]{1,0:T(8,128)(2,1)}, bf16[256,4096]{1,0:T(8,128)(2,1)}, u32[]{:S(2)}, u32[]{:S(2)}) collective-permute-start(bf16[256,4096]{1,0:T(8,128)(2,1)} %refs_5_), channel_id=1, source_target_pairs={{0,1},{1,0},{2,3},{3,2},{4,5},{5,4},{6,7},{7,6},{8,9},{9,8},{10,11... | collective-permute-start | bytes 6291464 | tf_op jit(solution)/shard_map/ppermute | solution.py:347
  2.6 13.5 %all-to-all-start = ((s32[8,8,128]{2,1,0:T(8,128)}), s32[8,8,128]{2,1,0:T(8,128)S(1)}, u32[]{:S(2)}, u32[]{:S(2)}) async-start(s32[8,8,128]{2,1,0:T(8,128)} %shard_map.94), calls=%async_computation | async-start | bytes 65536 | tf_op jit(solution)/shard_map/all_to_all | solution.py:324
  17.5 17.5 %all-to-all-start.1 = ((bf16[8,16,2048]{2,1,0:T(8,128)(2,1)}), bf16[8,16,2048]{2,1,0:T(8,128)(2,1)S(1)}, u32[]{:S(2)}, u32[]{:S(2)}) async-start(bf16[8,16,2048]{2,1,0:T(8,128)(2,1)} %bitcast.15), calls=%async_computation.1 | async-start | bytes 1048576 | tf_op jit(solution)/shard_map/all_to_all | solution.py:324
  25.1 1.6 %collective-permute-start = (bf16[256,512]{1,0:T(8,128)(2,1)S(1)}, bf16[256,512]{1,0:T(8,128)(2,1)S(1)}, u32[]{:S(2)}, u32[]{:S(2)}) collective-permute-start(bf16[256,512]{1,0:T(8,128)(2,1)S(1)} %convolution_convert_fusion.basis_ref.refs_2_), channel_id=1, source_target_pairs={{0,1},{1,0},{2,3},{3,2},{4,5},{5,4},{6,7},{7,6},{8,9},{9,8},{10,11... | collective-permute-start | bytes 786440 | tf_op jit(solution)/shard_map/ppermute | solution.py:366
  35.1 12.9 %copy-start.1 = (bf16[256,4096]{1,0:T(8,128)(2,1)S(1)}, bf16[256,4096]{1,0:T(8,128)(2,1)}, u32[]{:S(2)}) copy-start(bf16[256,4096]{1,0:T(8,128)(2,1)} %refs_5_) | copy-start | bytes 6291460
  35.1 7.8 %collective-permute-start.9 = (bf16[16,2048]{1,0:T(8,128)(2,1)S(1)}, bf16[16,2048]{1,0:T(8,128)(2,1)S(1)}, u32[]{:S(2)}, u32[]{:S(2)}) collective-permute-start(bf16[16,2048]{1,0:T(8,128)(2,1)S(1)} %shard_map.97.own_ref.refs_0_), channel_id=1, source_target_pairs={{0,1},{1,0},{2,3},{3,2},{4,5},{5,4},{6,7},{7,6},{8,9},{9,8},{10,11... | collective-permute-start | bytes 196616 | tf_op jit(solution)/shard_map/ppermute | solution.py:383
  35.2 7.8 %collective-permute-start.8 = (bf16[16,2048]{1,0:T(8,128)(2,1)S(1)}, bf16[16,2048]{1,0:T(8,128)(2,1)S(1)}, u32[]{:S(2)}, u32[]{:S(2)}) collective-permute-start(bf16[16,2048]{1,0:T(8,128)(2,1)S(1)} %shard_map.97.own_ref.refs_0_), channel_id=1, source_target_pairs={{0,14},{2,12},{4,10},{6,8},{8,6},{10,4},{12,2},{14,0},{1,15},{3,13... | collective-permute-start | bytes 196616 | tf_op jit(solution)/shard_map/ppermute | solution.py:377
  37.6 8.4 %collective-permute-start.7 = (bf16[16,2048]{1,0:T(8,128)(2,1)S(1)}, bf16[16,2048]{1,0:T(8,128)(2,1)S(1)}, u32[]{:S(2)}, u32[]{:S(2)}) collective-permute-start(bf16[16,2048]{1,0:T(8,128)(2,1)S(1)} %shard_map.97.own_ref.refs_0_), channel_id=1, source_target_pairs={{0,12},{2,14},{4,8},{6,10},{8,4},{10,6},{12,0},{14,2},{1,13},{3,15... | collective-permute-start | bytes 196616 | tf_op jit(solution)/shard_map/ppermute | solution.py:377
  40.0 9.8 %collective-permute-start.6 = (bf16[16,2048]{1,0:T(8,128)(2,1)S(1)}, bf16[16,2048]{1,0:T(8,128)(2,1)S(1)}, u32[]{:S(2)}, u32[]{:S(2)}) collective-permute-start(bf16[16,2048]{1,0:T(8,128)(2,1)S(1)} %shard_map.97.own_ref.refs_0_), channel_id=1, source_target_pairs={{0,10},{2,8},{4,14},{6,12},{8,2},{10,0},{12,6},{14,4},{1,11},{3,9}... | collective-permute-start | bytes 196616 | tf_op jit(solution)/shard_map/ppermute | solution.py:377
  40.0 9.8 %collective-permute-start.5 = (bf16[16,2048]{1,0:T(8,128)(2,1)S(1)}, bf16[16,2048]{1,0:T(8,128)(2,1)S(1)}, u32[]{:S(2)}, u32[]{:S(2)}) collective-permute-start(bf16[16,2048]{1,0:T(8,128)(2,1)S(1)} %shard_map.97.own_ref.refs_0_), channel_id=1, source_target_pairs={{0,8},{2,10},{4,12},{6,14},{8,0},{10,2},{12,4},{14,6},{1,9},{3,11}... | collective-permute-start | bytes 196616 | tf_op jit(solution)/shard_map/ppermute | solution.py:377
  42.9 6.8 %collective-permute-start.4 = (bf16[16,2048]{1,0:T(8,128)(2,1)S(1)}, bf16[16,2048]{1,0:T(8,128)(2,1)S(1)}, u32[]{:S(2)}, u32[]{:S(2)}) collective-permute-start(bf16[16,2048]{1,0:T(8,128)(2,1)S(1)} %shard_map.97.own_ref.refs_0_), channel_id=1, source_target_pairs={{0,6},{2,4},{4,2},{6,0},{8,14},{10,12},{12,10},{14,8},{1,7},{3,5},... | collective-permute-start | bytes 196616 | tf_op jit(solution)/shard_map/ppermute | solution.py:377
  43.0 8.3 %collective-permute-start.3 = (bf16[16,2048]{1,0:T(8,128)(2,1)S(1)}, bf16[16,2048]{1,0:T(8,128)(2,1)S(1)}, u32[]{:S(2)}, u32[]{:S(2)}) collective-permute-start(bf16[16,2048]{1,0:T(8,128)(2,1)S(1)} %shard_map.97.own_ref.refs_0_), channel_id=1, source_target_pairs={{0,4},{2,6},{4,0},{6,2},{8,12},{10,14},{12,8},{14,10},{1,5},{3,7},... | collective-permute-start | bytes 196616 | tf_op jit(solution)/shard_map/ppermute | solution.py:377
  46.0 5.2 %collective-permute-start.2 = (bf16[16,2048]{1,0:T(8,128)(2,1)S(1)}, bf16[16,2048]{1,0:T(8,128)(2,1)S(1)}, u32[]{:S(2)}, u32[]{:S(2)}) collective-permute-start(bf16[16,2048]{1,0:T(8,128)(2,1)S(1)} %shard_map.97.own_ref.refs_0_), channel_id=1, source_target_pairs={{0,2},{2,0},{4,6},{6,4},{8,10},{10,8},{12,14},{14,12},{1,3},{3,1},... | collective-permute-start | bytes 196616 | tf_op jit(solution)/shard_map/ppermute | solution.py:377
  51.7 1.6 %collective-permute-start.10 = (f32[128,512]{1,0:T(8,128)S(1)}, f32[128,512]{1,0:T(8,128)S(1)}, u32[]{:S(2)}, u32[]{:S(2)}) collective-permute-start(f32[128,512]{1,0:T(8,128)S(1)} %get-tuple-element.52.pre_own_ref), channel_id=1, source_target_pairs={{0,1},{1,0},{2,3},{3,2},{4,5},{5,4},{6,7},{7,6},{8,9},{9,8},{10,11... | collective-permute-start | bytes 786440 | tf_op jit(solution)/shard_map/ppermute | solution.py:400
  73.6 1.3 %collective-permute-start.11 = (bf16[8,48,128]{2,1,0:T(8,128)(2,1)S(1)}, bf16[8,48,128]{2,1,0:T(8,128)(2,1)S(1)}, u32[]{:S(2)}, u32[]{:S(2)}) collective-permute-start(bf16[8,48,128]{2,1,0:T(8,128)(2,1)S(1)} %all_to_all.21.own_packets_ref), channel_id=1, source_target_pairs={{0,1},{1,0},{2,3},{3,2},{4,5},{5,4},{6,7},{7,6},{8,9},{9,8},{10,11... | collective-permute-start | bytes 294920 | tf_op jit(solution)/shard_map/ppermute | solution.py:419

commit v7 on v6

--- a/solution.py
+++ b/solution.py
@@ -372,11 +372,12 @@
         add_body, shaped((new_rows, half_width), jnp.bfloat16), (adder, arrived, scale)
     )
     if groups in (2, 4, 8):
-        steps = range(groups - 1, 0, -1)
-        blocks = [
-            lax.ppermute(new_own, "vocab", [(i, i ^ k) for i in range(groups)]) for k in steps
-        ]
-        blocks = [new_own] + blocks[::-1]
+        got = {}
+        for k in (4, 6, 2, 3, 1):
+            got[k] = lax.ppermute(new_own, "vocab", [(i, i ^ k) for i in range(groups)])
+        for k in (5, 7):
+            got[k] = lax.ppermute(got[k ^ 1], "vocab", [(i, i ^ 1) for i in range(groups)])
+        blocks = [new_own] + [got[k] for k in range(1, groups)]
     else:
         copies = jnp.broadcast_to(new_own[None], (groups, new_rows, half_width))
         blocks = [exchange(copies).reshape(columns, half_width)]
@@ -386,8 +387,7 @@
         shaped((tokens, columns), jnp.float32),
         (hidden_states, new_own, new_other),
     )
-    w_held = held(w_in)
-    blocks, direct, w_held = lax.optimization_barrier((blocks, direct, w_held))
+    blocks, direct = lax.optimization_barrier((blocks, direct))
 
     new_all, pre_own = whole_call(
         functools.partial(pre_body, len(blocks)),
@@ -395,7 +395,7 @@
             shaped((columns, half_width), jnp.bfloat16),
             shaped((columns, hidden), jnp.float32),
         ),
-        (*blocks, w_held),
+        (*blocks, w_in),
     )
     pre_other = lax.ppermute(pre_own, "dp", swap)
     pre_units, hidden_units, share = whole_call(

time: 81.8 us -> 79.8 us (0.976)
  starting transfers between devices: 22.1 us -> 19.7 us
  Pallas kernels: 12.3 us -> 10.7 us
  local copies, waits for them, and re-layouts: 0.92 us -> 2.52 us
    ppermute x7, starting transfers between devices: 11.2 us -> 8.78 us  [the longest x5 5.92 us: shards(): got[k] = lax.ppermute(new_own, 'vocab', [(i, i ^ k) for i in range(groups)])]
    pallas_call x1 -> x0, Pallas kernels: 1.6 us -> none  [held(): pl.pallas_call(copy_body, out_shape=pltpu.VMEM(array.shape, array.dtype),...]
    unnamed x12 -> x16, local copies, waits for them, and re-layouts: 0.85 us -> 2.45 us
  transfers between devices with their start and end apart: 14 -> 14, of which waited for: 7 -> 8; matrix products, arithmetic and copies ran while one was open for 5% -> 5% of each run, Pallas kernels for 5% -> 3%
where the time goes in v7:
time: 79.8 us; the launch traced here: 79.4 us
  waiting for transfers between devices  21.1 us (26%)
  blocking collectives  20.3 us (25%)
  starting transfers between devices  19.7 us (25%)
  Pallas kernels  10.7 us (13%)
  matrix products  4.11 us (5%)
  local copies, waits for them, and re-layouts  2.52 us (3%)
  between operations  0.82 us (1%)
    all_to_all x2, blocking collectives, exchange(): return lax.all_to_all(array, 'vocab', 0, 0, tiled=True)  20.3 us
    all_to_all x2, waiting for transfers between devices, exchange(): return lax.all_to_all(array, 'vocab', 0, 0, tiled=True)  14.5 us
    all_to_all x2, starting transfers between devices, exchange(): return lax.all_to_all(array, 'vocab', 0, 0, tiled=True)  10.3 us
    pallas_call x1, Pallas kernels, final_call(): pl.pallas_call(functools.partial(final_body, own_tokens), out_shape=(jax....  6.48 us
    ppermute x5, starting transfers between devices, shards(): got[k] = lax.ppermute(new_own, 'vocab', [(i, i ^ k) for i in range(groups)])  5.92 us
    dot_general x1, matrix products, dot(): return lax.dot_general(a, b, dims, preferred_element_type=jnp.float32)  4.11 us
    pallas_call x7, Pallas kernels, whole_call(): pl.pallas_call(body, out_shape=outs, in_specs=[pl.BlockSpec(memory_space=...  2.86 us
    ppermute x2, starting transfers between devices, shards(): lax.ppermute(got[k ^ 1], 'vocab', [(i, i ^ 1) for i in range(groups)])  2.86 us
  transfers between devices with their start and end apart: 14, of which 8 were waited for; matrix products, arithmetic and copies ran while one was open for 5% of the time, Pallas kernels for 3%

profile of v7, /device:TPU:0, one launch (start us, length us, event | category | flops | bytes accessed | tf_op | source)
XLA Modules:
  0.0 79.4 jit_solution(7350232675990664214)
XLA Ops:
  0.7 0.8 %copy-done.4 = s32[16,8]{0,1:T(8,128)S(1)} copy-done((s32[16,8]{0,1:T(8,128)S(1)}, s32[16,8]{0,1:T(8,128)}, u32[]{:S(2)}) %copy-start.4) | copy-done | bytes 536
  1.5 0.6 shard_map.94
  2.6 6.8 %all-to-all-start = ((s32[8,8,128]{2,1,0:T(8,128)}), s32[8,8,128]{2,1,0:T(8,128)S(1)}, u32[]{:S(2)}, u32[]{:S(2)}) async-start(s32[8,8,128]{2,1,0:T(8,128)} %shard_map.94), calls=%async_computation | async-start | bytes 65536 | tf_op jit(solution)/shard_map/all_to_all | solution.py:324
  9.8 6.2 %all-to-all-done.look_ref = s32[8,8,128]{2,1,0:T(8,128)S(1)} async-done(((s32[8,8,128]{2,1,0:T(8,128)}), s32[8,8,128]{2,1,0:T(8,128)S(1)}, u32[]{:S(2)}, u32[]{:S(2)}) %all-to-all-start) | async-done | bytes 32800 | tf_op jit(solution)/shard_map/all_to_all | solution.py:324
  16.1 1.4 %shard_map.96 = bf16[128,2048]{1,0:T(8,128)(2,1)} custom-call(s32[8,8,128]{2,1,0:T(8,128)S(1)} %all-to-all-done.look_ref, bf16[256,2048]{1,0:T(8,128)(2,1)S(1)} %constant_dynamic-slice_fusion.old_ref), custom_call_target="tpu_custom_call" | custom-call | flops 16777216 | bytes 2097152 | tf_op jit(solution)/shard_map/pallas_call | solution.py:122
  17.5 3.5 %all-to-all-start.1 = ((bf16[8,16,2048]{2,1,0:T(8,128)(2,1)}), bf16[8,16,2048]{2,1,0:T(8,128)(2,1)S(1)}, u32[]{:S(2)}, u32[]{:S(2)}) async-start(bf16[8,16,2048]{2,1,0:T(8,128)(2,1)} %bitcast.15), calls=%async_computation.1 | async-start | bytes 1048576 | tf_op jit(solution)/shard_map/all_to_all | solution.py:324
  21.0 4.1 %convolution_convert_fusion.basis_ref.refs_2_ = bf16[256,512]{1,0:T(8,128)(2,1)S(1)} fusion(bf16[256,4096]{1,0:T(8,128)(2,1)} %refs_5_, bf16[512,4096]{1,0:T(8,128)(2,1)} %param.13), kind=kOutput, calls=%fused_computation | convolution fusion | flops 1073872896 | bytes 6553600 | tf_op jit(solution)/shard_map/dot_general | solution.py:21
  25.2 1.5 %collective-permute-done.refs_3_ = bf16[256,512]{1,0:T(8,128)(2,1)S(1)} collective-permute-done((bf16[256,512]{1,0:T(8,128)(2,1)S(1)}, bf16[256,512]{1,0:T(8,128)(2,1)S(1)}, u32[]{:S(2)}, u32[]{:S(2)}) %collective-permute-start) | collective-permute-done | bytes 262176 | tf_op jit(solution)/shard_map/ppermute | solution.py:366
  26.7 8.2 %all-to-all-done.1 = bf16[8,16,2048]{2,1,0:T(8,128)(2,1)S(1)} async-done(((bf16[8,16,2048]{2,1,0:T(8,128)(2,1)}), bf16[8,16,2048]{2,1,0:T(8,128)(2,1)S(1)}, u32[]{:S(2)}, u32[]{:S(2)}) %all-to-all-start.1) | async-done | bytes 524320 | tf_op jit(solution)/shard_map/all_to_all | solution.py:324
  35.2 1.2 %collective-permute-start.7 = (bf16[16,2048]{1,0:T(8,128)(2,1)S(1)}, bf16[16,2048]{1,0:T(8,128)(2,1)S(1)}, u32[]{:S(2)}, u32[]{:S(2)}) collective-permute-start(bf16[16,2048]{1,0:T(8,128)(2,1)S(1)} %shard_map.97.own_ref.refs_0_), channel_id=1, source_target_pairs={{0,12},{2,14},{4,8},{6,10},{8,4},{10,6},{12,0},{14,2},{1,13},{3,15... | collective-permute-start | bytes 196616 | tf_op jit(solution)/shard_map/ppermute | solution.py:377
  36.4 1.0 %collective-permute-start.5 = (bf16[16,2048]{1,0:T(8,128)(2,1)S(1)}, bf16[16,2048]{1,0:T(8,128)(2,1)S(1)}, u32[]{:S(2)}, u32[]{:S(2)}) collective-permute-start(bf16[16,2048]{1,0:T(8,128)(2,1)S(1)} %shard_map.97.own_ref.refs_0_), channel_id=1, source_target_pairs={{0,8},{2,10},{4,12},{6,14},{8,0},{10,2},{12,4},{14,6},{1,9},{3,11}... | collective-permute-start | bytes 196616 | tf_op jit(solution)/shard_map/ppermute | solution.py:377
  37.4 3.1 %collective-permute-start.4 = (bf16[16,2048]{1,0:T(8,128)(2,1)S(1)}, bf16[16,2048]{1,0:T(8,128)(2,1)S(1)}, u32[]{:S(2)}, u32[]{:S(2)}) collective-permute-start(bf16[16,2048]{1,0:T(8,128)(2,1)S(1)} %shard_map.97.own_ref.refs_0_), channel_id=1, source_target_pairs={{0,6},{2,4},{4,2},{6,0},{8,14},{10,12},{12,10},{14,8},{1,7},{3,5},... | collective-permute-start | bytes 196616 | tf_op jit(solution)/shard_map/ppermute | solution.py:377
  40.5 0.6 collective-permute-start.2
  41.1 0.9 %collective-permute-done.7.refs_6_ = bf16[16,2048]{1,0:T(8,128)(2,1)S(1)} collective-permute-done((bf16[16,2048]{1,0:T(8,128)(2,1)S(1)}, bf16[16,2048]{1,0:T(8,128)(2,1)S(1)}, u32[]{:S(2)}, u32[]{:S(2)}) %collective-permute-start.7) | collective-permute-done | bytes 65568 | tf_op jit(solution)/shard_map/ppermute | solution.py:377
  42.0 1.4 %collective-permute-start.8 = (bf16[16,2048]{1,0:T(8,128)(2,1)S(1)}, bf16[16,2048]{1,0:T(8,128)(2,1)S(1)}, u32[]{:S(2)}, u32[]{:S(2)}) collective-permute-start(bf16[16,2048]{1,0:T(8,128)(2,1)S(1)} %collective-permute-done.7.refs_6_), channel_id=1, source_target_pairs={{0,2},{2,0},{4,6},{6,4},{8,10},{10,8},{12,14},{14,12},{1,3},{3,1},... | collective-permute-start | bytes 196616 | tf_op jit(solution)/shard_map/ppermute | solution.py:379
  43.5 0.9 %collective-permute-done.5.refs_4_ = bf16[16,2048]{1,0:T(8,128)(2,1)S(1)} collective-permute-done((bf16[16,2048]{1,0:T(8,128)(2,1)S(1)}, bf16[16,2048]{1,0:T(8,128)(2,1)S(1)}, u32[]{:S(2)}, u32[]{:S(2)}) %collective-permute-start.5) | collective-permute-done | bytes 65568 | tf_op jit(solution)/shard_map/ppermute | solution.py:377
  44.4 1.4 %collective-permute-start.6 = (bf16[16,2048]{1,0:T(8,128)(2,1)S(1)}, bf16[16,2048]{1,0:T(8,128)(2,1)S(1)}, u32[]{:S(2)}, u32[]{:S(2)}) collective-permute-start(bf16[16,2048]{1,0:T(8,128)(2,1)S(1)} %collective-permute-done.5.refs_4_), channel_id=1, source_target_pairs={{0,2},{2,0},{4,6},{6,4},{8,10},{10,8},{12,14},{14,12},{1,3},{3,1},... | collective-permute-start | bytes 196616 | tf_op jit(solution)/shard_map/ppermute | solution.py:379
  45.8 1.6 %copy-done.2 = bf16[256,4096]{1,0:T(8,128)(2,1)S(1)} copy-done((bf16[256,4096]{1,0:T(8,128)(2,1)S(1)}, bf16[256,4096]{1,0:T(8,128)(2,1)}, u32[]{:S(2)}) %copy-start.2) | copy-done | bytes 2097176
  47.4 0.7 shard_map.98.direct_ref
  49.2 1.5 %collective-permute-done.10.pre_other_ref = f32[128,512]{1,0:T(8,128)S(1)} collective-permute-done((f32[128,512]{1,0:T(8,128)S(1)}, f32[128,512]{1,0:T(8,128)S(1)}, u32[]{:S(2)}, u32[]{:S(2)}) %collective-permute-start.10) | collective-permute-done | bytes 262176 | tf_op jit(solution)/shard_map/ppermute | solution.py:400
  51.0 10.8 %all_to_all.20.shares_ref = f32[8,32,128]{2,1,0:T(8,128)S(1)} all-to-all(f32[8,32,128]{2,1,0:T(8,128)S(1)} %bitcast.10), channel_id=1, replica_groups=mesh['groups'=2,'vocab'=8,'dp'=2] {'vocab'}, dimensions={0} | all-to-all | bytes 262144 | tf_op jit(solution)/shard_map/all_to_all | solution.py:324
  62.0 9.6 %all_to_all.21.own_packets_ref = bf16[8,48,128]{2,1,0:T(8,128)(2,1)S(1)} all-to-all(bf16[8,48,128]{2,1,0:T(8,128)(2,1)S(1)} %shard_map.101), channel_id=1, replica_groups=mesh['groups'=2,'vocab'=8,'dp'=2] {'vocab'}, dimensions={0} | all-to-all | bytes 196608 | tf_op jit(solution)/shard_map/all_to_all | solution.py:324
  71.6 1.3 %collective-permute-done.11.other_packets_ref = bf16[8,48,128]{2,1,0:T(8,128)(2,1)S(1)} collective-permute-done((bf16[8,48,128]{2,1,0:T(8,128)(2,1)S(1)}, bf16[8,48,128]{2,1,0:T(8,128)(2,1)S(1)}, u32[]{:S(2)}, u32[]{:S(2)}) %collective-permute-start.11) | collective-permute-done | bytes 98336 | tf_op jit(solution)/shard_map/ppermute | solution.py:419
  72.9 6.5 %shard_map.102 = (f32[1,1]{1,0:T(1,128)}, f32[2048,512]{1,0:T(8,128)}, f32[512,4096]{1,0:T(8,128)}) custom-call(bf16[8,48,128]{2,1,0:T(8,128)(2,1)S(1)} %all_to_all.21.own_packets_ref, bf16[8,48,128]{2,1,0:T(8,128)(2,1)S(1)} %collective-permute-done.11.other_packets_ref, bf16[128,512]{1,0:T(8,128)(2,1)S(1)} %get-tuple-element.55.refs_0_, ...), custom_call_target="tpu_custom_call" | custom-call | flops 2147483648 | bytes 12582912 | tf_op jit(solution)/shard_map/pallas_call | solution.py:303
  (33 shorter events, 2.7 us)
Async XLA Ops:
  0.6 8.7 %copy-start = (bf16[256,4096]{1,0:T(8,128)(2,1)S(1)}, bf16[256,4096]{1,0:T(8,128)(2,1)}, u32[]{:S(2)}) copy-start(bf16[256,4096]{1,0:T(8,128)(2,1)} %param.9) | copy-start | bytes 6291460
  0.6 8.8 %copy-start.7 = (s32[16]{0:T(128)S(1)}, s32[16]{0:T(128)}, u32[]{:S(2)}) copy-start(s32[16]{0:T(128)} %param.11) | copy-start | bytes 196
  0.7 8.8 %copy-start.6 = (s32[256]{0:T(256)S(1)}, s32[256]{0:T(256)}, u32[]{:S(2)}) copy-start(s32[256]{0:T(256)} %param.8) | copy-start | bytes 3076
  0.7 0.8 %copy-start.4 = (s32[16,8]{0,1:T(8,128)S(1)}, s32[16,8]{0,1:T(8,128)}, u32[]{:S(2)}) copy-start(s32[16,8]{0,1:T(8,128)} %param.10) | copy-start | bytes 1540
  1.5 8.0 %copy-start.5 = (s32[16,8]{0,1:T(8,128)S(1)}, s32[16,8]{0,1:T(8,128)}, u32[]{:S(2)}) copy-start(s32[16,8]{0,1:T(8,128)} %param.10) | copy-start | bytes 1540
  2.1 32.8 %collective-permute-start.1 = (bf16[256,4096]{1,0:T(8,128)(2,1)}, bf16[256,4096]{1,0:T(8,128)(2,1)}, u32[]{:S(2)}, u32[]{:S(2)}) collective-permute-start(bf16[256,4096]{1,0:T(8,128)(2,1)} %refs_5_), channel_id=1, source_target_pairs={{0,1},{1,0},{2,3},{3,2},{4,5},{5,4},{6,7},{7,6},{8,9},{9,8},{10,11... | collective-permute-start | bytes 6291464 | tf_op jit(solution)/shard_map/ppermute | solution.py:347
  2.6 13.5 %all-to-all-start = ((s32[8,8,128]{2,1,0:T(8,128)}), s32[8,8,128]{2,1,0:T(8,128)S(1)}, u32[]{:S(2)}, u32[]{:S(2)}) async-start(s32[8,8,128]{2,1,0:T(8,128)} %shard_map.94), calls=%async_computation | async-start | bytes 65536 | tf_op jit(solution)/shard_map/all_to_all | solution.py:324
  17.5 17.5 %all-to-all-start.1 = ((bf16[8,16,2048]{2,1,0:T(8,128)(2,1)}), bf16[8,16,2048]{2,1,0:T(8,128)(2,1)S(1)}, u32[]{:S(2)}, u32[]{:S(2)}) async-start(bf16[8,16,2048]{2,1,0:T(8,128)(2,1)} %bitcast.15), calls=%async_computation.1 | async-start | bytes 1048576 | tf_op jit(solution)/shard_map/all_to_all | solution.py:324
  25.1 1.6 %collective-permute-start = (bf16[256,512]{1,0:T(8,128)(2,1)S(1)}, bf16[256,512]{1,0:T(8,128)(2,1)S(1)}, u32[]{:S(2)}, u32[]{:S(2)}) collective-permute-start(bf16[256,512]{1,0:T(8,128)(2,1)S(1)} %convolution_convert_fusion.basis_ref.refs_2_), channel_id=1, source_target_pairs={{0,1},{1,0},{2,3},{3,2},{4,5},{5,4},{6,7},{7,6},{8,9},{9,8},{10,11... | collective-permute-start | bytes 786440 | tf_op jit(solution)/shard_map/ppermute | solution.py:366
  34.9 13.7 %copy-start.1 = (bf16[2048,512]{1,0:T(8,128)(2,1)S(1)}, bf16[2048,512]{1,0:T(8,128)(2,1)}, u32[]{:S(2)}) copy-start(bf16[2048,512]{1,0:T(8,128)(2,1)} %refs_8_.1) | copy-start | bytes 6291460
  35.1 5.4 %collective-permute-start.9 = (bf16[16,2048]{1,0:T(8,128)(2,1)S(1)}, bf16[16,2048]{1,0:T(8,128)(2,1)S(1)}, u32[]{:S(2)}, u32[]{:S(2)}) collective-permute-start(bf16[16,2048]{1,0:T(8,128)(2,1)S(1)} %shard_map.97.own_ref.refs_0_), channel_id=1, source_target_pairs={{0,1},{1,0},{2,3},{3,2},{4,5},{5,4},{6,7},{7,6},{8,9},{9,8},{10,11... | collective-permute-start | bytes 196616 | tf_op jit(solution)/shard_map/ppermute | solution.py:384
  35.2 6.9 %collective-permute-start.7 = (bf16[16,2048]{1,0:T(8,128)(2,1)S(1)}, bf16[16,2048]{1,0:T(8,128)(2,1)S(1)}, u32[]{:S(2)}, u32[]{:S(2)}) collective-permute-start(bf16[16,2048]{1,0:T(8,128)(2,1)S(1)} %shard_map.97.own_ref.refs_0_), channel_id=1, source_target_pairs={{0,12},{2,14},{4,8},{6,10},{8,4},{10,6},{12,0},{14,2},{1,13},{3,15... | collective-permute-start | bytes 196616 | tf_op jit(solution)/shard_map/ppermute | solution.py:377
  36.4 8.0 %collective-permute-start.5 = (bf16[16,2048]{1,0:T(8,128)(2,1)S(1)}, bf16[16,2048]{1,0:T(8,128)(2,1)S(1)}, u32[]{:S(2)}, u32[]{:S(2)}) collective-permute-start(bf16[16,2048]{1,0:T(8,128)(2,1)S(1)} %shard_map.97.own_ref.refs_0_), channel_id=1, source_target_pairs={{0,8},{2,10},{4,12},{6,14},{8,0},{10,2},{12,4},{14,6},{1,9},{3,11}... | collective-permute-start | bytes 196616 | tf_op jit(solution)/shard_map/ppermute | solution.py:377
  37.4 10.7 %collective-permute-start.4 = (bf16[16,2048]{1,0:T(8,128)(2,1)S(1)}, bf16[16,2048]{1,0:T(8,128)(2,1)S(1)}, u32[]{:S(2)}, u32[]{:S(2)}) collective-permute-start(bf16[16,2048]{1,0:T(8,128)(2,1)S(1)} %shard_map.97.own_ref.refs_0_), channel_id=1, source_target_pairs={{0,6},{2,4},{4,2},{6,0},{8,14},{10,12},{12,10},{14,8},{1,7},{3,5},... | collective-permute-start | bytes 196616 | tf_op jit(solution)/shard_map/ppermute | solution.py:377
  40.5 7.7 %collective-permute-start.3 = (bf16[16,2048]{1,0:T(8,128)(2,1)S(1)}, bf16[16,2048]{1,0:T(8,128)(2,1)S(1)}, u32[]{:S(2)}, u32[]{:S(2)}) collective-permute-start(bf16[16,2048]{1,0:T(8,128)(2,1)S(1)} %shard_map.97.own_ref.refs_0_), channel_id=1, source_target_pairs={{0,4},{2,6},{4,0},{6,2},{8,12},{10,14},{12,8},{14,10},{1,5},{3,7},... | collective-permute-start | bytes 196616 | tf_op jit(solution)/shard_map/ppermute | solution.py:377
  40.5 7.7 %collective-permute-start.2 = (bf16[16,2048]{1,0:T(8,128)(2,1)S(1)}, bf16[16,2048]{1,0:T(8,128)(2,1)S(1)}, u32[]{:S(2)}, u32[]{:S(2)}) collective-permute-start(bf16[16,2048]{1,0:T(8,128)(2,1)S(1)} %shard_map.97.own_ref.refs_0_), channel_id=1, source_target_pairs={{0,2},{2,0},{4,6},{6,4},{8,10},{10,8},{12,14},{14,12},{1,3},{3,1},... | collective-permute-start | bytes 196616 | tf_op jit(solution)/shard_map/ppermute | solution.py:377
  42.0 6.2 %collective-permute-start.8 = (bf16[16,2048]{1,0:T(8,128)(2,1)S(1)}, bf16[16,2048]{1,0:T(8,128)(2,1)S(1)}, u32[]{:S(2)}, u32[]{:S(2)}) collective-permute-start(bf16[16,2048]{1,0:T(8,128)(2,1)S(1)} %collective-permute-done.7.refs_6_), channel_id=1, source_target_pairs={{0,2},{2,0},{4,6},{6,4},{8,10},{10,8},{12,14},{14,12},{1,3},{3,1},... | collective-permute-start | bytes 196616 | tf_op jit(solution)/shard_map/ppermute | solution.py:379
  44.4 4.3 %collective-permute-start.6 = (bf16[16,2048]{1,0:T(8,128)(2,1)S(1)}, bf16[16,2048]{1,0:T(8,128)(2,1)S(1)}, u32[]{:S(2)}, u32[]{:S(2)}) collective-permute-start(bf16[16,2048]{1,0:T(8,128)(2,1)S(1)} %collective-permute-done.5.refs_4_), channel_id=1, source_target_pairs={{0,2},{2,0},{4,6},{6,4},{8,10},{10,8},{12,14},{14,12},{1,3},{3,1},... | collective-permute-start | bytes 196616 | tf_op jit(solution)/shard_map/ppermute | solution.py:379
  45.8 1.6 %copy-start.2 = (bf16[256,4096]{1,0:T(8,128)(2,1)S(1)}, bf16[256,4096]{1,0:T(8,128)(2,1)}, u32[]{:S(2)}) copy-start(bf16[256,4096]{1,0:T(8,128)(2,1)} %refs_5_) | copy-start | bytes 6291460
  48.2 24.7 %copy-start.3 = (bf16[256,4096]{1,0:T(8,128)(2,1)S(1)}, bf16[256,4096]{1,0:T(8,128)(2,1)}, u32[]{:S(2)}) copy-start(bf16[256,4096]{1,0:T(8,128)(2,1)} %refs_5_) | copy-start | bytes 6291460
  49.1 1.6 %collective-permute-start.10 = (f32[128,512]{1,0:T(8,128)S(1)}, f32[128,512]{1,0:T(8,128)S(1)}, u32[]{:S(2)}, u32[]{:S(2)}) collective-permute-start(f32[128,512]{1,0:T(8,128)S(1)} %get-tuple-element.50.pre_own_ref), channel_id=1, source_target_pairs={{0,1},{1,0},{2,3},{3,2},{4,5},{5,4},{6,7},{7,6},{8,9},{9,8},{10,11... | collective-permute-start | bytes 786440 | tf_op jit(solution)/shard_map/ppermute | solution.py:400
  71.6 1.3 %collective-permute-start.11 = (bf16[8,48,128]{2,1,0:T(8,128)(2,1)S(1)}, bf16[8,48,128]{2,1,0:T(8,128)(2,1)S(1)}, u32[]{:S(2)}, u32[]{:S(2)}) collective-permute-start(bf16[8,48,128]{2,1,0:T(8,128)(2,1)S(1)} %all_to_all.21.own_packets_ref), channel_id=1, source_target_pairs={{0,1},{1,0},{2,3},{3,2},{4,5},{5,4},{6,7},{7,6},{8,9},{9,8},{10,11... | collective-permute-start | bytes 294920 | tf_op jit(solution)/shard_map/ppermute | solution.py:419

commit v8 on v7

--- a/solution.py
+++ b/solution.py
@@ -213,19 +213,62 @@
     return pltpu.with_memory_space_constraint(array, pltpu.HBM)
 
 
+def dlogits(packets_ref, own_tokens):
+    if len(packets_ref.shape) == 2:
+        return packets_ref[...]
+    parts = [packets_ref[g, :own_tokens] for g in range(packets_ref.shape[0])]
+    return jnp.concatenate(parts, 0)
+
+
+def ahead_body(
+    own_tokens,
+    packets_ref,
+    units_ref,
+    pre_ref,
+    basis_ref,
+    new_ref,
+    units_t_ref,
+    new_t_ref,
+    slope_ref,
+    mixed_ref,
+    grad_units_ref,
+):
+    dl = dlogits(packets_ref, own_tokens)
+    units_t = units_ref[...].T
+    units_t_ref[...] = units_t
+    mixed_ref[...] = dot(units_t, dl, LAST).astype(jnp.bfloat16)
+    grad_units_ref[...] = dot(dl, basis_ref[...], FIRST)
+    pre = pre_ref[...]
+    slope_ref[...] = jax.vjp(activate, pre)[1](jnp.ones_like(pre))[0]
+    high = min(256, new_ref.shape[1])
+    for j in range(new_ref.shape[1] // high):
+        part = pl.ds(j * high, high)
+        new_t_ref[part] = new_ref[:, part].T
+
+
 def final_body(
     own_tokens,
     own_packets_ref,
     other_packets_ref,
-    *refs,
+    other_dl_ref,
+    units_t_ref,
+    new_t_ref,
+    slope_ref,
+    own_mixed_ref,
+    own_grad_units_ref,
+    other_basis_ref,
+    own_hidden_ref,
+    other_hidden_ref,
+    loss_ref,
+    grad_in_ref,
+    grad_out_ref,
+    hidden_blocks,
+    in_blocks,
+    out_blocks,
+    sems,
 ):
-    dlogits_refs, refs = refs[:-14], refs[-14:]
-    units_ref, pre_ref, own_basis_ref, other_basis_ref, new_ref = refs[:5]
-    own_hidden_ref, other_hidden_ref, loss_ref, grad_in_ref, grad_out_ref = refs[5:10]
-    hidden_blocks, in_blocks, out_blocks, sems = refs[10:]
     groups, _, columns = own_packets_ref.shape
     steps = out_blocks.shape[0]
-    tokens = groups * own_tokens
     wide = out_blocks.shape[2]
     high = in_blocks.shape[1]
 
@@ -239,31 +282,21 @@
         )
         arriving[-1].start()
 
-    def dlogits(packets_ref):
-        return jnp.concatenate([packets_ref[g, :own_tokens] for g in range(groups)], 0)
-
-    if own_tokens % 16 == 0:
-        own_dl, other_dl = dlogits(own_packets_ref), dlogits(other_packets_ref)
-    else:
-        own_dl, other_dl = (ref[...] for ref in dlogits_refs)
+    other_dl = dlogits(other_dl_ref, own_tokens)
     leaving = []
 
-    grad_units = dot(own_dl, own_basis_ref[...], FIRST) + dot(
-        other_dl, other_basis_ref[...], FIRST
-    )
-    grad_pre = jax.vjp(activate, pre_ref[...])[1](grad_units)[0].astype(jnp.bfloat16)
+    grad_units = own_grad_units_ref[...] + dot(other_dl, other_basis_ref[...], FIRST)
+    grad_pre = (grad_units * slope_ref[...]).astype(jnp.bfloat16)
     for j in range(in_blocks.shape[0]):
         part = pl.ds(j * high, high)
-        in_blocks[j] = dot(new_ref[:, part], grad_pre, FIRST)
+        in_blocks[j] = dot(new_t_ref[part], grad_pre)
         leaving.append(
             pltpu.make_async_copy(in_blocks.at[j], grad_in_ref.at[part], sems.at[steps + j])
         )
         leaving[-1].start()
 
-    units_t = units_ref[...].T
-    mixed = jnp.concatenate(
-        [dot(units_t, dl, LAST).astype(jnp.bfloat16) for dl in (own_dl, other_dl)], 1
-    )
+    other_mixed = dot(units_t_ref[...], other_dl, LAST).astype(jnp.bfloat16)
+    mixed = jnp.concatenate([own_mixed_ref[...], other_mixed], 1)
     for j in range(steps):
         part = pl.ds(j * wide, wide)
         arriving[j].wait()
@@ -282,24 +315,18 @@
             loss = loss + packets_ref[g, first : first + 16].astype(jnp.float32)
     loss = jnp.where(iota(loss.shape, 0) == own_tokens - first, loss, 0.0)
     loss = jnp.sum(jnp.sum(loss, 0, keepdims=True), 1, keepdims=True)
-    loss_ref[...] = loss / (2 * tokens)
+    loss_ref[...] = loss / (2 * groups * own_tokens)
     for copy in leaving:
         copy.wait()
 
 
-def final_call(
-    own_tokens, packets, units, pre, own_basis, other_basis, own_hidden, other_hidden, new, steps=8
-):
+def final_call(own_tokens, packets, ahead, other_basis, own_hidden, other_hidden, steps=8):
     tokens, width = own_hidden.shape
-    hidden = pre.shape[1]
-    half = new.shape[1]
+    units_t, new_t = ahead[:2]
+    hidden, half = units_t.shape[0], new_t.shape[0]
     vmem = pl.BlockSpec(memory_space=pltpu.VMEM)
     hbm = pl.BlockSpec(memory_space=pltpu.HBM)
-    if own_tokens % 16 == 0:
-        parts = ()
-    else:
-        parts = tuple(p[:, :own_tokens].reshape(tokens, -1) for p in packets)
-    args = (*packets, *parts, units, pre, own_basis, other_basis, new)
+    args = (*packets, whole_tiles(packets[1], own_tokens), *ahead, other_basis, own_hidden)
     return pl.pallas_call(
         functools.partial(final_body, own_tokens),
         out_shape=(
@@ -307,7 +334,7 @@
             jax.ShapeDtypeStruct((half, hidden), jnp.float32),
             jax.ShapeDtypeStruct((hidden, width), jnp.float32),
         ),
-        in_specs=[vmem] * len(args) + [vmem, hbm],
+        in_specs=[vmem] * len(args) + [hbm],
         out_specs=(vmem, hbm, hbm),
         scratch_shapes=[
             pltpu.VMEM((steps, tokens, width // steps), jnp.bfloat16),
@@ -317,11 +344,22 @@
         ],
         compiler_params=pltpu.CompilerParams(vmem_limit_bytes=44 * MIB),
         cost_estimate=cost(4 * tokens * hidden * width, 4 * (half + width) * hidden),
-    )(*args, own_hidden, in_hbm(other_hidden))
+    )(*args, in_hbm(other_hidden))
+
+
+def whole_tiles(packets, own_tokens):
+    if own_tokens % 16 == 0:
+        return packets
+    return packets[:, :own_tokens].reshape(-1, packets.shape[2])
 
 
 def exchange(array):
     return lax.all_to_all(array, "vocab", 0, 0, tiled=True)
+
+
+def to_xor(array, k):
+    groups = lax.axis_size("vocab")
+    return lax.ppermute(array, "vocab", [(i, i ^ k) for i in range(groups)])
 
 
 def shards(hidden_states, targets, old_embed, decomp, counts, w_in, w_out):
@@ -371,23 +409,19 @@
     new_own = whole_call(
         add_body, shaped((new_rows, half_width), jnp.bfloat16), (adder, arrived, scale)
     )
-    if groups in (2, 4, 8):
+    if groups == 8:
         got = {}
-        for k in (4, 6, 2, 3, 1):
-            got[k] = lax.ppermute(new_own, "vocab", [(i, i ^ k) for i in range(groups)])
-        for k in (5, 7):
-            got[k] = lax.ppermute(got[k ^ 1], "vocab", [(i, i ^ 1) for i in range(groups)])
+        for k in (5, 4, 6, 2, 1):
+            got[k] = to_xor(new_own, k)
+        for k in (7,3,):
+            got[k] = to_xor(got[k ^ 1], 1)
         blocks = [new_own] + [got[k] for k in range(1, groups)]
     else:
         copies = jnp.broadcast_to(new_own[None], (groups, new_rows, half_width))
         blocks = [exchange(copies).reshape(columns, half_width)]
     new_other = lax.ppermute(new_own, "dp", swap)
-    direct = whole_call(
-        direct_body,
-        shaped((tokens, columns), jnp.float32),
-        (hidden_states, new_own, new_other),
-    )
-    blocks, direct = lax.optimization_barrier((blocks, direct))
+    w_held = held(w_in)
+    blocks, new_other, w_held = lax.optimization_barrier((blocks, new_other, w_held))
 
     new_all, pre_own = whole_call(
         functools.partial(pre_body, len(blocks)),
@@ -395,9 +429,15 @@
             shaped((columns, half_width), jnp.bfloat16),
             shaped((columns, hidden), jnp.float32),
         ),
-        (*blocks, w_in),
+        (*blocks, w_held),
     )
     pre_other = lax.ppermute(pre_own, "dp", swap)
+    pre_own, new_other = lax.optimization_barrier((pre_own, new_other))
+    direct = whole_call(
+        direct_body,
+        shaped((tokens, columns), jnp.float32),
+        (hidden_states, new_own, new_other),
+    )
     pre_units, hidden_units, share = whole_call(
         share_body,
         (
@@ -417,16 +457,19 @@
     )
     packets = exchange(packets)
     packets_other = lax.ppermute(packets, "dp", swap)
+    ahead = whole_call(
+        functools.partial(ahead_body, own_tokens),
+        (
+            shaped((hidden, columns), jnp.bfloat16),
+            shaped((half_width, columns), jnp.bfloat16),
+            shaped((columns, hidden), jnp.float32),
+            shaped((hidden, tokens), jnp.bfloat16),
+            shaped((columns, hidden), jnp.float32),
+        ),
+        (whole_tiles(packets, own_tokens), hidden_units, pre_units, basis, new_all),
+    )
     loss_value, grad_in, grad_out = final_call(
-        own_tokens,
-        (packets, packets_other),
-        hidden_units,
-        pre_units,
-        basis,
-        basis_other,
-        hidden_states,
-        hidden_other,
-        new_all,
+        own_tokens, (packets, packets_other), ahead, basis_other, hidden_states, hidden_other
     )
     loss_value = loss_value.reshape(1)
     return (loss_value, grad_in, grad_out)

time: 79.8 us -> 79.6 us (level)
  Pallas kernels: 10.7 us -> 12.8 us
  local copies, waits for them, and re-layouts: 2.52 us -> 0.93 us
  waiting for transfers between devices: 21.1 us -> 19.7 us
    pallas_call x0 -> x1, Pallas kernels: none -> 1.6 us  [held(): pl.pallas_call(copy_body, out_shape=pltpu.VMEM(array.shape, array.dtype),...]
    unnamed x16 -> x12, local copies, waits for them, and re-layouts: 2.45 us -> 0.85 us
    pallas_call x7 -> x8, Pallas kernels: 2.86 us -> 3.38 us  [whole_call(): pl.pallas_call(body, out_shape=outs, in_specs=[pl.BlockSpec(memory_space=...]
  transfers between devices with their start and end apart: 14 -> 14, of which waited for: 8 -> 9; matrix products, arithmetic and copies ran while one was open for 5% -> 5% of each run, Pallas kernels for 3% -> 6%
where the time goes in v8:
time: 79.6 us; the launch traced here: 79.2 us
  blocking collectives  20.9 us (26%)
  starting transfers between devices  20 us (25%)
  waiting for transfers between devices  19.7 us (25%)
  Pallas kernels  12.8 us (16%)
  matrix products  4.11 us (5%)
  local copies, waits for them, and re-layouts  0.93 us (1%)
  between operations  0.82 us (1%)
    all_to_all x2, blocking collectives, exchange(): return lax.all_to_all(array, 'vocab', 0, 0, tiled=True)  20.9 us
    all_to_all x2, waiting for transfers between devices, exchange(): return lax.all_to_all(array, 'vocab', 0, 0, tiled=True)  14.5 us
    all_to_all x2, starting transfers between devices, exchange(): return lax.all_to_all(array, 'vocab', 0, 0, tiled=True)  10.3 us
    ppermute x7, starting transfers between devices, to_xor(): return lax.ppermute(array, 'vocab', [(i, i ^ k) for i in range(groups)])  9.04 us
    pallas_call x1, Pallas kernels, final_call(): pl.pallas_call(functools.partial(final_body, own_tokens), out_shape=(jax....  6.38 us
    dot_general x1, matrix products, dot(): return lax.dot_general(a, b, dims, preferred_element_type=jnp.float32)  4.11 us
    pallas_call x8, Pallas kernels, whole_call(): pl.pallas_call(body, out_shape=outs, in_specs=[pl.BlockSpec(memory_space=...  3.38 us
    ppermute x7, waiting for transfers between devices, to_xor(): return lax.ppermute(array, 'vocab', [(i, i ^ k) for i in range(groups)])  2.14 us
  transfers between devices with their start and end apart: 14, of which 9 were waited for; matrix products, arithmetic and copies ran while one was open for 5% of the time, Pallas kernels for 6%

profile of v8, /device:TPU:0, one launch (start us, length us, event | category | flops | bytes accessed | tf_op | source)
XLA Modules:
  0.0 79.2 jit_solution(3863523834577753179)
XLA Ops:
  0.7 0.8 %copy-done.2 = s32[16,8]{0,1:T(8,128)S(1)} copy-done((s32[16,8]{0,1:T(8,128)S(1)}, s32[16,8]{0,1:T(8,128)}, u32[]{:S(2)}) %copy-start.2) | copy-done | bytes 536
  1.5 0.6 shard_map.94
  2.6 6.8 %all-to-all-start = ((s32[8,8,128]{2,1,0:T(8,128)}), s32[8,8,128]{2,1,0:T(8,128)S(1)}, u32[]{:S(2)}, u32[]{:S(2)}) async-start(s32[8,8,128]{2,1,0:T(8,128)} %shard_map.94), calls=%async_computation | async-start | bytes 65536 | tf_op jit(solution)/shard_map/all_to_all | solution.py:357
  9.8 6.2 %all-to-all-done.look_ref = s32[8,8,128]{2,1,0:T(8,128)S(1)} async-done(((s32[8,8,128]{2,1,0:T(8,128)}), s32[8,8,128]{2,1,0:T(8,128)S(1)}, u32[]{:S(2)}, u32[]{:S(2)}) %all-to-all-start) | async-done | bytes 32800 | tf_op jit(solution)/shard_map/all_to_all | solution.py:357
  16.1 1.4 %shard_map.96 = bf16[128,2048]{1,0:T(8,128)(2,1)} custom-call(s32[8,8,128]{2,1,0:T(8,128)S(1)} %all-to-all-done.look_ref, bf16[256,2048]{1,0:T(8,128)(2,1)S(1)} %constant_dynamic-slice_fusion.old_ref), custom_call_target="tpu_custom_call" | custom-call | flops 16777216 | bytes 2097152 | tf_op jit(solution)/shard_map/pallas_call | solution.py:122
  17.5 3.5 %all-to-all-start.1 = ((bf16[8,16,2048]{2,1,0:T(8,128)(2,1)}), bf16[8,16,2048]{2,1,0:T(8,128)(2,1)S(1)}, u32[]{:S(2)}, u32[]{:S(2)}) async-start(bf16[8,16,2048]{2,1,0:T(8,128)(2,1)} %bitcast.15), calls=%async_computation.1 | async-start | bytes 1048576 | tf_op jit(solution)/shard_map/all_to_all | solution.py:357
  21.0 4.1 %convolution_convert_fusion.basis_ref = bf16[256,512]{1,0:T(8,128)(2,1)S(1)} fusion(bf16[256,4096]{1,0:T(8,128)(2,1)} %own_hidden_ref, bf16[512,4096]{1,0:T(8,128)(2,1)} %param.13), kind=kOutput, calls=%fused_computation | convolution fusion | flops 1073872896 | bytes 6553600 | tf_op jit(solution)/shard_map/dot_general | solution.py:21
  25.2 1.5 %collective-permute-done.other_basis_ref = bf16[256,512]{1,0:T(8,128)(2,1)S(1)} collective-permute-done((bf16[256,512]{1,0:T(8,128)(2,1)S(1)}, bf16[256,512]{1,0:T(8,128)(2,1)S(1)}, u32[]{:S(2)}, u32[]{:S(2)}) %collective-permute-start) | collective-permute-done | bytes 262176 | tf_op jit(solution)/shard_map/ppermute | solution.py:404
  26.7 8.2 %all-to-all-done.1 = bf16[8,16,2048]{2,1,0:T(8,128)(2,1)S(1)} async-done(((bf16[8,16,2048]{2,1,0:T(8,128)(2,1)}), bf16[8,16,2048]{2,1,0:T(8,128)(2,1)S(1)}, u32[]{:S(2)}, u32[]{:S(2)}) %all-to-all-start.1) | async-done | bytes 524320 | tf_op jit(solution)/shard_map/all_to_all | solution.py:357
  35.2 1.2 %collective-permute-start.7 = (bf16[16,2048]{1,0:T(8,128)(2,1)S(1)}, bf16[16,2048]{1,0:T(8,128)(2,1)S(1)}, u32[]{:S(2)}, u32[]{:S(2)}) collective-permute-start(bf16[16,2048]{1,0:T(8,128)(2,1)S(1)} %shard_map.97.refs_0_.own_ref), channel_id=1, source_target_pairs={{0,12},{2,14},{4,8},{6,10},{8,4},{10,6},{12,0},{14,2},{1,13},{3,15... | collective-permute-start | bytes 196616 | tf_op jit(solution)/shard_map/ppermute | solution.py:362
  36.4 4.1 %collective-permute-start.6 = (bf16[16,2048]{1,0:T(8,128)(2,1)S(1)}, bf16[16,2048]{1,0:T(8,128)(2,1)S(1)}, u32[]{:S(2)}, u32[]{:S(2)}) collective-permute-start(bf16[16,2048]{1,0:T(8,128)(2,1)S(1)} %shard_map.97.refs_0_.own_ref), channel_id=1, source_target_pairs={{0,10},{2,8},{4,14},{6,12},{8,2},{10,0},{12,6},{14,4},{1,11},{3,9}... | collective-permute-start | bytes 196616 | tf_op jit(solution)/shard_map/ppermute | solution.py:362
  40.5 0.6 collective-permute-start.2
  41.1 0.9 %collective-permute-done.7.refs_6_ = bf16[16,2048]{1,0:T(8,128)(2,1)S(1)} collective-permute-done((bf16[16,2048]{1,0:T(8,128)(2,1)S(1)}, bf16[16,2048]{1,0:T(8,128)(2,1)S(1)}, u32[]{:S(2)}, u32[]{:S(2)}) %collective-permute-start.7) | collective-permute-done | bytes 65568 | tf_op jit(solution)/shard_map/ppermute | solution.py:362
  42.0 1.4 %collective-permute-start.8 = (bf16[16,2048]{1,0:T(8,128)(2,1)S(1)}, bf16[16,2048]{1,0:T(8,128)(2,1)S(1)}, u32[]{:S(2)}, u32[]{:S(2)}) collective-permute-start(bf16[16,2048]{1,0:T(8,128)(2,1)S(1)} %collective-permute-done.7.refs_6_), channel_id=1, source_target_pairs={{0,2},{2,0},{4,6},{6,4},{8,10},{10,8},{12,14},{14,12},{1,3},{3,1},... | collective-permute-start | bytes 196616 | tf_op jit(solution)/shard_map/ppermute | solution.py:362
  43.5 1.7 %collective-permute-start.4 = (bf16[16,2048]{1,0:T(8,128)(2,1)S(1)}, bf16[16,2048]{1,0:T(8,128)(2,1)S(1)}, u32[]{:S(2)}, u32[]{:S(2)}) collective-permute-start(bf16[16,2048]{1,0:T(8,128)(2,1)S(1)} %collective-permute-done.3.refs_2_), channel_id=1, source_target_pairs={{0,2},{2,0},{4,6},{6,4},{8,10},{10,8},{12,14},{14,12},{1,3},{3,1},... | collective-permute-start | bytes 196616 | tf_op jit(solution)/shard_map/ppermute | solution.py:362
  45.2 1.6 %shard_map.98.refs_8_ = bf16[2048,512]{1,0:T(8,128)(2,1)S(1)} custom-call(bf16[2048,512]{1,0:T(8,128)(2,1)} %source_ref.1), custom_call_target="tpu_custom_call" | custom-call | bytes 2097152 | tf_op jit(solution)/shard_map/pallas_call | solution.py:169
  47.2 0.8 %collective-permute-done.4.refs_3_ = bf16[16,2048]{1,0:T(8,128)(2,1)S(1)} collective-permute-done((bf16[16,2048]{1,0:T(8,128)(2,1)S(1)}, bf16[16,2048]{1,0:T(8,128)(2,1)S(1)}, u32[]{:S(2)}, u32[]{:S(2)}) %collective-permute-start.4) | collective-permute-done | bytes 65568 | tf_op jit(solution)/shard_map/ppermute | solution.py:362
  48.6 0.7 shard_map.100.direct_ref
  49.3 0.8 collective-permute-done.10.pre_other_ref
  50.4 11.3 %all_to_all.20.shares_ref = f32[8,32,128]{2,1,0:T(8,128)S(1)} all-to-all(f32[8,32,128]{2,1,0:T(8,128)S(1)} %bitcast.10), channel_id=1, replica_groups=mesh['groups'=2,'vocab'=8,'dp'=2] {'vocab'}, dimensions={0} | all-to-all | bytes 262144 | tf_op jit(solution)/shard_map/all_to_all | solution.py:357
  61.9 9.6 %all_to_all.21.packets_ref.own_packets_ref = bf16[8,48,128]{2,1,0:T(8,128)(2,1)S(1)} all-to-all(bf16[8,48,128]{2,1,0:T(8,128)(2,1)S(1)} %shard_map.102), channel_id=1, replica_groups=mesh['groups'=2,'vocab'=8,'dp'=2] {'vocab'}, dimensions={0} | all-to-all | bytes 196608 | tf_op jit(solution)/shard_map/all_to_all | solution.py:357
  71.5 0.5 shard_map.103
  72.0 0.8 collective-permute-done.11.other_packets_ref.other_dl_ref
  72.8 6.4 %shard_map.104 = (f32[1,1]{1,0:T(1,128)}, f32[2048,512]{1,0:T(8,128)}, f32[512,4096]{1,0:T(8,128)}) custom-call(bf16[8,48,128]{2,1,0:T(8,128)(2,1)S(1)} %all_to_all.21.packets_ref.own_packets_ref, bf16[8,48,128]{2,1,0:T(8,128)(2,1)S(1)} %collective-permute-done.11.other_packets_ref.other_dl_ref, ...), custom_call_target="tpu_custom_call" | custom-call | flops 2147483648 | bytes 12582912 | tf_op jit(solution)/shard_map/pallas_call | solution.py:330
  (31 shorter events, 2.7 us)
Async XLA Ops:
  0.6 8.7 %copy-start = (bf16[256,4096]{1,0:T(8,128)(2,1)S(1)}, bf16[256,4096]{1,0:T(8,128)(2,1)}, u32[]{:S(2)}) copy-start(bf16[256,4096]{1,0:T(8,128)(2,1)} %param.9) | copy-start | bytes 6291460
  0.6 8.8 %copy-start.5 = (s32[16]{0:T(128)S(1)}, s32[16]{0:T(128)}, u32[]{:S(2)}) copy-start(s32[16]{0:T(128)} %param.11) | copy-start | bytes 196
  0.7 8.8 %copy-start.4 = (s32[256]{0:T(256)S(1)}, s32[256]{0:T(256)}, u32[]{:S(2)}) copy-start(s32[256]{0:T(256)} %param.8) | copy-start | bytes 3076
  0.7 0.8 %copy-start.2 = (s32[16,8]{0,1:T(8,128)S(1)}, s32[16,8]{0,1:T(8,128)}, u32[]{:S(2)}) copy-start(s32[16,8]{0,1:T(8,128)} %param.10) | copy-start | bytes 1540
  1.5 8.0 %copy-start.3 = (s32[16,8]{0,1:T(8,128)S(1)}, s32[16,8]{0,1:T(8,128)}, u32[]{:S(2)}) copy-start(s32[16,8]{0,1:T(8,128)} %param.10) | copy-start | bytes 1540
  2.1 32.8 %collective-permute-start.1 = (bf16[256,4096]{1,0:T(8,128)(2,1)}, bf16[256,4096]{1,0:T(8,128)(2,1)}, u32[]{:S(2)}, u32[]{:S(2)}) collective-permute-start(bf16[256,4096]{1,0:T(8,128)(2,1)} %own_hidden_ref), channel_id=1, source_target_pairs={{0,1},{1,0},{2,3},{3,2},{4,5},{5,4},{6,7},{7,6},{8,9},{9,8},{10,11... | collective-permute-start | bytes 6291464 | tf_op jit(solution)/shard_map/ppermute | solution.py:385
  2.6 13.5 %all-to-all-start = ((s32[8,8,128]{2,1,0:T(8,128)}), s32[8,8,128]{2,1,0:T(8,128)S(1)}, u32[]{:S(2)}, u32[]{:S(2)}) async-start(s32[8,8,128]{2,1,0:T(8,128)} %shard_map.94), calls=%async_computation | async-start | bytes 65536 | tf_op jit(solution)/shard_map/all_to_all | solution.py:357
  17.5 17.5 %all-to-all-start.1 = ((bf16[8,16,2048]{2,1,0:T(8,128)(2,1)}), bf16[8,16,2048]{2,1,0:T(8,128)(2,1)S(1)}, u32[]{:S(2)}, u32[]{:S(2)}) async-start(bf16[8,16,2048]{2,1,0:T(8,128)(2,1)} %bitcast.15), calls=%async_computation.1 | async-start | bytes 1048576 | tf_op jit(solution)/shard_map/all_to_all | solution.py:357
  25.1 1.6 %collective-permute-start = (bf16[256,512]{1,0:T(8,128)(2,1)S(1)}, bf16[256,512]{1,0:T(8,128)(2,1)S(1)}, u32[]{:S(2)}, u32[]{:S(2)}) collective-permute-start(bf16[256,512]{1,0:T(8,128)(2,1)S(1)} %convolution_convert_fusion.basis_ref), channel_id=1, source_target_pairs={{0,1},{1,0},{2,3},{3,2},{4,5},{5,4},{6,7},{7,6},{8,9},{9,8},{10,11... | collective-permute-start | bytes 786440 | tf_op jit(solution)/shard_map/ppermute | solution.py:404
  35.1 5.4 %collective-permute-start.9 = (bf16[16,2048]{1,0:T(8,128)(2,1)S(1)}, bf16[16,2048]{1,0:T(8,128)(2,1)S(1)}, u32[]{:S(2)}, u32[]{:S(2)}) collective-permute-start(bf16[16,2048]{1,0:T(8,128)(2,1)S(1)} %shard_map.97.refs_0_.own_ref), channel_id=1, source_target_pairs={{0,1},{1,0},{2,3},{3,2},{4,5},{5,4},{6,7},{7,6},{8,9},{9,8},{10,11... | collective-permute-start | bytes 196616 | tf_op jit(solution)/shard_map/ppermute | solution.py:422
  35.2 6.8 %collective-permute-start.7 = (bf16[16,2048]{1,0:T(8,128)(2,1)S(1)}, bf16[16,2048]{1,0:T(8,128)(2,1)S(1)}, u32[]{:S(2)}, u32[]{:S(2)}) collective-permute-start(bf16[16,2048]{1,0:T(8,128)(2,1)S(1)} %shard_map.97.refs_0_.own_ref), channel_id=1, source_target_pairs={{0,12},{2,14},{4,8},{6,10},{8,4},{10,6},{12,0},{14,2},{1,13},{3,15... | collective-permute-start | bytes 196616 | tf_op jit(solution)/shard_map/ppermute | solution.py:362
  36.4 7.1 %collective-permute-start.3 = (bf16[16,2048]{1,0:T(8,128)(2,1)S(1)}, bf16[16,2048]{1,0:T(8,128)(2,1)S(1)}, u32[]{:S(2)}, u32[]{:S(2)}) collective-permute-start(bf16[16,2048]{1,0:T(8,128)(2,1)S(1)} %shard_map.97.refs_0_.own_ref), channel_id=1, source_target_pairs={{0,4},{2,6},{4,0},{6,2},{8,12},{10,14},{12,8},{14,10},{1,5},{3,7},... | collective-permute-start | bytes 196616 | tf_op jit(solution)/shard_map/ppermute | solution.py:362
  36.4 10.4 %collective-permute-start.6 = (bf16[16,2048]{1,0:T(8,128)(2,1)S(1)}, bf16[16,2048]{1,0:T(8,128)(2,1)S(1)}, u32[]{:S(2)}, u32[]{:S(2)}) collective-permute-start(bf16[16,2048]{1,0:T(8,128)(2,1)S(1)} %shard_map.97.refs_0_.own_ref), channel_id=1, source_target_pairs={{0,10},{2,8},{4,14},{6,12},{8,2},{10,0},{12,6},{14,4},{1,11},{3,9}... | collective-permute-start | bytes 196616 | tf_op jit(solution)/shard_map/ppermute | solution.py:362
  40.5 6.7 %collective-permute-start.5 = (bf16[16,2048]{1,0:T(8,128)(2,1)S(1)}, bf16[16,2048]{1,0:T(8,128)(2,1)S(1)}, u32[]{:S(2)}, u32[]{:S(2)}) collective-permute-start(bf16[16,2048]{1,0:T(8,128)(2,1)S(1)} %shard_map.97.refs_0_.own_ref), channel_id=1, source_target_pairs={{0,8},{2,10},{4,12},{6,14},{8,0},{10,2},{12,4},{14,6},{1,9},{3,11}... | collective-permute-start | bytes 196616 | tf_op jit(solution)/shard_map/ppermute | solution.py:362
  40.5 6.6 %collective-permute-start.2 = (bf16[16,2048]{1,0:T(8,128)(2,1)S(1)}, bf16[16,2048]{1,0:T(8,128)(2,1)S(1)}, u32[]{:S(2)}, u32[]{:S(2)}) collective-permute-start(bf16[16,2048]{1,0:T(8,128)(2,1)S(1)} %shard_map.97.refs_0_.own_ref), channel_id=1, source_target_pairs={{0,2},{2,0},{4,6},{6,4},{8,10},{10,8},{12,14},{14,12},{1,3},{3,1},... | collective-permute-start | bytes 196616 | tf_op jit(solution)/shard_map/ppermute | solution.py:362
  42.0 5.2 %collective-permute-start.8 = (bf16[16,2048]{1,0:T(8,128)(2,1)S(1)}, bf16[16,2048]{1,0:T(8,128)(2,1)S(1)}, u32[]{:S(2)}, u32[]{:S(2)}) collective-permute-start(bf16[16,2048]{1,0:T(8,128)(2,1)S(1)} %collective-permute-done.7.refs_6_), channel_id=1, source_target_pairs={{0,2},{2,0},{4,6},{6,4},{8,10},{10,8},{12,14},{14,12},{1,3},{3,1},... | collective-permute-start | bytes 196616 | tf_op jit(solution)/shard_map/ppermute | solution.py:362
  43.5 4.5 %collective-permute-start.4 = (bf16[16,2048]{1,0:T(8,128)(2,1)S(1)}, bf16[16,2048]{1,0:T(8,128)(2,1)S(1)}, u32[]{:S(2)}, u32[]{:S(2)}) collective-permute-start(bf16[16,2048]{1,0:T(8,128)(2,1)S(1)} %collective-permute-done.3.refs_2_), channel_id=1, source_target_pairs={{0,2},{2,0},{4,6},{6,4},{8,10},{10,8},{12,14},{14,12},{1,3},{3,1},... | collective-permute-start | bytes 196616 | tf_op jit(solution)/shard_map/ppermute | solution.py:362
  46.8 1.8 %copy-start.1 = (bf16[256,4096]{1,0:T(8,128)(2,1)S(1)}, bf16[256,4096]{1,0:T(8,128)(2,1)}, u32[]{:S(2)}) copy-start(bf16[256,4096]{1,0:T(8,128)(2,1)} %own_hidden_ref) | copy-start | bytes 6291460
  48.5 1.6 %collective-permute-start.10 = (f32[128,512]{1,0:T(8,128)S(1)}, f32[128,512]{1,0:T(8,128)S(1)}, u32[]{:S(2)}, u32[]{:S(2)}) collective-permute-start(f32[128,512]{1,0:T(8,128)S(1)} %get-tuple-element.61.pre_own_ref), channel_id=1, source_target_pairs={{0,1},{1,0},{2,3},{3,2},{4,5},{5,4},{6,7},{7,6},{8,9},{9,8},{10,11... | collective-permute-start | bytes 786440 | tf_op jit(solution)/shard_map/ppermute | solution.py:434
  71.5 1.3 %collective-permute-start.11 = (bf16[8,48,128]{2,1,0:T(8,128)(2,1)S(1)}, bf16[8,48,128]{2,1,0:T(8,128)(2,1)S(1)}, u32[]{:S(2)}, u32[]{:S(2)}) collective-permute-start(bf16[8,48,128]{2,1,0:T(8,128)(2,1)S(1)} %all_to_all.21.packets_ref.own_packets_ref), channel_id=1, source_target_pairs={{0,1},{1,0},{2,3},{3,2},{4,5},{5,4},{6,7},{7,6},{8,9},{9,8},{10,11... | collective-permute-start | bytes 294920 | tf_op jit(solution)/shard_map/ppermute | solution.py:459

commit v9 on v8

--- a/solution.py
+++ b/solution.py
@@ -262,7 +262,6 @@
     loss_ref,
     grad_in_ref,
     grad_out_ref,
-    hidden_blocks,
     in_blocks,
     out_blocks,
     sems,
@@ -271,16 +270,6 @@
     steps = out_blocks.shape[0]
     wide = out_blocks.shape[2]
     high = in_blocks.shape[1]
-
-    arriving = []
-    for j in range(steps):
-        part = pl.ds(j * wide, wide)
-        arriving.append(
-            pltpu.make_async_copy(
-                other_hidden_ref.at[:, part], hidden_blocks.at[j], sems.at[2 * steps + j]
-            )
-        )
-        arriving[-1].start()
 
     other_dl = dlogits(other_dl_ref, own_tokens)
     leaving = []
@@ -299,9 +288,8 @@
     mixed = jnp.concatenate([own_mixed_ref[...], other_mixed], 1)
     for j in range(steps):
         part = pl.ds(j * wide, wide)
-        arriving[j].wait()
         out_blocks[j] = dot(
-            mixed, jnp.concatenate([own_hidden_ref[:, part], hidden_blocks[j]], 0)
+            mixed, jnp.concatenate([own_hidden_ref[:, part], other_hidden_ref[:, part]], 0)
         )
         leaving.append(
             pltpu.make_async_copy(out_blocks.at[j], grad_out_ref.at[:, part], sems.at[j])
@@ -326,7 +314,8 @@
     hidden, half = units_t.shape[0], new_t.shape[0]
     vmem = pl.BlockSpec(memory_space=pltpu.VMEM)
     hbm = pl.BlockSpec(memory_space=pltpu.HBM)
-    args = (*packets, whole_tiles(packets[1], own_tokens), *ahead, other_basis, own_hidden)
+    hiddens = (own_hidden, other_hidden)
+    args = (*packets, whole_tiles(packets[1], own_tokens), *ahead, other_basis, *hiddens)
     return pl.pallas_call(
         functools.partial(final_body, own_tokens),
         out_shape=(
@@ -334,17 +323,16 @@
             jax.ShapeDtypeStruct((half, hidden), jnp.float32),
             jax.ShapeDtypeStruct((hidden, width), jnp.float32),
         ),
-        in_specs=[vmem] * len(args) + [hbm],
+        in_specs=[vmem] * len(args),
         out_specs=(vmem, hbm, hbm),
         scratch_shapes=[
-            pltpu.VMEM((steps, tokens, width // steps), jnp.bfloat16),
             pltpu.VMEM((steps, half // steps, hidden), jnp.float32),
             pltpu.VMEM((steps, hidden, width // steps), jnp.float32),
-            pltpu.SemaphoreType.DMA((3 * steps,)),
+            pltpu.SemaphoreType.DMA((2 * steps,)),
         ],
         compiler_params=pltpu.CompilerParams(vmem_limit_bytes=44 * MIB),
         cost_estimate=cost(4 * tokens * hidden * width, 4 * (half + width) * hidden),
-    )(*args, in_hbm(other_hidden))
+    )(*args)
 
 
 def whole_tiles(packets, own_tokens):
@@ -413,15 +401,15 @@
         got = {}
         for k in (5, 4, 6, 2, 1):
             got[k] = to_xor(new_own, k)
-        for k in (7,3,):
+        for k in (7, 3):
             got[k] = to_xor(got[k ^ 1], 1)
         blocks = [new_own] + [got[k] for k in range(1, groups)]
     else:
         copies = jnp.broadcast_to(new_own[None], (groups, new_rows, half_width))
         blocks = [exchange(copies).reshape(columns, half_width)]
     new_other = lax.ppermute(new_own, "dp", swap)
-    w_held = held(w_in)
-    blocks, new_other, w_held = lax.optimization_barrier((blocks, new_other, w_held))
+    hidden_other = held(hidden_other)
+    blocks, new_other, hidden_other = lax.optimization_barrier((blocks, new_other, hidden_other))
 
     new_all, pre_own = whole_call(
         functools.partial(pre_body, len(blocks)),
@@ -429,7 +417,7 @@
             shaped((columns, half_width), jnp.bfloat16),
             shaped((columns, hidden), jnp.float32),
         ),
-        (*blocks, w_held),
+        (*blocks, w_in),
     )
     pre_other = lax.ppermute(pre_own, "dp", swap)
     pre_own, new_other = lax.optimization_barrier((pre_own, new_other))

time: 79.6 us -> 78.9 us (level)
  Pallas kernels: 12.8 us -> 12 us
where the time goes in v9:
time: 78.9 us; the launch traced here: 78.5 us
  blocking collectives  20.9 us (26%)
  starting transfers between devices  20 us (25%)
  waiting for transfers between devices  19.7 us (25%)
  Pallas kernels  12 us (15%)
  matrix products  4.11 us (5%)
  local copies, waits for them, and re-layouts  0.93 us (1%)
  between operations  0.82 us (1%)
    all_to_all x2, blocking collectives, exchange(): return lax.all_to_all(array, 'vocab', 0, 0, tiled=True)  20.9 us
    all_to_all x2, waiting for transfers between devices, exchange(): return lax.all_to_all(array, 'vocab', 0, 0, tiled=True)  14.5 us
    all_to_all x2, starting transfers between devices, exchange(): return lax.all_to_all(array, 'vocab', 0, 0, tiled=True)  10.3 us
    ppermute x7, starting transfers between devices, to_xor(): return lax.ppermute(array, 'vocab', [(i, i ^ k) for i in range(groups)])  9.04 us
    pallas_call x1, Pallas kernels, final_call(): pl.pallas_call(functools.partial(final_body, own_tokens), out_shape=(jax....  5.68 us
    dot_general x1, matrix products, dot(): return lax.dot_general(a, b, dims, preferred_element_type=jnp.float32)  4.11 us
    pallas_call x8, Pallas kernels, whole_call(): pl.pallas_call(body, out_shape=outs, in_specs=[pl.BlockSpec(memory_space=...  3.38 us
    ppermute x7, waiting for transfers between devices, to_xor(): return lax.ppermute(array, 'vocab', [(i, i ^ k) for i in range(groups)])  2.14 us
  transfers between devices with their start and end apart: 14, of which 9 were waited for; matrix products, arithmetic and copies ran while one was open for 5% of the time, Pallas kernels for 6%

profile of v9, /device:TPU:0, one launch (start us, length us, event | category | flops | bytes accessed | tf_op | source)
XLA Modules:
  0.0 78.5 jit_solution(14981150870933799326)
XLA Ops:
  0.7 0.8 %copy-done.3 = s32[16,8]{0,1:T(8,128)S(1)} copy-done((s32[16,8]{0,1:T(8,128)S(1)}, s32[16,8]{0,1:T(8,128)}, u32[]{:S(2)}) %copy-start.3) | copy-done | bytes 536
  1.5 0.6 shard_map.94
  2.6 6.8 %all-to-all-start = ((s32[8,8,128]{2,1,0:T(8,128)}), s32[8,8,128]{2,1,0:T(8,128)S(1)}, u32[]{:S(2)}, u32[]{:S(2)}) async-start(s32[8,8,128]{2,1,0:T(8,128)} %shard_map.94), calls=%async_computation | async-start | bytes 65536 | tf_op jit(solution)/shard_map/all_to_all | solution.py:345
  9.8 6.2 %all-to-all-done.look_ref = s32[8,8,128]{2,1,0:T(8,128)S(1)} async-done(((s32[8,8,128]{2,1,0:T(8,128)}), s32[8,8,128]{2,1,0:T(8,128)S(1)}, u32[]{:S(2)}, u32[]{:S(2)}) %all-to-all-start) | async-done | bytes 32800 | tf_op jit(solution)/shard_map/all_to_all | solution.py:345
  16.1 1.4 %shard_map.96 = bf16[128,2048]{1,0:T(8,128)(2,1)} custom-call(s32[8,8,128]{2,1,0:T(8,128)S(1)} %all-to-all-done.look_ref, bf16[256,2048]{1,0:T(8,128)(2,1)S(1)} %constant_dynamic-slice_fusion.old_ref), custom_call_target="tpu_custom_call" | custom-call | flops 16777216 | bytes 2097152 | tf_op jit(solution)/shard_map/pallas_call | solution.py:122
  17.5 3.5 %all-to-all-start.1 = ((bf16[8,16,2048]{2,1,0:T(8,128)(2,1)}), bf16[8,16,2048]{2,1,0:T(8,128)(2,1)S(1)}, u32[]{:S(2)}, u32[]{:S(2)}) async-start(bf16[8,16,2048]{2,1,0:T(8,128)(2,1)} %bitcast.15), calls=%async_computation.1 | async-start | bytes 1048576 | tf_op jit(solution)/shard_map/all_to_all | solution.py:345
  21.0 4.1 %convolution_convert_fusion.basis_ref = bf16[256,512]{1,0:T(8,128)(2,1)S(1)} fusion(bf16[256,4096]{1,0:T(8,128)(2,1)} %own_hidden_ref, bf16[512,4096]{1,0:T(8,128)(2,1)} %param.13), kind=kOutput, calls=%fused_computation | convolution fusion | flops 1073872896 | bytes 6553600 | tf_op jit(solution)/shard_map/dot_general | solution.py:21
  25.2 1.5 %collective-permute-done.other_basis_ref = bf16[256,512]{1,0:T(8,128)(2,1)S(1)} collective-permute-done((bf16[256,512]{1,0:T(8,128)(2,1)S(1)}, bf16[256,512]{1,0:T(8,128)(2,1)S(1)}, u32[]{:S(2)}, u32[]{:S(2)}) %collective-permute-start) | collective-permute-done | bytes 262176 | tf_op jit(solution)/shard_map/ppermute | solution.py:392
  26.7 8.2 %all-to-all-done.1 = bf16[8,16,2048]{2,1,0:T(8,128)(2,1)S(1)} async-done(((bf16[8,16,2048]{2,1,0:T(8,128)(2,1)}), bf16[8,16,2048]{2,1,0:T(8,128)(2,1)S(1)}, u32[]{:S(2)}, u32[]{:S(2)}) %all-to-all-start.1) | async-done | bytes 524320 | tf_op jit(solution)/shard_map/all_to_all | solution.py:345
  35.2 1.2 %collective-permute-start.7 = (bf16[16,2048]{1,0:T(8,128)(2,1)S(1)}, bf16[16,2048]{1,0:T(8,128)(2,1)S(1)}, u32[]{:S(2)}, u32[]{:S(2)}) collective-permute-start(bf16[16,2048]{1,0:T(8,128)(2,1)S(1)} %shard_map.97.refs_0_.own_ref), channel_id=1, source_target_pairs={{0,12},{2,14},{4,8},{6,10},{8,4},{10,6},{12,0},{14,2},{1,13},{3,15... | collective-permute-start | bytes 196616 | tf_op jit(solution)/shard_map/ppermute | solution.py:350
  36.4 4.1 %collective-permute-start.6 = (bf16[16,2048]{1,0:T(8,128)(2,1)S(1)}, bf16[16,2048]{1,0:T(8,128)(2,1)S(1)}, u32[]{:S(2)}, u32[]{:S(2)}) collective-permute-start(bf16[16,2048]{1,0:T(8,128)(2,1)S(1)} %shard_map.97.refs_0_.own_ref), channel_id=1, source_target_pairs={{0,10},{2,8},{4,14},{6,12},{8,2},{10,0},{12,6},{14,4},{1,11},{3,9}... | collective-permute-start | bytes 196616 | tf_op jit(solution)/shard_map/ppermute | solution.py:350
  40.5 0.6 collective-permute-start.2
  41.1 0.9 %collective-permute-done.7.refs_6_ = bf16[16,2048]{1,0:T(8,128)(2,1)S(1)} collective-permute-done((bf16[16,2048]{1,0:T(8,128)(2,1)S(1)}, bf16[16,2048]{1,0:T(8,128)(2,1)S(1)}, u32[]{:S(2)}, u32[]{:S(2)}) %collective-permute-start.7) | collective-permute-done | bytes 65568 | tf_op jit(solution)/shard_map/ppermute | solution.py:350
  42.0 1.4 %collective-permute-start.8 = (bf16[16,2048]{1,0:T(8,128)(2,1)S(1)}, bf16[16,2048]{1,0:T(8,128)(2,1)S(1)}, u32[]{:S(2)}, u32[]{:S(2)}) collective-permute-start(bf16[16,2048]{1,0:T(8,128)(2,1)S(1)} %collective-permute-done.7.refs_6_), channel_id=1, source_target_pairs={{0,2},{2,0},{4,6},{6,4},{8,10},{10,8},{12,14},{14,12},{1,3},{3,1},... | collective-permute-start | bytes 196616 | tf_op jit(solution)/shard_map/ppermute | solution.py:350
  43.5 1.7 %collective-permute-start.4 = (bf16[16,2048]{1,0:T(8,128)(2,1)S(1)}, bf16[16,2048]{1,0:T(8,128)(2,1)S(1)}, u32[]{:S(2)}, u32[]{:S(2)}) collective-permute-start(bf16[16,2048]{1,0:T(8,128)(2,1)S(1)} %collective-permute-done.3.refs_2_), channel_id=1, source_target_pairs={{0,2},{2,0},{4,6},{6,4},{8,10},{10,8},{12,14},{14,12},{1,3},{3,1},... | collective-permute-start | bytes 196616 | tf_op jit(solution)/shard_map/ppermute | solution.py:350
  45.2 1.6 %shard_map.98.other_hidden_ref = bf16[256,4096]{1,0:T(8,128)(2,1)S(1)} custom-call(bf16[256,4096]{1,0:T(8,128)(2,1)} %collective-permute-done.1.source_ref), custom_call_target="tpu_custom_call" | custom-call | bytes 2097152 | tf_op jit(solution)/shard_map/pallas_call | solution.py:169
  47.2 0.8 %collective-permute-done.4.refs_3_ = bf16[16,2048]{1,0:T(8,128)(2,1)S(1)} collective-permute-done((bf16[16,2048]{1,0:T(8,128)(2,1)S(1)}, bf16[16,2048]{1,0:T(8,128)(2,1)S(1)}, u32[]{:S(2)}, u32[]{:S(2)}) %collective-permute-start.4) | collective-permute-done | bytes 65568 | tf_op jit(solution)/shard_map/ppermute | solution.py:350
  48.6 0.7 shard_map.100.direct_ref
  49.3 0.8 collective-permute-done.10.pre_other_ref
  50.4 11.3 %all_to_all.20.shares_ref = f32[8,32,128]{2,1,0:T(8,128)S(1)} all-to-all(f32[8,32,128]{2,1,0:T(8,128)S(1)} %bitcast.10), channel_id=1, replica_groups=mesh['groups'=2,'vocab'=8,'dp'=2] {'vocab'}, dimensions={0} | all-to-all | bytes 262144 | tf_op jit(solution)/shard_map/all_to_all | solution.py:345
  61.9 9.6 %all_to_all.21.packets_ref.own_packets_ref = bf16[8,48,128]{2,1,0:T(8,128)(2,1)S(1)} all-to-all(bf16[8,48,128]{2,1,0:T(8,128)(2,1)S(1)} %shard_map.102), channel_id=1, replica_groups=mesh['groups'=2,'vocab'=8,'dp'=2] {'vocab'}, dimensions={0} | all-to-all | bytes 196608 | tf_op jit(solution)/shard_map/all_to_all | solution.py:345
  71.5 0.5 shard_map.103
  72.0 0.8 collective-permute-done.11.other_packets_ref.other_dl_ref
  72.8 5.7 %shard_map.104 = (f32[1,1]{1,0:T(1,128)}, f32[2048,512]{1,0:T(8,128)}, f32[512,4096]{1,0:T(8,128)}) custom-call(bf16[8,48,128]{2,1,0:T(8,128)(2,1)S(1)} %all_to_all.21.packets_ref.own_packets_ref, bf16[8,48,128]{2,1,0:T(8,128)(2,1)S(1)} %collective-permute-done.11.other_packets_ref.other_dl_ref, ...), custom_call_target="tpu_custom_call" | custom-call | flops 2147483648 | bytes 12582912 | tf_op jit(solution)/shard_map/pallas_call | solution.py:319
  (33 shorter events, 2.7 us)
Async XLA Ops:
  0.6 8.7 %copy-start = (bf16[256,4096]{1,0:T(8,128)(2,1)S(1)}, bf16[256,4096]{1,0:T(8,128)(2,1)}, u32[]{:S(2)}) copy-start(bf16[256,4096]{1,0:T(8,128)(2,1)} %param.9) | copy-start | bytes 6291460
  0.6 8.8 %copy-start.6 = (s32[16]{0:T(128)S(1)}, s32[16]{0:T(128)}, u32[]{:S(2)}) copy-start(s32[16]{0:T(128)} %param.11) | copy-start | bytes 196
  0.7 8.8 %copy-start.5 = (s32[256]{0:T(256)S(1)}, s32[256]{0:T(256)}, u32[]{:S(2)}) copy-start(s32[256]{0:T(256)} %param.8) | copy-start | bytes 3076
  0.7 0.8 %copy-start.3 = (s32[16,8]{0,1:T(8,128)S(1)}, s32[16,8]{0,1:T(8,128)}, u32[]{:S(2)}) copy-start(s32[16,8]{0,1:T(8,128)} %param.10) | copy-start | bytes 1540
  1.5 8.0 %copy-start.4 = (s32[16,8]{0,1:T(8,128)S(1)}, s32[16,8]{0,1:T(8,128)}, u32[]{:S(2)}) copy-start(s32[16,8]{0,1:T(8,128)} %param.10) | copy-start | bytes 1540
  2.1 32.8 %collective-permute-start.1 = (bf16[256,4096]{1,0:T(8,128)(2,1)}, bf16[256,4096]{1,0:T(8,128)(2,1)}, u32[]{:S(2)}, u32[]{:S(2)}) collective-permute-start(bf16[256,4096]{1,0:T(8,128)(2,1)} %own_hidden_ref), channel_id=1, source_target_pairs={{0,1},{1,0},{2,3},{3,2},{4,5},{5,4},{6,7},{7,6},{8,9},{9,8},{10,11... | collective-permute-start | bytes 6291464 | tf_op jit(solution)/shard_map/ppermute | solution.py:373
  2.6 13.5 %all-to-all-start = ((s32[8,8,128]{2,1,0:T(8,128)}), s32[8,8,128]{2,1,0:T(8,128)S(1)}, u32[]{:S(2)}, u32[]{:S(2)}) async-start(s32[8,8,128]{2,1,0:T(8,128)} %shard_map.94), calls=%async_computation | async-start | bytes 65536 | tf_op jit(solution)/shard_map/all_to_all | solution.py:345
  17.5 17.5 %all-to-all-start.1 = ((bf16[8,16,2048]{2,1,0:T(8,128)(2,1)}), bf16[8,16,2048]{2,1,0:T(8,128)(2,1)S(1)}, u32[]{:S(2)}, u32[]{:S(2)}) async-start(bf16[8,16,2048]{2,1,0:T(8,128)(2,1)} %bitcast.15), calls=%async_computation.1 | async-start | bytes 1048576 | tf_op jit(solution)/shard_map/all_to_all | solution.py:345
  25.1 1.6 %collective-permute-start = (bf16[256,512]{1,0:T(8,128)(2,1)S(1)}, bf16[256,512]{1,0:T(8,128)(2,1)S(1)}, u32[]{:S(2)}, u32[]{:S(2)}) collective-permute-start(bf16[256,512]{1,0:T(8,128)(2,1)S(1)} %convolution_convert_fusion.basis_ref), channel_id=1, source_target_pairs={{0,1},{1,0},{2,3},{3,2},{4,5},{5,4},{6,7},{7,6},{8,9},{9,8},{10,11... | collective-permute-start | bytes 786440 | tf_op jit(solution)/shard_map/ppermute | solution.py:392
  35.1 12.9 %copy-start.1 = (bf16[2048,512]{1,0:T(8,128)(2,1)S(1)}, bf16[2048,512]{1,0:T(8,128)(2,1)}, u32[]{:S(2)}) copy-start(bf16[2048,512]{1,0:T(8,128)(2,1)} %refs_8_.1) | copy-start | bytes 6291460
  35.1 5.4 %collective-permute-start.9 = (bf16[16,2048]{1,0:T(8,128)(2,1)S(1)}, bf16[16,2048]{1,0:T(8,128)(2,1)S(1)}, u32[]{:S(2)}, u32[]{:S(2)}) collective-permute-start(bf16[16,2048]{1,0:T(8,128)(2,1)S(1)} %shard_map.97.refs_0_.own_ref), channel_id=1, source_target_pairs={{0,1},{1,0},{2,3},{3,2},{4,5},{5,4},{6,7},{7,6},{8,9},{9,8},{10,11... | collective-permute-start | bytes 196616 | tf_op jit(solution)/shard_map/ppermute | solution.py:410
  35.2 6.8 %collective-permute-start.7 = (bf16[16,2048]{1,0:T(8,128)(2,1)S(1)}, bf16[16,2048]{1,0:T(8,128)(2,1)S(1)}, u32[]{:S(2)}, u32[]{:S(2)}) collective-permute-start(bf16[16,2048]{1,0:T(8,128)(2,1)S(1)} %shard_map.97.refs_0_.own_ref), channel_id=1, source_target_pairs={{0,12},{2,14},{4,8},{6,10},{8,4},{10,6},{12,0},{14,2},{1,13},{3,15... | collective-permute-start | bytes 196616 | tf_op jit(solution)/shard_map/ppermute | solution.py:350
  36.4 7.1 %collective-permute-start.3 = (bf16[16,2048]{1,0:T(8,128)(2,1)S(1)}, bf16[16,2048]{1,0:T(8,128)(2,1)S(1)}, u32[]{:S(2)}, u32[]{:S(2)}) collective-permute-start(bf16[16,2048]{1,0:T(8,128)(2,1)S(1)} %shard_map.97.refs_0_.own_ref), channel_id=1, source_target_pairs={{0,4},{2,6},{4,0},{6,2},{8,12},{10,14},{12,8},{14,10},{1,5},{3,7},... | collective-permute-start | bytes 196616 | tf_op jit(solution)/shard_map/ppermute | solution.py:350
  36.4 10.4 %collective-permute-start.6 = (bf16[16,2048]{1,0:T(8,128)(2,1)S(1)}, bf16[16,2048]{1,0:T(8,128)(2,1)S(1)}, u32[]{:S(2)}, u32[]{:S(2)}) collective-permute-start(bf16[16,2048]{1,0:T(8,128)(2,1)S(1)} %shard_map.97.refs_0_.own_ref), channel_id=1, source_target_pairs={{0,10},{2,8},{4,14},{6,12},{8,2},{10,0},{12,6},{14,4},{1,11},{3,9}... | collective-permute-start | bytes 196616 | tf_op jit(solution)/shard_map/ppermute | solution.py:350
  40.5 6.7 %collective-permute-start.5 = (bf16[16,2048]{1,0:T(8,128)(2,1)S(1)}, bf16[16,2048]{1,0:T(8,128)(2,1)S(1)}, u32[]{:S(2)}, u32[]{:S(2)}) collective-permute-start(bf16[16,2048]{1,0:T(8,128)(2,1)S(1)} %shard_map.97.refs_0_.own_ref), channel_id=1, source_target_pairs={{0,8},{2,10},{4,12},{6,14},{8,0},{10,2},{12,4},{14,6},{1,9},{3,11}... | collective-permute-start | bytes 196616 | tf_op jit(solution)/shard_map/ppermute | solution.py:350
  40.5 6.6 %collective-permute-start.2 = (bf16[16,2048]{1,0:T(8,128)(2,1)S(1)}, bf16[16,2048]{1,0:T(8,128)(2,1)S(1)}, u32[]{:S(2)}, u32[]{:S(2)}) collective-permute-start(bf16[16,2048]{1,0:T(8,128)(2,1)S(1)} %shard_map.97.refs_0_.own_ref), channel_id=1, source_target_pairs={{0,2},{2,0},{4,6},{6,4},{8,10},{10,8},{12,14},{14,12},{1,3},{3,1},... | collective-permute-start | bytes 196616 | tf_op jit(solution)/shard_map/ppermute | solution.py:350
  42.0 5.2 %collective-permute-start.8 = (bf16[16,2048]{1,0:T(8,128)(2,1)S(1)}, bf16[16,2048]{1,0:T(8,128)(2,1)S(1)}, u32[]{:S(2)}, u32[]{:S(2)}) collective-permute-start(bf16[16,2048]{1,0:T(8,128)(2,1)S(1)} %collective-permute-done.7.refs_6_), channel_id=1, source_target_pairs={{0,2},{2,0},{4,6},{6,4},{8,10},{10,8},{12,14},{14,12},{1,3},{3,1},... | collective-permute-start | bytes 196616 | tf_op jit(solution)/shard_map/ppermute | solution.py:350
  43.5 4.5 %collective-permute-start.4 = (bf16[16,2048]{1,0:T(8,128)(2,1)S(1)}, bf16[16,2048]{1,0:T(8,128)(2,1)S(1)}, u32[]{:S(2)}, u32[]{:S(2)}) collective-permute-start(bf16[16,2048]{1,0:T(8,128)(2,1)S(1)} %collective-permute-done.3.refs_2_), channel_id=1, source_target_pairs={{0,2},{2,0},{4,6},{6,4},{8,10},{10,8},{12,14},{14,12},{1,3},{3,1},... | collective-permute-start | bytes 196616 | tf_op jit(solution)/shard_map/ppermute | solution.py:350
  46.8 1.8 %copy-start.2 = (bf16[256,4096]{1,0:T(8,128)(2,1)S(1)}, bf16[256,4096]{1,0:T(8,128)(2,1)}, u32[]{:S(2)}) copy-start(bf16[256,4096]{1,0:T(8,128)(2,1)} %own_hidden_ref) | copy-start | bytes 6291460
  48.5 1.6 %collective-permute-start.10 = (f32[128,512]{1,0:T(8,128)S(1)}, f32[128,512]{1,0:T(8,128)S(1)}, u32[]{:S(2)}, u32[]{:S(2)}) collective-permute-start(f32[128,512]{1,0:T(8,128)S(1)} %get-tuple-element.61.pre_own_ref), channel_id=1, source_target_pairs={{0,1},{1,0},{2,3},{3,2},{4,5},{5,4},{6,7},{7,6},{8,9},{9,8},{10,11... | collective-permute-start | bytes 786440 | tf_op jit(solution)/shard_map/ppermute | solution.py:422
  71.5 1.3 %collective-permute-start.11 = (bf16[8,48,128]{2,1,0:T(8,128)(2,1)S(1)}, bf16[8,48,128]{2,1,0:T(8,128)(2,1)S(1)}, u32[]{:S(2)}, u32[]{:S(2)}) collective-permute-start(bf16[8,48,128]{2,1,0:T(8,128)(2,1)S(1)} %all_to_all.21.packets_ref.own_packets_ref), channel_id=1, source_target_pairs={{0,1},{1,0},{2,3},{3,2},{4,5},{5,4},{6,7},{7,6},{8,9},{9,8},{10,11... | collective-permute-start | bytes 294920 | tf_op jit(solution)/shard_map/ppermute | solution.py:447

commit v10 on v9

--- a/solution.py
+++ b/solution.py
@@ -159,22 +159,28 @@
     pre_ref[...] = dot(new_ref[...], w_ref[...])
 
 
-def copy_body(source_ref, out_ref, sem):
-    copy = pltpu.make_async_copy(source_ref, out_ref, sem)
-    copy.start()
-    copy.wait()
-
-
-def held(array):
+def copy_body(count, *refs):
+    sources, outs, sems = refs[:count], refs[count : 2 * count], refs[2 * count]
+    copies = [
+        pltpu.make_async_copy(source, out, sems.at[index])
+        for index, (source, out) in enumerate(zip(sources, outs, strict=True))
+    ]
+    for copy in copies:
+        copy.start()
+    for copy in copies:
+        copy.wait()
+
+
+def held(*arrays):
     return pl.pallas_call(
-        copy_body,
-        out_shape=pltpu.VMEM(array.shape, array.dtype),
-        in_specs=[pl.BlockSpec(memory_space=pltpu.HBM)],
-        out_specs=pl.BlockSpec(memory_space=pltpu.VMEM),
-        scratch_shapes=[pltpu.SemaphoreType.DMA],
+        functools.partial(copy_body, len(arrays)),
+        out_shape=[pltpu.VMEM(array.shape, array.dtype) for array in arrays],
+        in_specs=[pl.BlockSpec(memory_space=pltpu.HBM)] * len(arrays),
+        out_specs=[pl.BlockSpec(memory_space=pltpu.VMEM)] * len(arrays),
+        scratch_shapes=[pltpu.SemaphoreType.DMA((len(arrays),))],
         compiler_params=pltpu.CompilerParams(vmem_limit_bytes=8 * MIB),
-        cost_estimate=cost(0, 2 * array.size),
-    )(in_hbm(array))
+        cost_estimate=cost(0, sum(2 * array.size for array in arrays)),
+    )(*[in_hbm(array) for array in arrays])
 
 
 def share_body(pre_own_ref, pre_other_ref, basis_ref, direct_ref, pre_ref, units_ref, share_ref):
@@ -369,8 +375,6 @@
         copies_body, shaped((groups, k_slots, max(new_rows, 128)), jnp.int32), (decomp.T,)
     )
     look = exchange(ids)
-    ids, hidden_states = lax.optimization_barrier((ids, hidden_states))
-    hidden_other = lax.ppermute(hidden_states, "dp", swap)
     old_half = lax.dynamic_slice_in_dim(old_embed, dp_index * half_width, half_width, 1)
     own_tokens = tokens // groups
     adder, scale, own_targets = whole_call(
@@ -382,6 +386,8 @@
         ),
         (decomp.T, counts[None], targets[None]),
     )
+    old_half, hidden_sent = lax.optimization_barrier((old_half, hidden_states))
+    hidden_other = lax.ppermute(hidden_sent, "dp", swap)
     look, old_half, adder, scale, own_targets = lax.optimization_barrier(
         (look, old_half, adder, scale, own_targets)
     )
@@ -408,8 +414,9 @@
         copies = jnp.broadcast_to(new_own[None], (groups, new_rows, half_width))
         blocks = [exchange(copies).reshape(columns, half_width)]
     new_other = lax.ppermute(new_own, "dp", swap)
-    hidden_other = held(hidden_other)
-    blocks, new_other, hidden_other = lax.optimization_barrier((blocks, new_other, hidden_other))
+    hiddens = held(hidden_states, hidden_other)
+    blocks, new_other, hiddens = lax.optimization_barrier((blocks, new_other, hiddens))
+    hidden_states, hidden_other = hiddens
 
     new_all, pre_own = whole_call(
         functools.partial(pre_body, len(blocks)),

time: 78.9 us -> 79.8 us (1.011)
  transfers between devices with their start and end apart: 14 -> 14, of which waited for: 9 -> 8; matrix products, arithmetic and copies ran while one was open for 5% -> 5% of each run, Pallas kernels for 6% -> 7%
where the time goes in v10:
time: 79.8 us; the launch traced here: 79.4 us
  blocking collectives  20.9 us (26%)
  starting transfers between devices  20.1 us (25%)
  waiting for transfers between devices  19.1 us (24%)
  Pallas kernels  12.7 us (16%)
  matrix products  4.11 us (5%)
  local copies, waits for them, and re-layouts  1.67 us (2%)
  between operations  0.82 us (1%)
    all_to_all x2, blocking collectives, exchange(): return lax.all_to_all(array, 'vocab', 0, 0, tiled=True)  20.9 us
    all_to_all x2, waiting for transfers between devices, exchange(): return lax.all_to_all(array, 'vocab', 0, 0, tiled=True)  14.5 us
    all_to_all x2, starting transfers between devices, exchange(): return lax.all_to_all(array, 'vocab', 0, 0, tiled=True)  10.3 us
    ppermute x7, starting transfers between devices, to_xor(): return lax.ppermute(array, 'vocab', [(i, i ^ k) for i in range(groups)])  9.04 us
    pallas_call x1, Pallas kernels, final_call(): pl.pallas_call(functools.partial(final_body, own_tokens), out_shape=(jax....  5.68 us
    dot_general x1, matrix products, dot(): return lax.dot_general(a, b, dims, preferred_element_type=jnp.float32)  4.11 us
    pallas_call x8, Pallas kernels, whole_call(): pl.pallas_call(body, out_shape=outs, in_specs=[pl.BlockSpec(memory_space=...  3.39 us
    pallas_call x1, Pallas kernels, held(): pl.pallas_call(functools.partial(copy_body, len(arrays)), out_shape=[pltp...  2.24 us
  transfers between devices with their start and end apart: 14, of which 8 were waited for; matrix products, arithmetic and copies ran while one was open for 5% of the time, Pallas kernels for 7%

profile of v10, /device:TPU:0, one launch (start us, length us, event | category | flops | bytes accessed | tf_op | source)
XLA Modules:
  0.0 79.4 jit_solution(12966456646865557139)
XLA Ops:
  0.7 1.5 %copy-done = bf16[256,4096]{1,0:T(8,128)(2,1)S(1)} copy-done((bf16[256,4096]{1,0:T(8,128)(2,1)S(1)}, bf16[256,4096]{1,0:T(8,128)(2,1)}, u32[]{:S(2)}) %copy-start) | copy-done | bytes 2097176
  2.3 0.5 collective-permute-start.1
  2.9 0.6 shard_map.94
  3.5 6.8 %all-to-all-start = ((s32[8,8,128]{2,1,0:T(8,128)}), s32[8,8,128]{2,1,0:T(8,128)S(1)}, u32[]{:S(2)}, u32[]{:S(2)}) async-start(s32[8,8,128]{2,1,0:T(8,128)} %shard_map.94), calls=%async_computation | async-start | bytes 65536 | tf_op jit(solution)/shard_map/all_to_all | solution.py:351
  10.7 6.3 %all-to-all-done.look_ref = s32[8,8,128]{2,1,0:T(8,128)S(1)} async-done(((s32[8,8,128]{2,1,0:T(8,128)}), s32[8,8,128]{2,1,0:T(8,128)S(1)}, u32[]{:S(2)}, u32[]{:S(2)}) %all-to-all-start) | async-done | bytes 32800 | tf_op jit(solution)/shard_map/all_to_all | solution.py:351
  17.0 1.4 %shard_map.96 = bf16[128,2048]{1,0:T(8,128)(2,1)} custom-call(s32[8,8,128]{2,1,0:T(8,128)S(1)} %all-to-all-done.look_ref, bf16[256,2048]{1,0:T(8,128)(2,1)S(1)} %constant_dynamic-slice_fusion.old_ref), custom_call_target="tpu_custom_call" | custom-call | flops 16777216 | bytes 2097152 | tf_op jit(solution)/shard_map/pallas_call | solution.py:122
  18.4 3.5 %all-to-all-start.1 = ((bf16[8,16,2048]{2,1,0:T(8,128)(2,1)}), bf16[8,16,2048]{2,1,0:T(8,128)(2,1)S(1)}, u32[]{:S(2)}, u32[]{:S(2)}) async-start(bf16[8,16,2048]{2,1,0:T(8,128)(2,1)} %bitcast.15), calls=%async_computation.1 | async-start | bytes 1048576 | tf_op jit(solution)/shard_map/all_to_all | solution.py:351
  21.9 4.1 %convolution_convert_fusion.basis_ref = bf16[256,512]{1,0:T(8,128)(2,1)S(1)} fusion(bf16[256,4096]{1,0:T(8,128)(2,1)} %refs_0_.1, bf16[512,4096]{1,0:T(8,128)(2,1)} %param.13), kind=kOutput, calls=%fused_computation | convolution fusion | flops 1073872896 | bytes 6553600 | tf_op jit(solution)/shard_map/dot_general | solution.py:21
  26.1 1.5 %collective-permute-done.other_basis_ref = bf16[256,512]{1,0:T(8,128)(2,1)S(1)} collective-permute-done((bf16[256,512]{1,0:T(8,128)(2,1)S(1)}, bf16[256,512]{1,0:T(8,128)(2,1)S(1)}, u32[]{:S(2)}, u32[]{:S(2)}) %collective-permute-start) | collective-permute-done | bytes 262176 | tf_op jit(solution)/shard_map/ppermute | solution.py:398
  27.6 8.2 %all-to-all-done.1 = bf16[8,16,2048]{2,1,0:T(8,128)(2,1)S(1)} async-done(((bf16[8,16,2048]{2,1,0:T(8,128)(2,1)}), bf16[8,16,2048]{2,1,0:T(8,128)(2,1)S(1)}, u32[]{:S(2)}, u32[]{:S(2)}) %all-to-all-start.1) | async-done | bytes 524320 | tf_op jit(solution)/shard_map/all_to_all | solution.py:351
  36.1 1.2 %collective-permute-start.7 = (bf16[16,2048]{1,0:T(8,128)(2,1)S(1)}, bf16[16,2048]{1,0:T(8,128)(2,1)S(1)}, u32[]{:S(2)}, u32[]{:S(2)}) collective-permute-start(bf16[16,2048]{1,0:T(8,128)(2,1)S(1)} %shard_map.97.refs_0_.own_ref), channel_id=1, source_target_pairs={{0,12},{2,14},{4,8},{6,10},{8,4},{10,6},{12,0},{14,2},{1,13},{3,15... | collective-permute-start | bytes 196616 | tf_op jit(solution)/shard_map/ppermute | solution.py:356
  37.3 4.1 %collective-permute-start.6 = (bf16[16,2048]{1,0:T(8,128)(2,1)S(1)}, bf16[16,2048]{1,0:T(8,128)(2,1)S(1)}, u32[]{:S(2)}, u32[]{:S(2)}) collective-permute-start(bf16[16,2048]{1,0:T(8,128)(2,1)S(1)} %shard_map.97.refs_0_.own_ref), channel_id=1, source_target_pairs={{0,10},{2,8},{4,14},{6,12},{8,2},{10,0},{12,6},{14,4},{1,11},{3,9}... | collective-permute-start | bytes 196616 | tf_op jit(solution)/shard_map/ppermute | solution.py:356
  41.4 0.6 collective-permute-start.2
  42.0 0.9 %collective-permute-done.7.refs_6_ = bf16[16,2048]{1,0:T(8,128)(2,1)S(1)} collective-permute-done((bf16[16,2048]{1,0:T(8,128)(2,1)S(1)}, bf16[16,2048]{1,0:T(8,128)(2,1)S(1)}, u32[]{:S(2)}, u32[]{:S(2)}) %collective-permute-start.7) | collective-permute-done | bytes 65568 | tf_op jit(solution)/shard_map/ppermute | solution.py:356
  42.9 1.4 %collective-permute-start.8 = (bf16[16,2048]{1,0:T(8,128)(2,1)S(1)}, bf16[16,2048]{1,0:T(8,128)(2,1)S(1)}, u32[]{:S(2)}, u32[]{:S(2)}) collective-permute-start(bf16[16,2048]{1,0:T(8,128)(2,1)S(1)} %collective-permute-done.7.refs_6_), channel_id=1, source_target_pairs={{0,2},{2,0},{4,6},{6,4},{8,10},{10,8},{12,14},{14,12},{1,3},{3,1},... | collective-permute-start | bytes 196616 | tf_op jit(solution)/shard_map/ppermute | solution.py:356
  44.4 1.7 %collective-permute-start.4 = (bf16[16,2048]{1,0:T(8,128)(2,1)S(1)}, bf16[16,2048]{1,0:T(8,128)(2,1)S(1)}, u32[]{:S(2)}, u32[]{:S(2)}) collective-permute-start(bf16[16,2048]{1,0:T(8,128)(2,1)S(1)} %collective-permute-done.3.refs_2_), channel_id=1, source_target_pairs={{0,2},{2,0},{4,6},{6,4},{8,10},{10,8},{12,14},{14,12},{1,3},{3,1},... | collective-permute-start | bytes 196616 | tf_op jit(solution)/shard_map/ppermute | solution.py:356
  46.1 2.2 %shard_map.98 = (bf16[256,4096]{1,0:T(8,128)(2,1)S(1)}, bf16[256,4096]{1,0:T(8,128)(2,1)S(1)}) custom-call(bf16[256,4096]{1,0:T(8,128)(2,1)} %refs_0_.1, bf16[256,4096]{1,0:T(8,128)(2,1)} %collective-permute-done.1.refs_1_), custom_call_target="tpu_custom_call" | custom-call | bytes 4194304 | tf_op jit(solution)/shard_map/pallas_call | solution.py:175
  48.4 0.5 collective-permute-done.4.refs_3_
  49.5 0.7 shard_map.100.direct_ref
  50.2 0.8 collective-permute-done.10.pre_other_ref
  51.3 11.3 %all_to_all.20.shares_ref = f32[8,32,128]{2,1,0:T(8,128)S(1)} all-to-all(f32[8,32,128]{2,1,0:T(8,128)S(1)} %bitcast.10), channel_id=1, replica_groups=mesh['groups'=2,'vocab'=8,'dp'=2] {'vocab'}, dimensions={0} | all-to-all | bytes 262144 | tf_op jit(solution)/shard_map/all_to_all | solution.py:351
  62.8 9.6 %all_to_all.21.packets_ref.own_packets_ref = bf16[8,48,128]{2,1,0:T(8,128)(2,1)S(1)} all-to-all(bf16[8,48,128]{2,1,0:T(8,128)(2,1)S(1)} %shard_map.102), channel_id=1, replica_groups=mesh['groups'=2,'vocab'=8,'dp'=2] {'vocab'}, dimensions={0} | all-to-all | bytes 196608 | tf_op jit(solution)/shard_map/all_to_all | solution.py:351
  72.9 0.8 collective-permute-done.11.other_packets_ref.other_dl_ref
  73.7 5.7 %shard_map.104 = (f32[1,1]{1,0:T(1,128)}, f32[2048,512]{1,0:T(8,128)}, f32[512,4096]{1,0:T(8,128)}) custom-call(bf16[8,48,128]{2,1,0:T(8,128)(2,1)S(1)} %all_to_all.21.packets_ref.own_packets_ref, bf16[8,48,128]{2,1,0:T(8,128)(2,1)S(1)} %collective-permute-done.11.other_packets_ref.other_dl_ref, ...), custom_call_target="tpu_custom_call" | custom-call | flops 2147483648 | bytes 12582912 | tf_op jit(solution)/shard_map/pallas_call | solution.py:325
  (29 shorter events, 2.5 us)
Async XLA Ops:
  0.6 1.6 %copy-start = (bf16[256,4096]{1,0:T(8,128)(2,1)S(1)}, bf16[256,4096]{1,0:T(8,128)(2,1)}, u32[]{:S(2)}) copy-start(bf16[256,4096]{1,0:T(8,128)(2,1)} %param.9) | copy-start | bytes 6291460
  0.6 2.2 %copy-start.2 = (s32[16,8]{0,1:T(8,128)S(1)}, s32[16,8]{0,1:T(8,128)}, u32[]{:S(2)}) copy-start(s32[16,8]{0,1:T(8,128)} %param.10) | copy-start | bytes 1540
  0.7 9.6 %copy-start.4 = (s32[16]{0:T(128)S(1)}, s32[16]{0:T(128)}, u32[]{:S(2)}) copy-start(s32[16]{0:T(128)} %param.11) | copy-start | bytes 196
  0.7 9.6 %copy-start.3 = (s32[256]{0:T(256)S(1)}, s32[256]{0:T(256)}, u32[]{:S(2)}) copy-start(s32[256]{0:T(256)} %param.8) | copy-start | bytes 3076
  2.3 33.5 %collective-permute-start.1 = (bf16[256,4096]{1,0:T(8,128)(2,1)}, bf16[256,4096]{1,0:T(8,128)(2,1)}, u32[]{:S(2)}, u32[]{:S(2)}) collective-permute-start(bf16[256,4096]{1,0:T(8,128)(2,1)} %refs_0_.1), channel_id=1, source_target_pairs={{0,1},{1,0},{2,3},{3,2},{4,5},{5,4},{6,7},{7,6},{8,9},{9,8},{10,11... | collective-permute-start | bytes 6291464 | tf_op jit(solution)/shard_map/ppermute | solution.py:390
  3.5 13.5 %all-to-all-start = ((s32[8,8,128]{2,1,0:T(8,128)}), s32[8,8,128]{2,1,0:T(8,128)S(1)}, u32[]{:S(2)}, u32[]{:S(2)}) async-start(s32[8,8,128]{2,1,0:T(8,128)} %shard_map.94), calls=%async_computation | async-start | bytes 65536 | tf_op jit(solution)/shard_map/all_to_all | solution.py:351
  18.4 17.5 %all-to-all-start.1 = ((bf16[8,16,2048]{2,1,0:T(8,128)(2,1)}), bf16[8,16,2048]{2,1,0:T(8,128)(2,1)S(1)}, u32[]{:S(2)}, u32[]{:S(2)}) async-start(bf16[8,16,2048]{2,1,0:T(8,128)(2,1)} %bitcast.15), calls=%async_computation.1 | async-start | bytes 1048576 | tf_op jit(solution)/shard_map/all_to_all | solution.py:351
  26.0 1.6 %collective-permute-start = (bf16[256,512]{1,0:T(8,128)(2,1)S(1)}, bf16[256,512]{1,0:T(8,128)(2,1)S(1)}, u32[]{:S(2)}, u32[]{:S(2)}) collective-permute-start(bf16[256,512]{1,0:T(8,128)(2,1)S(1)} %convolution_convert_fusion.basis_ref), channel_id=1, source_target_pairs={{0,1},{1,0},{2,3},{3,2},{4,5},{5,4},{6,7},{7,6},{8,9},{9,8},{10,11... | collective-permute-start | bytes 786440 | tf_op jit(solution)/shard_map/ppermute | solution.py:398
  36.0 12.9 %copy-start.1 = (bf16[2048,512]{1,0:T(8,128)(2,1)S(1)}, bf16[2048,512]{1,0:T(8,128)(2,1)}, u32[]{:S(2)}) copy-start(bf16[2048,512]{1,0:T(8,128)(2,1)} %refs_8_.1) | copy-start | bytes 6291460
  36.0 5.4 %collective-permute-start.9 = (bf16[16,2048]{1,0:T(8,128)(2,1)S(1)}, bf16[16,2048]{1,0:T(8,128)(2,1)S(1)}, u32[]{:S(2)}, u32[]{:S(2)}) collective-permute-start(bf16[16,2048]{1,0:T(8,128)(2,1)S(1)} %shard_map.97.refs_0_.own_ref), channel_id=1, source_target_pairs={{0,1},{1,0},{2,3},{3,2},{4,5},{5,4},{6,7},{7,6},{8,9},{9,8},{10,11... | collective-permute-start | bytes 196616 | tf_op jit(solution)/shard_map/ppermute | solution.py:416
  36.1 6.8 %collective-permute-start.7 = (bf16[16,2048]{1,0:T(8,128)(2,1)S(1)}, bf16[16,2048]{1,0:T(8,128)(2,1)S(1)}, u32[]{:S(2)}, u32[]{:S(2)}) collective-permute-start(bf16[16,2048]{1,0:T(8,128)(2,1)S(1)} %shard_map.97.refs_0_.own_ref), channel_id=1, source_target_pairs={{0,12},{2,14},{4,8},{6,10},{8,4},{10,6},{12,0},{14,2},{1,13},{3,15... | collective-permute-start | bytes 196616 | tf_op jit(solution)/shard_map/ppermute | solution.py:356
  37.3 7.1 %collective-permute-start.3 = (bf16[16,2048]{1,0:T(8,128)(2,1)S(1)}, bf16[16,2048]{1,0:T(8,128)(2,1)S(1)}, u32[]{:S(2)}, u32[]{:S(2)}) collective-permute-start(bf16[16,2048]{1,0:T(8,128)(2,1)S(1)} %shard_map.97.refs_0_.own_ref), channel_id=1, source_target_pairs={{0,4},{2,6},{4,0},{6,2},{8,12},{10,14},{12,8},{14,10},{1,5},{3,7},... | collective-permute-start | bytes 196616 | tf_op jit(solution)/shard_map/ppermute | solution.py:356
  37.3 11.0 %collective-permute-start.6 = (bf16[16,2048]{1,0:T(8,128)(2,1)S(1)}, bf16[16,2048]{1,0:T(8,128)(2,1)S(1)}, u32[]{:S(2)}, u32[]{:S(2)}) collective-permute-start(bf16[16,2048]{1,0:T(8,128)(2,1)S(1)} %shard_map.97.refs_0_.own_ref), channel_id=1, source_target_pairs={{0,10},{2,8},{4,14},{6,12},{8,2},{10,0},{12,6},{14,4},{1,11},{3,9}... | collective-permute-start | bytes 196616 | tf_op jit(solution)/shard_map/ppermute | solution.py:356
  41.4 6.9 %collective-permute-start.5 = (bf16[16,2048]{1,0:T(8,128)(2,1)S(1)}, bf16[16,2048]{1,0:T(8,128)(2,1)S(1)}, u32[]{:S(2)}, u32[]{:S(2)}) collective-permute-start(bf16[16,2048]{1,0:T(8,128)(2,1)S(1)} %shard_map.97.refs_0_.own_ref), channel_id=1, source_target_pairs={{0,8},{2,10},{4,12},{6,14},{8,0},{10,2},{12,4},{14,6},{1,9},{3,11}... | collective-permute-start | bytes 196616 | tf_op jit(solution)/shard_map/ppermute | solution.py:356
  41.4 6.9 %collective-permute-start.2 = (bf16[16,2048]{1,0:T(8,128)(2,1)S(1)}, bf16[16,2048]{1,0:T(8,128)(2,1)S(1)}, u32[]{:S(2)}, u32[]{:S(2)}) collective-permute-start(bf16[16,2048]{1,0:T(8,128)(2,1)S(1)} %shard_map.97.refs_0_.own_ref), channel_id=1, source_target_pairs={{0,2},{2,0},{4,6},{6,4},{8,10},{10,8},{12,14},{14,12},{1,3},{3,1},... | collective-permute-start | bytes 196616 | tf_op jit(solution)/shard_map/ppermute | solution.py:356
  42.9 5.5 %collective-permute-start.8 = (bf16[16,2048]{1,0:T(8,128)(2,1)S(1)}, bf16[16,2048]{1,0:T(8,128)(2,1)S(1)}, u32[]{:S(2)}, u32[]{:S(2)}) collective-permute-start(bf16[16,2048]{1,0:T(8,128)(2,1)S(1)} %collective-permute-done.7.refs_6_), channel_id=1, source_target_pairs={{0,2},{2,0},{4,6},{6,4},{8,10},{10,8},{12,14},{14,12},{1,3},{3,1},... | collective-permute-start | bytes 196616 | tf_op jit(solution)/shard_map/ppermute | solution.py:356
  44.4 4.5 %collective-permute-start.4 = (bf16[16,2048]{1,0:T(8,128)(2,1)S(1)}, bf16[16,2048]{1,0:T(8,128)(2,1)S(1)}, u32[]{:S(2)}, u32[]{:S(2)}) collective-permute-start(bf16[16,2048]{1,0:T(8,128)(2,1)S(1)} %collective-permute-done.3.refs_2_), channel_id=1, source_target_pairs={{0,2},{2,0},{4,6},{6,4},{8,10},{10,8},{12,14},{14,12},{1,3},{3,1},... | collective-permute-start | bytes 196616 | tf_op jit(solution)/shard_map/ppermute | solution.py:356
  49.4 1.6 %collective-permute-start.10 = (f32[128,512]{1,0:T(8,128)S(1)}, f32[128,512]{1,0:T(8,128)S(1)}, u32[]{:S(2)}, u32[]{:S(2)}) collective-permute-start(f32[128,512]{1,0:T(8,128)S(1)} %get-tuple-element.68.pre_own_ref), channel_id=1, source_target_pairs={{0,1},{1,0},{2,3},{3,2},{4,5},{5,4},{6,7},{7,6},{8,9},{9,8},{10,11... | collective-permute-start | bytes 786440 | tf_op jit(solution)/shard_map/ppermute | solution.py:429
  72.4 1.3 %collective-permute-start.11 = (bf16[8,48,128]{2,1,0:T(8,128)(2,1)S(1)}, bf16[8,48,128]{2,1,0:T(8,128)(2,1)S(1)}, u32[]{:S(2)}, u32[]{:S(2)}) collective-permute-start(bf16[8,48,128]{2,1,0:T(8,128)(2,1)S(1)} %all_to_all.21.packets_ref.own_packets_ref), channel_id=1, source_target_pairs={{0,1},{1,0},{2,3},{3,2},{4,5},{5,4},{6,7},{7,6},{8,9},{9,8},{10,11... | collective-permute-start | bytes 294920 | tf_op jit(solution)/shard_map/ppermute | solution.py:454
